TPU v7x, 32 devices: a whole 2x2x4 slice. The times are simulated.
32 devices in a mesh: blk: 16 (over z, y, core), head: 2 (over x).
Axes of the slice: x: 2, y: 2, z: 4, core: 2. Of those that a mesh axis runs over, the one named last changes fastest.
Arguments:
- hidden_in: bfloat16 [2, 4096, 768], P(None, ('blk', 'head')), may hold values from -6 to 6
- segment_ids: int32 [2, 4096], P(None, ('blk', 'head')), may hold values from 0 to 4, never falling along the last dimension, each value on 1 to 2000 neighbouring positions
- neighbour_valid: int32 [2, 64], P(None, ('blk', 'head')), may hold values 0 or 1
- neighbours: bfloat16 [2, 64, 2, 128, 768], P(None, ('blk', 'head')), may hold values from -6 to 6
- out_grad: bfloat16 [2, 4096, 768], P(None, ('blk', 'head')), may hold values from -6 to 6
- norm_attn: bfloat16 [768], P(('blk', 'head')), may hold values from 0.099609375 to 1.8984375
- w_qkv: bfloat16 [768, 2304], P(('blk', 'head')), may hold values from -0.21875 to 0.21875
- w_attn_out: bfloat16 [768, 768], P(('blk', 'head')), may hold values from -1.5 to 1.5
- norm_cross: bfloat16 [768], P(('blk', 'head')), may hold values from 0.099609375 to 1.8984375
- w_cross_q: bfloat16 [768, 768], P(('blk', 'head')), may hold values from -0.21875 to 0.21875
- w_cross_kv: bfloat16 [768, 1536], P(('blk', 'head')), may hold values from -0.21875 to 0.21875
- w_cross_out: bfloat16 [768, 768], P(('blk', 'head')), may hold values from -2 to 2
- norm_mlp: bfloat16 [768], P(('blk', 'head')), may hold values from 0.099609375 to 1.8984375
- w_up: bfloat16 [768, 3072], P(('blk', 'head')), may hold values from -0.21875 to 0.21875
- w_down: bfloat16 [3072, 768], P(('blk', 'head')), may hold values from -0.109375 to 0.109375
Outputs:
- output: bfloat16 [2, 4096, 768], P(None, ('blk', 'head'))
- grad_in: bfloat16 [2, 4096, 768], P(None, ('blk', 'head'))
- grad_neighbours: bfloat16 [2, 64, 2, 128, 768], P(None, ('blk', 'head'))
- grad_norm_attn: float32 [768], P(('blk', 'head'))
- grad_qkv: float32 [768, 2304], P(('blk', 'head'))
- grad_attn_out: float32 [768, 768], P(('blk', 'head'))
- grad_norm_cross: float32 [768], P(('blk', 'head'))
- grad_cross_q: float32 [768, 768], P(('blk', 'head'))
- grad_cross_kv: float32 [768, 1536], P(('blk', 'head'))
- grad_cross_out: float32 [768, 768], P(('blk', 'head'))
- grad_norm_mlp: float32 [768], P(('blk', 'head'))
- grad_up: float32 [768, 3072], P(('blk', 'head'))
- grad_down: float32 [3072, 768], P(('blk', 'head'))
Inputs may be any that keep to these rules, and one draw needn't show every extreme that they name: `segment_ids`: along each micro-batch's sequence the numbers never fall and count documents from 0; each document has 1 to 2000 tokens, and one has exactly 2000.
All inputs are finite; a program needn't handle non-finite values. No bound on the sum of `neighbour_valid` on one device may be relied on, other than what follows from the above.
Results may differ from a plain program's by a relative error of at most 0.024.
Values may be sent and summed in bfloat16 or wider, within the bound.
A program may use at most 256 MiB of HBM per device.

v0:
```python
import math

import jax
import jax.numpy as jnp
from jax import lax
from jax.sharding import PartitionSpec as P

HEADS = 12
HEAD_DIM = 64
SPAN = 64
NEIGHBOURS = 2
NEIGH_LEN = 128
DOC_MAX = 2000
MICRO = 2


def from_behind(value, axis, steps):
    count = lax.axis_size(axis)
    first, last = (max(0, -steps), min(count, count - steps))
    return lax.ppermute(value, axis, [(source, source + steps) for source in range(first, last)])


def layer_norm(values, norm_gain):
    centred = values - jnp.mean(values, axis=-1, keepdims=True)
    spread = jnp.mean(centred * centred, axis=-1, keepdims=True)
    return centred * lax.rsqrt(spread + 1e-05) * norm_gain


def norm_backward(values, norm_gain, grad_out):
    result, pullback = jax.vjp(layer_norm, values, norm_gain)
    return pullback(grad_out)


def gelu_tanh(values):
    return jax.nn.gelu(values, approximate=True)


def doc_positions(seg_ids):
    length = seg_ids.shape[0]
    token_index = jnp.arange(length, dtype=jnp.int32)
    starts = jnp.concatenate([jnp.ones((1,), jnp.bool_), seg_ids[1:] != seg_ids[:-1]])
    first_index = lax.cummax(jnp.where(starts, token_index, 0), axis=0)
    return token_index - first_index


def rotary(values, positions, direction):
    half_dim = values.shape[-1] // 2
    frequency = jnp.exp(
        jnp.arange(half_dim, dtype=jnp.float32) * (-2.0 * math.log(10000.0) / values.shape[-1])
    )
    angles = positions.astype(jnp.float32)[:, None] * frequency[None, :]
    cosine = jnp.cos(angles)[:, None, :]
    sine_part = direction * jnp.sin(angles)[:, None, :]
    first_half = values[..., :half_dim]
    second_half = values[..., half_dim:]
    return jnp.concatenate(
        [
            first_half * cosine - second_half * sine_part,
            second_half * cosine + first_half * sine_part,
        ],
        axis=-1,
    )


def gather_weights(shards):
    return (
        lax.all_gather(shards[0], ("blk", "head"), axis=0, tiled=True),
        lax.all_gather(shards[1], ("blk", "head"), axis=0, tiled=True),
        lax.all_gather(shards[2], ("blk", "head"), axis=0, tiled=True),
        lax.all_gather(shards[3], ("blk", "head"), axis=0, tiled=True),
        lax.all_gather(shards[4], ("blk", "head"), axis=0, tiled=True),
        lax.all_gather(shards[5], ("blk", "head"), axis=0, tiled=True),
        lax.all_gather(shards[6], ("blk", "head"), axis=0, tiled=True),
        lax.all_gather(shards[7], ("blk", "head"), axis=0, tiled=True),
        lax.all_gather(shards[8], ("blk", "head"), axis=0, tiled=True),
        lax.all_gather(shards[9], ("blk", "head"), axis=0, tiled=True),
    )


def to_heads(packed):
    return lax.all_to_all(packed, "head", split_axis=2, concat_axis=0, tiled=True)


def to_tokens(packed):
    return lax.all_to_all(packed, "head", split_axis=0, concat_axis=2, tiled=True)


def fetch_pairs(pairs, distance):
    return from_behind(pairs, "blk", distance)


def return_pairs(grad_piece, distance):
    return from_behind(grad_piece.astype(jnp.bfloat16), "blk", -distance).astype(grad_piece.dtype)


def send_lead(rows):
    return from_behind(rows, ("blk", "head"), -1)


def return_lead(rows):
    return from_behind(rows, ("blk", "head"), 1)


def soft_forward(scores):
    maximum = jnp.max(scores, axis=-1, keepdims=True)
    exp_rows = jnp.exp(scores - maximum)
    row_total = jnp.sum(exp_rows, axis=-1, keepdims=True)
    return (exp_rows / row_total, maximum + jnp.log(row_total))


def soft_backward(scores, log_total, grad_probs):
    attn_probs = jnp.exp(scores - log_total)
    row_delta = jnp.sum(attn_probs * grad_probs, axis=-1, keepdims=True)
    return (attn_probs, (attn_probs * (grad_probs - row_delta)).astype(jnp.bfloat16))


def self_scores(query_rows, key_rows, allowed, score_scale):
    scores = (
        jnp.einsum("qhd,khd->hqk", query_rows, key_rows, preferred_element_type=jnp.float32)
        * score_scale
    )
    return jnp.where(allowed[None], scores, -1e30)


def split_cross(query_groups, pair_groups):
    group_count, span_rows, model_width = query_groups.shape
    pair_rows = pair_groups.shape[1]
    query_rows = query_groups.reshape(group_count, span_rows, HEADS, HEAD_DIM)
    key_rows = pair_groups[..., :model_width].reshape(group_count, pair_rows, HEADS, HEAD_DIM)
    value_rows = pair_groups[..., model_width:].reshape(group_count, pair_rows, HEADS, HEAD_DIM)
    return (query_rows, key_rows, value_rows)


def cross_forward(query_groups, pair_groups, score_scale):
    group_count, span_rows, model_width = query_groups.shape
    query_rows, key_rows, value_rows = split_cross(query_groups, pair_groups)
    scores = (
        jnp.einsum("cqhd,ckhd->chqk", query_rows, key_rows, preferred_element_type=jnp.float32)
        * score_scale
    )
    attn_probs, log_total = soft_forward(scores)
    mixed_rows = jnp.einsum(
        "chqk,ckhd->cqhd",
        attn_probs.astype(jnp.bfloat16),
        value_rows,
        preferred_element_type=jnp.float32,
    )
    return (mixed_rows.reshape(group_count, span_rows, model_width), log_total)


def cross_backward(query_groups, pair_groups, log_total, grad_groups, score_scale):
    group_count, span_rows, model_width = query_groups.shape
    pair_rows = pair_groups.shape[1]
    query_rows, key_rows, value_rows = split_cross(query_groups, pair_groups)
    grad_rows = grad_groups.reshape(group_count, span_rows, HEADS, HEAD_DIM)
    scores = (
        jnp.einsum("cqhd,ckhd->chqk", query_rows, key_rows, preferred_element_type=jnp.float32)
        * score_scale
    )
    grad_probs = jnp.einsum(
        "cqhd,ckhd->chqk", grad_rows, value_rows, preferred_element_type=jnp.float32
    )
    attn_probs, grad_scores = soft_backward(scores, log_total, grad_probs)
    grad_query = (
        jnp.einsum("chqk,ckhd->cqhd", grad_scores, key_rows, preferred_element_type=jnp.float32)
        * score_scale
    )
    grad_key = (
        jnp.einsum("chqk,cqhd->ckhd", grad_scores, query_rows, preferred_element_type=jnp.float32)
        * score_scale
    )
    grad_value = jnp.einsum(
        "chqk,cqhd->ckhd",
        attn_probs.astype(jnp.bfloat16),
        grad_rows,
        preferred_element_type=jnp.float32,
    )
    grad_pairs = jnp.concatenate(
        [
            grad_key.reshape(group_count, pair_rows, model_width),
            grad_value.reshape(group_count, pair_rows, model_width),
        ],
        axis=-1,
    )
    return (grad_query.reshape(group_count, span_rows, model_width), grad_pairs)


def outer_total(lefts, rights):
    return jnp.einsum(
        "td,te->de",
        jnp.concatenate(lefts, axis=0),
        jnp.concatenate(rights, axis=0),
        preferred_element_type=jnp.float32,
    )


def on_device(
    hidden_in,
    segment_ids,
    neighbour_valid,
    neighbours,
    out_grad,
    norm_attn,
    w_qkv,
    w_attn_out,
    norm_cross,
    w_cross_q,
    w_cross_kv,
    w_cross_out,
    norm_mlp,
    w_up,
    w_down,
):
    shards = (
        norm_attn,
        w_qkv,
        w_attn_out,
        norm_cross,
        w_cross_q,
        w_cross_kv,
        w_cross_out,
        norm_mlp,
        w_up,
        w_down,
    )
    tok_count = hidden_in.shape[1]
    model_width = hidden_in.shape[2]
    head_groups = lax.axis_size("head")
    blk_count = lax.axis_size("blk")
    local_heads = HEADS // head_groups
    group_width = model_width // head_groups
    block_rows = tok_count * head_groups
    reach_blocks = (DOC_MAX + block_rows - 2) // block_rows
    key_count = (reach_blocks + 1) * block_rows
    span_count = tok_count // SPAN
    pair_rows = NEIGHBOURS * NEIGH_LEN
    lead_count = SPAN - 1
    kept_rows = tok_count - lead_count
    score_scale = 1.0 / math.sqrt(HEAD_DIM)
    device = lax.axis_index(("blk", "head"))
    token_start = device * tok_count
    block_start = lax.axis_index("blk") * block_rows
    all_segments, all_flags = (
        lax.all_gather(segment_ids, ("blk", "head"), axis=1, tiled=True),
        lax.all_gather(neighbour_valid, ("blk", "head"), axis=1, tiled=True),
    )
    gain_totals = None
    stash_n1, stash_raw, stash_att, stash_ga, stash_n2, stash_dcq = ([], [], [], [], [], [])
    stash_nb, stash_dp, stash_cm, stash_gc, stash_n3, stash_du, stash_act, stash_gy = (
        [],
        [],
        [],
        [],
        [],
        [],
        [],
        [],
    )
    outputs = []
    input_grads = []
    neigh_grads = []
    for micro_index in range(MICRO):
        full_weights = gather_weights(shards)
        gain_attn = full_weights[0].astype(jnp.float32)
        qkv_full = full_weights[1]
        attn_out_full = full_weights[2]
        gain_cross = full_weights[3].astype(jnp.float32)
        cross_q_full = full_weights[4]
        cross_kv_full = full_weights[5]
        cross_out_full = full_weights[6]
        gain_mlp = full_weights[7].astype(jnp.float32)
        up_full = full_weights[8]
        down_full = full_weights[9]
        seg_full = all_segments[micro_index]
        positions_full = doc_positions(seg_full)
        local_pos = lax.dynamic_slice_in_dim(positions_full, token_start, tok_count)
        hidden = hidden_in[micro_index].astype(jnp.float32)
        normed_attn = layer_norm(hidden, gain_attn).astype(jnp.bfloat16)
        raw_qkv = jnp.dot(normed_attn, qkv_full, preferred_element_type=jnp.float32).reshape(
            tok_count, 3, HEADS, HEAD_DIM
        )
        rotated = jnp.stack(
            [
                rotary(raw_qkv[:, 0], local_pos, 1.0),
                rotary(raw_qkv[:, 1], local_pos, 1.0),
                raw_qkv[:, 2],
            ],
            axis=1,
        )
        packed = rotated.astype(jnp.bfloat16).reshape(tok_count, 3, head_groups, group_width)
        head_rows = to_heads(packed)
        query_rows = head_rows[:, 0, 0].reshape(block_rows, local_heads, HEAD_DIM)
        own_pairs = head_rows[:, 1:, 0]
        far_pairs = [fetch_pairs(own_pairs, distance) for distance in range(reach_blocks, 0, -1)]
        key_pairs = jnp.concatenate(far_pairs + [own_pairs], axis=0)
        key_rows = key_pairs[:, 0].reshape(key_count, local_heads, HEAD_DIM)
        value_rows = key_pairs[:, 1].reshape(key_count, local_heads, HEAD_DIM)
        seg_padded = jnp.concatenate(
            [jnp.full((reach_blocks * block_rows,), -1, jnp.int32), seg_full]
        )
        key_segs = lax.dynamic_slice_in_dim(seg_padded, block_start, key_count)
        query_segs = lax.dynamic_slice_in_dim(seg_full, block_start, block_rows)
        key_place = jnp.arange(key_count, dtype=jnp.int32)[None, :]
        query_place = jnp.arange(block_rows, dtype=jnp.int32)[:, None] + reach_blocks * block_rows
        allowed = (query_segs[:, None] == key_segs[None, :]) & (key_place <= query_place)
        scores = self_scores(query_rows, key_rows, allowed, score_scale)
        attn_probs, attn_total = soft_forward(scores)
        attn_mixed = jnp.einsum(
            "hqk,khd->qhd",
            attn_probs.astype(jnp.bfloat16),
            value_rows,
            preferred_element_type=jnp.float32,
        )
        attn_mixed = attn_mixed.astype(jnp.bfloat16).reshape(block_rows, 1, 1, group_width)
        attended = to_tokens(attn_mixed).reshape(tok_count, model_width)
        after_attn = hidden + jnp.dot(attended, attn_out_full, preferred_element_type=jnp.float32)
        normed_cross = layer_norm(after_attn, gain_cross).astype(jnp.bfloat16)
        cross_query = jnp.dot(
            normed_cross, cross_q_full, preferred_element_type=jnp.float32
        ).astype(jnp.bfloat16)
        neigh_rows = neighbours[micro_index].reshape(span_count * pair_rows, model_width)
        pairs_local = (
            jnp.dot(neigh_rows, cross_kv_full, preferred_element_type=jnp.float32)
            .astype(jnp.bfloat16)
            .reshape(span_count, pair_rows, 2 * model_width)
        )
        flag_padded = jnp.concatenate(
            [jnp.zeros((1,), jnp.float32), all_flags[micro_index].astype(jnp.float32)]
        )
        group_flags = lax.dynamic_slice_in_dim(flag_padded, device * span_count, span_count + 1)
        lead_queries = send_lead(cross_query[:lead_count])
        query_groups = jnp.concatenate([cross_query[lead_count:], lead_queries], axis=0).reshape(
            span_count, SPAN, model_width
        )
        used_flags = group_flags[1:]
        cross_rows, cross_total = cross_forward(query_groups, pairs_local, score_scale)
        cross_rows = (
            (cross_rows * used_flags[:, None, None])
            .reshape(tok_count, model_width)
            .astype(jnp.bfloat16)
        )
        lead_out = return_lead(cross_rows[kept_rows:])
        cross_mixed = jnp.concatenate([lead_out, cross_rows[:kept_rows]], axis=0)
        after_cross = after_attn + jnp.dot(
            cross_mixed, cross_out_full, preferred_element_type=jnp.float32
        )
        normed_mlp = layer_norm(after_cross, gain_mlp).astype(jnp.bfloat16)
        mlp_upper = jnp.dot(normed_mlp, up_full, preferred_element_type=jnp.float32)
        activated, gelu_pull = jax.vjp(gelu_tanh, mlp_upper)
        activated = activated.astype(jnp.bfloat16)
        result_rows = after_cross + jnp.dot(
            activated, down_full, preferred_element_type=jnp.float32
        )
        outputs.append(result_rows.astype(jnp.bfloat16))
        cotangent = out_grad[micro_index].astype(jnp.float32)
        grad_low = cotangent.astype(jnp.bfloat16)
        d_activated = jnp.dot(grad_low, down_full.T, preferred_element_type=jnp.float32)
        d_upper = gelu_pull(d_activated)[0].astype(jnp.bfloat16)
        d_normed_mlp = jnp.dot(d_upper, up_full.T, preferred_element_type=jnp.float32)
        d_second_in, d_gain_mlp = norm_backward(after_cross, gain_mlp, d_normed_mlp)
        d_second = cotangent + d_second_in
        d_second_low = d_second.astype(jnp.bfloat16)
        d_mixed = jnp.dot(
            d_second_low, cross_out_full.T, preferred_element_type=jnp.float32
        ).astype(jnp.bfloat16)
        lead_grad = send_lead(d_mixed[:lead_count])
        d_rows = jnp.concatenate([d_mixed[lead_count:], lead_grad], axis=0).reshape(
            span_count, SPAN, model_width
        )
        d_groups = (d_rows.astype(jnp.float32) * used_flags[:, None, None]).astype(jnp.bfloat16)
        grad_query_groups, d_pairs = cross_backward(
            query_groups, pairs_local, cross_total, d_groups, score_scale
        )
        query_grad_rows = grad_query_groups.reshape(tok_count, model_width).astype(jnp.bfloat16)
        lead_query_grad = return_lead(query_grad_rows[kept_rows:])
        d_cross_query = jnp.concatenate([lead_query_grad, query_grad_rows[:kept_rows]], axis=0)
        d_pairs_low = d_pairs.astype(jnp.bfloat16).reshape(span_count * pair_rows, 2 * model_width)
        d_neigh = jnp.dot(d_pairs_low, cross_kv_full.T, preferred_element_type=jnp.float32).astype(
            jnp.bfloat16
        )
        neigh_grads.append(d_neigh.reshape(neighbours.shape[1:]))
        d_normed_cross = jnp.dot(d_cross_query, cross_q_full.T, preferred_element_type=jnp.float32)
        d_first_in, d_gain_cross = norm_backward(after_attn, gain_cross, d_normed_cross)
        d_first = d_second + d_first_in
        d_first_low = d_first.astype(jnp.bfloat16)
        d_attended = jnp.dot(
            d_first_low, attn_out_full.T, preferred_element_type=jnp.float32
        ).astype(jnp.bfloat16)
        d_head_rows = to_heads(d_attended.reshape(tok_count, 1, head_groups, group_width))[:, 0, 0]
        d_mix_rows = d_head_rows.reshape(block_rows, local_heads, HEAD_DIM)
        scores = self_scores(query_rows, key_rows, allowed, score_scale)
        grad_probs = jnp.einsum(
            "qhd,khd->hqk", d_mix_rows, value_rows, preferred_element_type=jnp.float32
        )
        attn_probs, grad_scores = soft_backward(scores, attn_total, grad_probs)
        d_query = (
            jnp.einsum("hqk,khd->qhd", grad_scores, key_rows, preferred_element_type=jnp.float32)
            * score_scale
        )
        d_key = (
            jnp.einsum("hqk,qhd->khd", grad_scores, query_rows, preferred_element_type=jnp.float32)
            * score_scale
        )
        d_value = jnp.einsum(
            "hqk,qhd->khd",
            attn_probs.astype(jnp.bfloat16),
            d_mix_rows,
            preferred_element_type=jnp.float32,
        )
        grad_kv = jnp.stack(
            [d_key.reshape(key_count, group_width), d_value.reshape(key_count, group_width)], axis=1
        )
        own_grad = grad_kv[reach_blocks * block_rows :]
        for distance in range(1, reach_blocks + 1):
            first_row = (reach_blocks - distance) * block_rows
            own_grad = own_grad + return_pairs(
                grad_kv[first_row : first_row + block_rows], distance
            )
        qkv_grad = jnp.concatenate(
            [
                d_query.astype(jnp.bfloat16).reshape(block_rows, 1, group_width),
                own_grad.astype(jnp.bfloat16),
            ],
            axis=1,
        )
        token_grad = (
            to_tokens(qkv_grad.reshape(block_rows, 3, 1, group_width))
            .reshape(tok_count, 3, HEADS, HEAD_DIM)
            .astype(jnp.float32)
        )
        raw_grad = jnp.stack(
            [
                rotary(token_grad[:, 0], local_pos, -1.0),
                rotary(token_grad[:, 1], local_pos, -1.0),
                token_grad[:, 2],
            ],
            axis=1,
        )
        raw_grad = raw_grad.reshape(tok_count, 3 * model_width).astype(jnp.bfloat16)
        d_normed_attn = jnp.dot(raw_grad, qkv_full.T, preferred_element_type=jnp.float32)
        d_hidden_in, d_gain_attn = norm_backward(hidden, gain_attn, d_normed_attn)
        input_grads.append((d_first + d_hidden_in).astype(jnp.bfloat16))
        stash_n1.append(normed_attn)
        stash_raw.append(raw_grad)
        stash_att.append(attended)
        stash_ga.append(d_first_low)
        stash_n2.append(normed_cross)
        stash_dcq.append(d_cross_query)
        stash_nb.append(neigh_rows)
        stash_dp.append(d_pairs_low)
        stash_cm.append(cross_mixed)
        stash_gc.append(d_second_low)
        stash_n3.append(normed_mlp)
        stash_du.append(d_upper)
        stash_act.append(activated)
        stash_gy.append(grad_low)
        gain_list = (d_gain_attn, d_gain_cross, d_gain_mlp)
        if gain_totals is None:
            gain_totals = gain_list
        else:
            gain_totals = jax.tree.map(
                lambda running, addend: running + addend, gain_totals, gain_list
            )
    grad_totals = (
        gain_totals[0],
        outer_total(stash_n1, stash_raw),
        outer_total(stash_att, stash_ga),
        gain_totals[1],
        outer_total(stash_n2, stash_dcq),
        outer_total(stash_nb, stash_dp),
        outer_total(stash_cm, stash_gc),
        gain_totals[2],
        outer_total(stash_n3, stash_du),
        outer_total(stash_act, stash_gy),
    )

    def split_rows(total):
        row_total = total.shape[0]
        col_total = total.shape[1] if total.ndim == 2 else 1
        return total.reshape(
            blk_count, head_groups, row_total // (blk_count * head_groups), col_total
        )

    halves = [split_rows(total) for total in grad_totals]
    swapped = (
        lax.all_to_all(
            halves[0].astype(jnp.bfloat16), "head", split_axis=1, concat_axis=1, tiled=True
        ).astype(jnp.float32),
        lax.all_to_all(
            halves[1].astype(jnp.bfloat16), "head", split_axis=1, concat_axis=1, tiled=True
        ).astype(jnp.float32),
        lax.all_to_all(
            halves[2].astype(jnp.bfloat16), "head", split_axis=1, concat_axis=1, tiled=True
        ).astype(jnp.float32),
        lax.all_to_all(
            halves[3].astype(jnp.bfloat16), "head", split_axis=1, concat_axis=1, tiled=True
        ).astype(jnp.float32),
        lax.all_to_all(
            halves[4].astype(jnp.bfloat16), "head", split_axis=1, concat_axis=1, tiled=True
        ).astype(jnp.float32),
        lax.all_to_all(
            halves[5].astype(jnp.bfloat16), "head", split_axis=1, concat_axis=1, tiled=True
        ).astype(jnp.float32),
        lax.all_to_all(
            halves[6].astype(jnp.bfloat16), "head", split_axis=1, concat_axis=1, tiled=True
        ).astype(jnp.float32),
        lax.all_to_all(
            halves[7].astype(jnp.bfloat16), "head", split_axis=1, concat_axis=1, tiled=True
        ).astype(jnp.float32),
        lax.all_to_all(
            halves[8].astype(jnp.bfloat16), "head", split_axis=1, concat_axis=1, tiled=True
        ).astype(jnp.float32),
        lax.all_to_all(
            halves[9].astype(jnp.bfloat16), "head", split_axis=1, concat_axis=1, tiled=True
        ).astype(jnp.float32),
    )
    combined = [jnp.sum(piece, axis=1) for piece in swapped]
    summed = (
        lax.psum_scatter(combined[0], "blk", scatter_dimension=0, tiled=True),
        lax.psum_scatter(combined[1], "blk", scatter_dimension=0, tiled=True),
        lax.psum_scatter(combined[2], "blk", scatter_dimension=0, tiled=True),
        lax.psum_scatter(combined[3], "blk", scatter_dimension=0, tiled=True),
        lax.psum_scatter(combined[4], "blk", scatter_dimension=0, tiled=True),
        lax.psum_scatter(combined[5], "blk", scatter_dimension=0, tiled=True),
        lax.psum_scatter(combined[6], "blk", scatter_dimension=0, tiled=True),
        lax.psum_scatter(combined[7], "blk", scatter_dimension=0, tiled=True),
        lax.psum_scatter(combined[8], "blk", scatter_dimension=0, tiled=True),
        lax.psum_scatter(combined[9], "blk", scatter_dimension=0, tiled=True),
    )
    shares = []
    for index_value in range(10):
        piece = summed[index_value][0]
        shares.append(piece.reshape(-1) if grad_totals[index_value].ndim == 1 else piece)
    return (
        jnp.stack(outputs),
        jnp.stack(input_grads),
        jnp.stack(neigh_grads),
        shares[0],
        shares[1],
        shares[2],
        shares[3],
        shares[4],
        shares[5],
        shares[6],
        shares[7],
        shares[8],
        shares[9],
    )


def solution(mesh):
    placed = (
        P(None, ("blk", "head"), None),
        P(None, ("blk", "head")),
        P(None, ("blk", "head")),
        P(None, ("blk", "head"), None, None, None),
        P(None, ("blk", "head"), None),
        P(("blk", "head")),
        P(("blk", "head"), None),
        P(("blk", "head"), None),
        P(("blk", "head")),
        P(("blk", "head"), None),
        P(("blk", "head"), None),
        P(("blk", "head"), None),
        P(("blk", "head")),
        P(("blk", "head"), None),
        P(("blk", "head"), None),
    )
    return jax.shard_map(
        on_device,
        mesh=mesh,
        in_specs=placed,
        out_specs=(
            P(None, ("blk", "head"), None),
            P(None, ("blk", "head"), None),
            P(None, ("blk", "head"), None, None, None),
            P(("blk", "head")),
            P(("blk", "head"), None),
            P(("blk", "head"), None),
            P(("blk", "head")),
            P(("blk", "head"), None),
            P(("blk", "head"), None),
            P(("blk", "head"), None),
            P(("blk", "head")),
            P(("blk", "head"), None),
            P(("blk", "head"), None),
        ),
        check_vma=False,
    )
```

profile of v0, /device:TPU:0, one launch (start us, length us, event | category | flops | bytes accessed | tf_op | source)
XLA Modules:
  0.0 1316.4 jit_solution(11401575240910480327)
XLA Ops:
  11.9 70.2 %all_gather.48 = s32[2,4096]{1,0:T(2,128)S(1)} all-gather(s32[2,128]{1,0:T(2,128)} %param.16), channel_id=1, replica_groups=mesh['blk'=16,'head'=2] {'blk','head'}, dimensions={1}, use_global_device_ids=true | all-gather | bytes 33792 | tf_op jit(solution)/shard_map/all_gather | solution.py:244
  89.1 37.6 %all-reduce.9 = (bf16[768]{0:T(1024)(128)(2,1)S(1)}, bf16[768]{0:T(1024)(128)(2,1)S(1)}, bf16[768]{0:T(1024)(128)(2,1)S(1)}) all-reduce(bf16[768]{0:T(1024)(128)(2,1)S(1)} %dynamic-update-slice, bf16[768]{0:T(1024)(128)(2,1)S(1)} %dynamic-update-slice.1, ...), channel_id=1, replica_groups=mesh['blk'=16,'head'=2] {'blk','head'}, use_global_device_ids=true, to_apply=%add.2 | all-reduce | flops 2304 | bytes 9216
  126.7 66.1 %all-gather = s32[32,2,2]{2,1,0:T(2,128)S(1)} all-gather(s32[1,2,2]{2,1,0:T(2,128)S(1)} %bitcast.539), channel_id=1, replica_groups=mesh['blk'=16,'head'=2] {'blk','head'}, dimensions={0}, use_global_device_ids=true | all-gather | bytes 528 | tf_op jit(solution)/shard_map/all_gather | solution.py:245
  261.1 23.8 %collective-permute-start.15 = (bf16[256,2,384]{2,0,1:T(8,128)(2,1)}, bf16[256,2,384]{2,0,1:T(8,128)(2,1)S(1)}, u32[]{:S(2)}, u32[]{:S(2)}) collective-permute-start(bf16[256,2,384]{2,0,1:T(8,128)(2,1)} %slice_bitcast_fusion.4), channel_id=1, source_target_pairs={{0,6},{2,8},{4,10},{6,12},{8,14},{10,16},{12,18},{14,20},{16,22},{... | collective-permute-start | bytes 1179656 | tf_op jit(solution)/shard_map/ppermute | solution.py:20
  290.9 13.5 %collective-permute-start.3 = (bf16[256,2,384]{2,0,1:T(8,128)(2,1)}, bf16[256,2,384]{2,0,1:T(8,128)(2,1)S(1)}, u32[]{:S(2)}, u32[]{:S(2)}) collective-permute-start(bf16[256,2,384]{2,0,1:T(8,128)(2,1)} %slice_bitcast_fusion.7), channel_id=1, source_target_pairs={{0,10},{2,12},{4,14},{6,16},{8,18},{10,20},{12,22},{14,24},{16,26}... | collective-permute-start | bytes 1179656 | tf_op jit(solution)/shard_map/ppermute | solution.py:20
  304.5 23.8 %collective-permute-start.2 = (bf16[256,2,384]{2,0,1:T(8,128)(2,1)}, bf16[256,2,384]{2,0,1:T(8,128)(2,1)S(1)}, u32[]{:S(2)}, u32[]{:S(2)}) collective-permute-start(bf16[256,2,384]{2,0,1:T(8,128)(2,1)} %slice_bitcast_fusion.7), channel_id=1, source_target_pairs={{0,12},{2,14},{4,16},{6,18},{8,20},{10,22},{12,24},{14,26},{16,28}... | collective-permute-start | bytes 1179656 | tf_op jit(solution)/shard_map/ppermute | solution.py:20
  328.5 38.1 %collective-permute-start.1 = (bf16[256,2,384]{2,0,1:T(8,128)(2,1)}, bf16[256,2,384]{2,0,1:T(8,128)(2,1)S(1)}, u32[]{:S(2)}, u32[]{:S(2)}) collective-permute-start(bf16[256,2,384]{2,0,1:T(8,128)(2,1)} %slice_bitcast_fusion.7), channel_id=1, source_target_pairs={{0,14},{2,16},{4,18},{6,20},{8,22},{10,24},{12,26},{14,28},{16,30}... | collective-permute-start | bytes 1179656 | tf_op jit(solution)/shard_map/ppermute | solution.py:20
  369.7 20.4 %collective-permute-done = bf16[256,2,384]{2,0,1:T(8,128)(2,1)S(1)} collective-permute-done((bf16[256,2,384]{2,0,1:T(8,128)(2,1)}, bf16[256,2,384]{2,0,1:T(8,128)(2,1)S(1)}, u32[]{:S(2)}, u32[]{:S(2)}) %collective-permute-start) | collective-permute-done | bytes 393248 | tf_op jit(solution)/shard_map/ppermute | solution.py:20
  392.1 42.1 %collective-permute-start.5 = (bf16[256,2,384]{2,0,1:T(8,128)(2,1)}, bf16[256,2,384]{2,0,1:T(8,128)(2,1)}, u32[]{:S(2)}, u32[]{:S(2)}) collective-permute-start(bf16[256,2,384]{2,0,1:T(8,128)(2,1)} %slice_bitcast_fusion.7), channel_id=1, source_target_pairs={{0,6},{2,8},{4,10},{6,12},{8,14},{10,16},{12,18},{14,20},{16,22},{... | collective-permute-start | bytes 1179656 | tf_op jit(solution)/shard_map/ppermute | solution.py:20
  467.3 7.6 fusion.61
  488.5 8.4 fusion.242
  659.4 9.2 fusion.6
  668.6 10.5 multiply_reduce_fusion
  737.1 12.4 multiply_reduce_fusion.1
  749.5 9.1 multiply_convert_fusion.1
  765.8 9.3 fusion.8
  807.3 9.1 collective-permute-done.35
  831.0 64.8 %collective-permute-done.29 = bf16[256,2,384]{2,0,1:T(8,128)(2,1)} collective-permute-done((bf16[256,2,384]{2,0,1:T(8,128)(2,1)}, bf16[256,2,384]{2,0,1:T(8,128)(2,1)}, u32[]{:S(2)}, u32[]{:S(2)}) %collective-permute-start.29) | collective-permute-done | bytes 393248 | tf_op jit(solution)/shard_map/ppermute | solution.py:20
  955.6 14.7 %all-to-all-done.13 = bf16[16,2,24,1536]{3,2,0,1:T(8,128)(2,1)} async-done(((bf16[16,2,24,1536]{3,2,0,1:T(8,128)(2,1)}), bf16[16,2,24,1536]{3,2,0,1:T(8,128)(2,1)}, u32[]{:S(2)}, u32[]{:S(2)}) %all-to-all-start.13) | async-done | bytes 2359328 | tf_op jit(solution)/shard_map/all_to_all | solution.py:501
  981.5 43.9 %all_to_all.164 = bf16[16,2,24,2304]{3,2,0,1:T(8,128)(2,1)S(1)} all-to-all(bf16[16,2,24,2304]{3,2,0,1:T(8,128)(2,1)S(1)} %copy.349), channel_id=1, replica_groups=mesh['blk'=16,'head'=2] {'head'}, dimensions={1} | all-to-all | bytes 7077888 | tf_op jit(solution)/shard_map/all_to_all | solution.py:489
  1031.2 56.4 %all_to_all.165 = bf16[16,2,24,3072]{3,2,0,1:T(8,128)(2,1)S(1)} all-to-all(bf16[16,2,24,3072]{3,2,0,1:T(8,128)(2,1)S(1)} %copy.356), channel_id=1, replica_groups=mesh['blk'=16,'head'=2] {'head'}, dimensions={1} | all-to-all | bytes 9437184 | tf_op jit(solution)/shard_map/all_to_all | solution.py:510
  1094.3 55.6 %all_to_all.166 = bf16[16,2,96,768]{3,2,0,1:T(8,128)(2,1)S(1)} all-to-all(bf16[16,2,96,768]{3,2,0,1:T(8,128)(2,1)S(1)} %copy.357), channel_id=1, replica_groups=mesh['blk'=16,'head'=2] {'head'}, dimensions={1} | all-to-all | bytes 9437184 | tf_op jit(solution)/shard_map/all_to_all | solution.py:513
  1189.0 66.4 %all-reduce.8 = (f32[16,24,1]{1,2,0:T(1,128)S(1)}, f32[16,24,1]{1,2,0:T(1,128)S(1)}, f32[16,24,1]{1,2,0:T(1,128)S(1)}) all-reduce(f32[16,24,1]{1,2,0:T(1,128)S(1)} %bitcast.535, f32[16,24,1]{1,2,0:T(1,128)S(1)} %bitcast.534, f32[16,24,1]{1,2,0:T(1,128)S(1)} %bitcast.533), channel_id=2, replica_groups=mesh['blk'=16,'head'=2] {'blk'}, use_global_device_ids=true, to_apply=%region_43.44.clone | all-reduce | flops 1152 | bytes 9216
  1258.9 50.8 %reduce-scatter.20.cloned.1.call-done = f32[1,96,768]{2,1,0:T(8,128)} async-done(((f32[16,96,768]{2,1,0:T(8,128)}), f32[1,96,768]{2,1,0:T(8,128)}) %reduce-scatter.20.cloned.1.call-update) | async-done | bytes 294928 | tf_op jit(solution)/shard_map/reduce_scatter | solution.py:528
  (926 shorter events, 534.5 us)
Async XLA Ops:
  7.2 192.4 %all-gather.13.cloned.1.call-start = ((), (), s32[]{:S(2)}) async-start(), calls=%async_computation.27 | async-start | bytes 2433024 | tf_op jit(solution)/shard_map/all_gather | solution.py:72
  7.9 199.5 %all-gather.9.cloned.1.call-start = ((), (), s32[]{:S(2)}) async-start(), calls=%async_computation.25 | async-start | bytes 3649536 | tf_op jit(solution)/shard_map/all_gather | solution.py:68
  8.7 508.7 %all-gather.11.cloned.1.call-start = ((), (), s32[]{:S(2)}) async-start(), calls=%async_computation.26 | async-start | bytes 1216512 | tf_op jit(solution)/shard_map/all_gather | solution.py:69
  9.4 510.5 %all-gather.15.cloned.1.call-start = ((), (), s32[]{:S(2)}) async-start(), calls=%async_computation.28 | async-start | bytes 1216512 | tf_op jit(solution)/shard_map/all_gather | solution.py:71
  10.0 530.0 %all-gather.17.cloned.1.call-start = ((), (), s32[]{:S(2)}) async-start(), calls=%async_computation.29 | async-start | bytes 1216512 | tf_op jit(solution)/shard_map/all_gather | solution.py:73
  10.6 536.8 %all-gather.19.cloned.1.call-start = ((), (), s32[]{:S(2)}) async-start(), calls=%async_computation.30 | async-start | bytes 4866048 | tf_op jit(solution)/shard_map/all_gather | solution.py:75
  11.1 541.2 %all-gather.21.cloned.1.call-start = ((), (), s32[]{:S(2)}) async-start(), calls=%async_computation.31 | async-start | bytes 4866048 | tf_op jit(solution)/shard_map/all_gather | solution.py:76
  249.9 116.7 %collective-permute-start.17 = (bf16[256,2,384]{2,0,1:T(8,128)(2,1)}, bf16[256,2,384]{2,0,1:T(8,128)(2,1)S(1)}, u32[]{:S(2)}, u32[]{:S(2)}) collective-permute-start(bf16[256,2,384]{2,0,1:T(8,128)(2,1)} %slice_bitcast_fusion.4), channel_id=1, source_target_pairs={{0,2},{2,4},{4,6},{6,8},{8,10},{10,12},{12,14},{14,16},{16,18},{18... | collective-permute-start | bytes 1179656 | tf_op jit(solution)/shard_map/ppermute | solution.py:20
  287.7 161.5 %collective-permute-start.7 = (bf16[256,2,384]{2,0,1:T(8,128)(2,1)}, bf16[256,2,384]{2,0,1:T(8,128)(2,1)}, u32[]{:S(2)}, u32[]{:S(2)}) collective-permute-start(bf16[256,2,384]{2,0,1:T(8,128)(2,1)} %slice_bitcast_fusion.7), channel_id=1, source_target_pairs={{0,2},{2,4},{4,6},{6,8},{8,10},{10,12},{12,14},{14,16},{16,18},{18... | collective-permute-start | bytes 1179656 | tf_op jit(solution)/shard_map/ppermute | solution.py:20
  290.9 145.5 %collective-permute-start.3 = (bf16[256,2,384]{2,0,1:T(8,128)(2,1)}, bf16[256,2,384]{2,0,1:T(8,128)(2,1)S(1)}, u32[]{:S(2)}, u32[]{:S(2)}) collective-permute-start(bf16[256,2,384]{2,0,1:T(8,128)(2,1)} %slice_bitcast_fusion.7), channel_id=1, source_target_pairs={{0,10},{2,12},{4,14},{6,16},{8,18},{10,20},{12,22},{14,24},{16,26}... | collective-permute-start | bytes 1179656 | tf_op jit(solution)/shard_map/ppermute | solution.py:20
  304.5 129.8 %collective-permute-start.2 = (bf16[256,2,384]{2,0,1:T(8,128)(2,1)}, bf16[256,2,384]{2,0,1:T(8,128)(2,1)S(1)}, u32[]{:S(2)}, u32[]{:S(2)}) collective-permute-start(bf16[256,2,384]{2,0,1:T(8,128)(2,1)} %slice_bitcast_fusion.7), channel_id=1, source_target_pairs={{0,12},{2,14},{4,16},{6,18},{8,20},{10,22},{12,24},{14,26},{16,28}... | collective-permute-start | bytes 1179656 | tf_op jit(solution)/shard_map/ppermute | solution.py:20
  707.8 94.3 %collective-permute-start.39 = (bf16[256,2,384]{2,0,1:T(8,128)(2,1)}, bf16[256,2,384]{2,0,1:T(8,128)(2,1)}, u32[]{:S(2)}, u32[]{:S(2)}) collective-permute-start(bf16[256,2,384]{2,0,1:T(8,128)(2,1)} %get-tuple-element.50), channel_id=1, source_target_pairs={{16,0},{18,2},{20,4},{22,6},{24,8},{26,10},{28,12},{30,14},{17,1},... | collective-permute-start | bytes 1179656 | tf_op jit(solution)/shard_map/ppermute | solution.py:20
  709.1 94.3 %collective-permute-start.38 = (bf16[256,2,384]{2,0,1:T(8,128)(2,1)}, bf16[256,2,384]{2,0,1:T(8,128)(2,1)}, u32[]{:S(2)}, u32[]{:S(2)}) collective-permute-start(bf16[256,2,384]{2,0,1:T(8,128)(2,1)} %get-tuple-element.51), channel_id=1, source_target_pairs={{14,0},{16,2},{18,4},{20,6},{22,8},{24,10},{26,12},{28,14},{30,16}... | collective-permute-start | bytes 1179656 | tf_op jit(solution)/shard_map/ppermute | solution.py:20
  710.4 94.3 %collective-permute-start.37 = (bf16[256,2,384]{2,0,1:T(8,128)(2,1)}, bf16[256,2,384]{2,0,1:T(8,128)(2,1)}, u32[]{:S(2)}, u32[]{:S(2)}) collective-permute-start(bf16[256,2,384]{2,0,1:T(8,128)(2,1)} %get-tuple-element.52), channel_id=1, source_target_pairs={{12,0},{14,2},{16,4},{18,6},{20,8},{22,10},{24,12},{26,14},{28,16}... | collective-permute-start | bytes 1179656 | tf_op jit(solution)/shard_map/ppermute | solution.py:20
  711.7 94.3 %collective-permute-start.36 = (bf16[256,2,384]{2,0,1:T(8,128)(2,1)}, bf16[256,2,384]{2,0,1:T(8,128)(2,1)}, u32[]{:S(2)}, u32[]{:S(2)}) collective-permute-start(bf16[256,2,384]{2,0,1:T(8,128)(2,1)} %get-tuple-element.53), channel_id=1, source_target_pairs={{10,0},{12,2},{14,4},{16,6},{18,8},{20,10},{22,12},{24,14},{26,16}... | collective-permute-start | bytes 1179656 | tf_op jit(solution)/shard_map/ppermute | solution.py:20
  763.1 495.8 %reduce-scatter.16.cloned.1.call-start = ((), (), s32[]{:S(2)}) async-start(), calls=%async_computation.36 | async-start | bytes 1253376 | tf_op jit(solution)/shard_map/reduce_scatter | solution.py:525
  792.9 118.9 %all-to-all-start.10 = ((bf16[16,2,24,768]{3,2,0,1:T(8,128)(2,1)}), bf16[16,2,24,768]{3,2,0,1:T(8,128)(2,1)}, u32[]{:S(2)}, u32[]{:S(2)}) async-start(bf16[16,2,24,768]{3,2,0,1:T(8,128)(2,1)} %copy.350), calls=%async_computation.11 | async-start | bytes 2359296 | tf_op jit(solution)/shard_map/all_to_all | solution.py:492
  797.4 461.4 %reduce-scatter.12.cloned.1.call-start = ((), (), s32[]{:S(2)}) async-start(), calls=%async_computation.34 | async-start | bytes 1253376 | tf_op jit(solution)/shard_map/reduce_scatter | solution.py:523
  806.0 89.8 %collective-permute-start.29 = (bf16[256,2,384]{2,0,1:T(8,128)(2,1)}, bf16[256,2,384]{2,0,1:T(8,128)(2,1)}, u32[]{:S(2)}, u32[]{:S(2)}) collective-permute-start(bf16[256,2,384]{2,0,1:T(8,128)(2,1)} %get-tuple-element.58), channel_id=1, source_target_pairs={{16,0},{18,2},{20,4},{22,6},{24,8},{26,10},{28,12},{30,14},{17,1},... | collective-permute-start | bytes 1179656 | tf_op jit(solution)/shard_map/ppermute | solution.py:20
  915.4 343.4 %reduce-scatter.10.cloned.1.call-start = ((), (), s32[]{:S(2)}) async-start(), calls=%async_computation.33 | async-start | bytes 1253376 | tf_op jit(solution)/shard_map/reduce_scatter | solution.py:521
  942.8 316.1 %reduce-scatter.14.cloned.1.call-start = ((), (), s32[]{:S(2)}) async-start(), calls=%async_computation.35 | async-start | bytes 2506752 | tf_op jit(solution)/shard_map/reduce_scatter | solution.py:524
  974.1 284.8 %reduce-scatter.8.cloned.1.call-start = ((), (), s32[]{:S(2)}) async-start(), calls=%async_computation.32 | async-start | bytes 3760128 | tf_op jit(solution)/shard_map/reduce_scatter | solution.py:520
  1027.9 231.0 %reduce-scatter.18.cloned.1.call-start = ((), (), s32[]{:S(2)}) async-start(), calls=%async_computation.37 | async-start | bytes 5013504 | tf_op jit(solution)/shard_map/reduce_scatter | solution.py:527
  1090.9 218.8 %reduce-scatter.20.cloned.1.call-start = ((), (), s32[]{:S(2)}) async-start(), calls=%async_computation.38 | async-start | bytes 5013504 | tf_op jit(solution)/shard_map/reduce_scatter | solution.py:528
  (262 other events, 3899.5 us)
Sparse Core Ops, SparseCore 0:
  10.9 60.0 all-gather.12
  74.0 59.3 all-gather.8
  136.3 53.1 all-gather.10
  192.3 56.1 all-gather.14
  251.3 68.0 all-gather.16
  322.1 74.7 all-gather.18
  399.9 72.8 all-gather.20
  768.1 81.2 reduce-scatter.15
  853.7 65.2 reduce-scatter.11
  923.0 89.8 reduce-scatter.9
  1017.2 61.9 reduce-scatter.13
  1084.0 67.0 reduce-scatter.7
  1156.0 74.6 reduce-scatter.17
  1235.0 74.6 reduce-scatter.19
where the time goes:
time: 1330 us; the launch traced here: 1320 us
  blocking collectives  396 us (30%)
  starting transfers between devices  273 us (21%)
  waiting for transfers between devices  223 us (17%)
  matrix products  168 us (13%)
  local copies, waits for them, and re-layouts  139 us (10%)
  other arithmetic  99.9 us (8%)
  between operations  18.2 us (1%)
    ppermute x40, starting transfers between devices, from_behind(): lax.ppermute(value, axis, [(source, source + steps) for source in range(f...  212 us
    ppermute x40, waiting for transfers between devices, from_behind(): lax.ppermute(value, axis, [(source, source + steps) for source in range(f...  132 us
    unnamed x2, blocking collectives  104 us
    all_gather x1, blocking collectives, on_device(): lax.all_gather(segment_ids, ('blk', 'head'), axis=1, tiled=True)  70.2 us
    all_gather x1, blocking collectives, on_device(): lax.all_gather(neighbour_valid, ('blk', 'head'), axis=1, tiled=True)  66.1 us
    all_to_all x1, blocking collectives, on_device(): lax.all_to_all(halves[8].astype(jnp.bfloat16), 'head', split_axis=1, conc...  56.4 us
    all_to_all x1, blocking collectives, on_device(): lax.all_to_all(halves[9].astype(jnp.bfloat16), 'head', split_axis=1, conc...  55.6 us
    reduce_scatter x1, waiting for transfers between devices, on_device(): lax.psum_scatter(combined[9], 'blk', scatter_dimension=0, tiled=True)  50.8 us
  transfers between devices with their start and end apart: 69, of which 22 were waited for; matrix products, arithmetic and copies ran while one was open for 26% of the time, Pallas kernels for 0%

commit v1 on v0

v1 whole, which is shorter than its diff:
```python
import functools
import math

import jax
import jax.numpy as jnp
from jax import lax
from jax.experimental import pallas as pl
from jax.experimental.pallas import tpu as pltpu
from jax.sharding import PartitionSpec as P

MESH = pl.DeviceIdType.MESH
ANY = pl.BlockSpec(memory_space=pl.ANY)


def coords():
    blk = lax.axis_index("blk")
    return blk // 4, (blk // 2) % 2, blk % 2, lax.axis_index("head")


def place(z, y, c, x):
    return (z * 4 + y * 2 + c, x)


def loop(count, body):
    if count <= 8:
        for step in range(count):
            body(step)
    else:
        lax.fori_loop(0, count, lambda step, carry: (body(step), carry)[1], 0)


def all_barrier(total, me):
    barrier = pltpu.get_barrier_semaphore()

    def greet(step, carry):
        peer = lax.rem(me + step, total)
        pl.semaphore_signal(
            barrier, inc=1, device_id=(peer // 2, lax.rem(peer, 2)), device_id_type=MESH
        )
        return carry

    lax.fori_loop(1, total, greet, 0)
    pl.semaphore_wait(barrier, total - 1)


def remote(src, dst, send, recv, where):
    return pltpu.make_async_remote_copy(
        src_ref=src, dst_ref=dst, send_sem=send, recv_sem=recv, device_id=where, device_id_type=MESH
    )


def gather_kernel(depth, items, *refs):
    count = len(items)
    w_refs = refs[:5]
    small_ref, hid_ref, grad_ref = refs[5:8]
    out_refs = refs[8:11]
    small_out, lead_hid, lead_grad = refs[11:14]
    own_sem, send_sem, recv_sem, misc_sem, lead_send, lead_recv = refs[14:]
    z, y, c, x = coords()
    total = depth * 8
    me = lax.axis_index("blk") * 2 + lax.axis_index("head")
    rows_per = w_refs[0].shape[0]

    def view(item, zs, ys, cs, xs):
        buffer, first, last, kind = item
        return out_refs[buffer].at[pl.ds(first, last - first), zs, ys, cs, xs]

    all_barrier(total, me)
    own_small = pltpu.make_async_copy(small_ref, small_out.at[me], misc_sem.at[1])
    own_small.start()

    def send_small(step, carry):
        peer = lax.rem(me + step, total)
        remote(
            small_ref, small_out.at[me], misc_sem.at[0], misc_sem.at[1], (peer // 2, lax.rem(peer, 2))
        ).start()
        return carry

    own = []
    for index, item in enumerate(items):
        buffer, first, last, kind = item
        width = out_refs[buffer].shape[-1]
        copies = []
        for block in range(first, last):
            if buffer == 1:
                src = w_refs[1 + block]
            else:
                src = w_refs[2 * buffer].at[:, pl.ds(block * width, width)]
            copies.append((src, out_refs[buffer].at[block, z, y, c, x]))
        for src, dst in copies:
            copy = pltpu.make_async_copy(src, dst, own_sem.at[index])
            copy.start()
        own.append(pltpu.make_async_copy(view(item, z, y, c, x), view(item, z, y, c, x), own_sem.at[index]))
    lax.fori_loop(1, total, send_small, 0)
    prev = lax.rem(me + total - 1, total)
    prev_at = (prev // 2, lax.rem(prev, 2))
    leads = [
        remote(hid_ref.at[:, pl.ds(0, 64)], lead_hid, lead_send.at[0], lead_recv.at[0], prev_at),
        remote(grad_ref.at[:, pl.ds(0, 64)], lead_grad, lead_send.at[1], lead_recv.at[1], prev_at),
    ]

    whole = slice(None)

    def phase_one(index):
        own[index].wait()
        item = items[index]

        def send(step):
            other = lax.rem(z + step + 1, depth)
            remote(
                view(item, z, y, c, x), view(item, z, y, c, x),
                send_sem.at[index, 0], recv_sem.at[index, 0], place(other, y, c, x),
            ).start()

        loop(depth - 1, send)

    def bulk(index, phase):
        item = items[index]
        first_x = item[3] == 0
        if phase == 1:
            ref = view(item, whole, y, c, x)
            where = place(z, y, c, 1 - x) if first_x else place(z, 1 - y, c, x)
        elif phase == 2:
            ref = view(item, whole, y, c, whole) if first_x else view(item, whole, whole, c, x)
            where = place(z, 1 - y, c, x) if first_x else place(z, y, c, 1 - x)
        else:
            ref = view(item, whole, whole, c, whole)
            where = place(z, y, 1 - c, x)
        return remote(ref, ref, send_sem.at[index, phase], recv_sem.at[index, phase], where)

    def arrived(index, phase):
        item = items[index]
        if phase == 0:
            ref = view(item, pl.ds(0, depth - 1), y, c, x)
            pltpu.make_async_copy(ref, ref, recv_sem.at[index, 0]).wait()
        else:
            bulk(index, phase).wait_recv()

    def sent(index, phase):
        item = items[index]
        if phase == 0:
            ref = view(item, pl.ds(0, depth - 1), y, c, x)
            pltpu.make_async_copy(ref, ref, send_sem.at[index, 0]).wait()
        else:
            bulk(index, phase).wait_send()

    pairs = (count + 1) // 2
    for step in range(pairs + 2 * 4):
        for phase in range(4, -1, -1):
            pair = step - 2 * phase
            if not 0 <= pair < pairs:
                continue
            for index in range(2 * pair, min(2 * pair + 2, count)):
                if phase == 0:
                    phase_one(index)
                else:
                    arrived(index, phase - 1)
                    if phase < 4:
                        bulk(index, phase).start()
        if step == 0:
            for lead in leads:
                lead.start()
    for index in range(count):
        for phase in range(4):
            sent(index, phase)
    for lead in leads:
        lead.wait()
    pltpu.make_async_copy(small_out, small_out, misc_sem.at[1]).wait()
    rest = small_out.at[pl.ds(0, total - 1)]
    pltpu.make_async_copy(rest, rest, misc_sem.at[0]).wait()


def gather_all(depth, w_qkv, w_attn_out, w_cross_q, w_cross_out, w_kv, small, hidden, grads):
    total = depth * 8
    rows = w_qkv.shape[0]
    items = [
        (0, 0, 3, 0), (0, 3, 6, 1),
        (2, 0, 1, 0), (2, 1, 2, 1),
        (1, 0, 1, 0), (1, 1, 2, 1),
        (1, 2, 3, 0),
    ]
    shapes = [
        (6, depth, 2, 2, 2, rows, w_qkv.shape[1] // 6),
        (3, depth, 2, 2, 2, rows, w_attn_out.shape[1]),
        (2, depth, 2, 2, 2, rows, w_kv.shape[1] // 2),
    ]
    lead_shape = (hidden.shape[0], 64, hidden.shape[2])
    outs = [jax.ShapeDtypeStruct(shape, jnp.bfloat16) for shape in shapes]
    outs += [jax.ShapeDtypeStruct((total,) + small.shape, small.dtype)]
    outs += [jax.ShapeDtypeStruct(lead_shape, jnp.bfloat16)] * 2
    count = len(items)
    return pl.pallas_call(
        functools.partial(gather_kernel, depth, items),
        out_shape=outs,
        in_specs=[ANY] * 8,
        out_specs=[ANY] * 6,
        scratch_shapes=[
            pltpu.SemaphoreType.DMA((count,)),
            pltpu.SemaphoreType.DMA((count, 4)),
            pltpu.SemaphoreType.DMA((count, 4)),
            pltpu.SemaphoreType.DMA((2,)),
            pltpu.SemaphoreType.DMA((2,)),
            pltpu.SemaphoreType.DMA((2,)),
        ],
        compiler_params=pltpu.CompilerParams(collective_id=0, has_side_effects=True),
    )(w_qkv, w_attn_out, w_cross_q, w_cross_out, w_kv, small, hidden, grads)


def unit_of(device, total):
    if total == 32:
        depth = device // 8
        middle = (depth == 1) | (depth == 2)
        end = 16 + (depth // 3) * 4 + (lax.rem(device, 8) // 4) * 2 + lax.rem(device, 2)
        unit = jnp.where(middle, device - 8, end)
        return unit, middle | (lax.rem(device // 2, 2) == 0)
    stride = total // UNITS
    return jnp.minimum(device // stride, UNITS - 1), (lax.rem(device, stride) == 0) & (device // stride < UNITS)


def to_units_kernel(total, src, dst, send_sem, recv_sem):
    me = lax.axis_index("blk") * 2 + lax.axis_index("head")
    mine, holder = unit_of(me, total)
    all_barrier(total, me)
    lanes = src.shape[-1]

    def slot(device):
        return dst.at[:, :, pl.ds(pl.multiple_of(device * lanes, 128), lanes)]

    @pl.when(holder)
    def _():
        pltpu.make_async_copy(src.at[mine], slot(me), recv_sem).start()

    def send(step, carry):
        peer = lax.rem(me + step, total)
        unit, held = unit_of(peer, total)

        @pl.when(held)
        def _():
            remote(src.at[unit], slot(me), send_sem, recv_sem, (peer // 2, lax.rem(peer, 2))).start()

        return carry

    lax.fori_loop(1, total, send, 0)

    @pl.when(holder)
    def _():
        part = src.at[pl.ds(0, UNITS - 1)]
        pltpu.make_async_copy(dst, dst, recv_sem).wait()
        pltpu.make_async_copy(part, part, send_sem).wait()

    @pl.when(jnp.logical_not(holder))
    def _():
        pltpu.make_async_copy(src, src, send_sem).wait()


def to_units(total, message, collective):
    units, parts, width, lanes = message.shape
    return pl.pallas_call(
        functools.partial(to_units_kernel, total),
        out_shape=jax.ShapeDtypeStruct((parts, width, lanes * total), message.dtype),
        in_specs=[ANY],
        out_specs=ANY,
        scratch_shapes=[pltpu.SemaphoreType.DMA, pltpu.SemaphoreType.DMA],
        compiler_params=pltpu.CompilerParams(collective_id=collective, has_side_effects=True),
    )(message)


def to_tokens_kernel(total, extras, *refs):
    src = refs[0]
    extra_in = refs[1 : 1 + extras]
    dst = refs[1 + extras]
    extra_out = refs[2 + extras : 2 + 2 * extras]
    send_sem, recv_sem, extra_send, extra_recv = refs[2 + 2 * extras :]
    me = lax.axis_index("blk") * 2 + lax.axis_index("head")
    mine, holder = unit_of(me, total)
    all_barrier(total, me)
    lanes = dst.shape[-1]
    after = lax.rem(me + 1, total)
    moves = [
        remote(
            extra_in[index], extra_out[index], extra_send.at[index], extra_recv.at[index],
            (after // 2, lax.rem(after, 2)),
        )
        for index in range(extras)
    ]
    for move in moves:
        move.start()

    def slot(device):
        return src.at[:, :, pl.ds(pl.multiple_of(device * lanes, 128), lanes)]

    @pl.when(holder)
    def _():
        pltpu.make_async_copy(slot(me), dst.at[mine], recv_sem).start()

        def send(step, carry):
            peer = lax.rem(me + step, total)
            remote(
                slot(peer), dst.at[mine], send_sem, recv_sem, (peer // 2, lax.rem(peer, 2))
            ).start()
            return carry

        lax.fori_loop(1, total, send, 0)

    pltpu.make_async_copy(dst, dst, recv_sem).wait()

    @pl.when(holder)
    def _():
        part = src.at[:, :, pl.ds(0, lanes * (total - 1))]
        pltpu.make_async_copy(part, part, send_sem).wait()

    for move in moves:
        move.wait()


def to_tokens(total, units, extra, collective):
    parts, width, length = units.shape
    count = len(extra)
    result = jax.ShapeDtypeStruct((UNITS, parts, width, length // total), units.dtype)
    return pl.pallas_call(
        functools.partial(to_tokens_kernel, total, count),
        out_shape=[result] + [jax.ShapeDtypeStruct(e.shape, e.dtype) for e in extra],
        in_specs=[ANY] * (1 + count),
        out_specs=[ANY] * (1 + count),
        scratch_shapes=[
            pltpu.SemaphoreType.DMA,
            pltpu.SemaphoreType.DMA,
            pltpu.SemaphoreType.DMA((max(count, 1),)),
            pltpu.SemaphoreType.DMA((max(count, 1),)),
        ],
        compiler_params=pltpu.CompilerParams(collective_id=collective, has_side_effects=True),
    )(units, *extra)


def scatter_kernel(depth, items, *refs):
    count = len(items)
    total = depth * 8
    d_refs = refs[:3]
    gain_ref = refs[3]
    out_refs = refs[4:7]
    gain_out = refs[7]
    own = refs[8 : 8 + count]
    got_core = refs[8 + count : 8 + 2 * count]
    got_one = refs[8 + 2 * count : 8 + 3 * count]
    got_two = refs[8 + 3 * count : 8 + 4 * count]
    got_z = refs[8 + 4 * count : 8 + 5 * count]
    gains, local_sem, send_sem, recv_sem, gain_sem = refs[8 + 5 * count :]
    z, y, c, x = coords()
    me = lax.axis_index("blk") * 2 + lax.axis_index("head")
    all_barrier(total, me)
    whole = slice(None)

    pltpu.make_async_copy(gain_ref.at[me], gains.at[me], gain_sem.at[1]).start()

    def send_gain(step, carry):
        peer = lax.rem(me + step, total)
        remote(
            gain_ref.at[peer], gains.at[me], gain_sem.at[0], gain_sem.at[1], (peer // 2, lax.rem(peer, 2))
        ).start()
        return carry

    def local(index):
        buffer, first, last, kind = items[index]
        src = d_refs[buffer].at[pl.ds(first, last - first), whole, whole, c]
        return pltpu.make_async_copy(src, own[index], local_sem.at[index])

    def core(index):
        buffer, first, last, kind = items[index]
        src = d_refs[buffer].at[pl.ds(first, last - first), whole, whole, 1 - c]
        return remote(
            src, got_core[index], send_sem.at[index, 0], recv_sem.at[index, 0], place(z, y, 1 - c, x)
        )

    def one(index):
        if items[index][3] == 0:
            src, where = own[index].at[whole, whole, 1 - y], place(z, 1 - y, c, x)
        else:
            src, where = own[index].at[whole, whole, whole, 1 - x], place(z, y, c, 1 - x)
        return remote(src, got_one[index], send_sem.at[index, 1], recv_sem.at[index, 1], where)

    def two(index):
        if items[index][3] == 0:
            src, where = own[index].at[whole, whole, y, 1 - x], place(z, y, c, 1 - x)
        else:
            src, where = own[index].at[whole, whole, 1 - y, x], place(z, 1 - y, c, x)
        return remote(src, got_two[index], send_sem.at[index, 2], recv_sem.at[index, 2], where)

    def send_z(index):
        def send(step):
            other = lax.rem(z + step + 1, depth)
            remote(
                own[index].at[whole, other, y, x], got_z[index].at[z],
                send_sem.at[index, 3], recv_sem.at[index, 3], place(other, y, c, x),
            ).start()

        loop(depth - 1, send)

    def add_into(target, source):
        target[...] = (target[...].astype(jnp.float32) + source[...].astype(jnp.float32)).astype(
            jnp.bfloat16
        )

    def sum_core(index):
        blocks = own[index].shape[0]

        def body(step):
            block, level = step // depth, lax.rem(step, depth)
            for row in range(2):
                for col in range(2):
                    add_into(own[index].at[block, level, row, col], got_core[index].at[block, level, row, col])

        lax.fori_loop(0, blocks * depth, lambda step, carry: (body(step), carry)[1], 0)

    def sum_one(index):
        blocks = own[index].shape[0]

        def body(step):
            block, level = step // depth, lax.rem(step, depth)
            for side in range(2):
                if items[index][3] == 0:
                    target = own[index].at[block, level, y, side]
                else:
                    target = own[index].at[block, level, side, x]
                add_into(target, got_one[index].at[block, level, side])

        lax.fori_loop(0, blocks * depth, lambda step, carry: (body(step), carry)[1], 0)

    def sum_two(index):
        blocks = own[index].shape[0]

        def body(step):
            block, level = step // depth, lax.rem(step, depth)
            add_into(own[index].at[block, level, y, x], got_two[index].at[block, level])

        lax.fori_loop(0, blocks * depth, lambda step, carry: (body(step), carry)[1], 0)

    def sum_z(index):
        buffer, first, last, kind = items[index]
        for block in range(last - first):
            running = own[index][block, z, y, x].astype(jnp.float32)

            def body(step, value):
                other = lax.rem(z + step, depth)
                return value + got_z[index][other, block].astype(jnp.float32)

            out_refs[buffer][first + block] = lax.fori_loop(1, depth, body, running)

    for index in range(count):
        local(index).start()
    pairs = (count + 1) // 2
    for step in range(pairs + 4):
        for phase in range(4, -1, -1):
            pair = step - phase
            if not 0 <= pair < pairs:
                continue
            for index in range(2 * pair, min(2 * pair + 2, count)):
                if phase == 0:
                    core(index).start()
                elif phase == 1:
                    local(index).wait()
                    core(index).wait_recv()
                    sum_core(index)
                    one(index).start()
                elif phase == 2:
                    one(index).wait_recv()
                    sum_one(index)
                    two(index).start()
                elif phase == 3:
                    two(index).wait_recv()
                    sum_two(index)
                    send_z(index)
                else:
                    landed = got_z[index].at[pl.ds(0, depth - 1)]
                    pltpu.make_async_copy(landed, landed, recv_sem.at[index, 3]).wait()
                    sum_z(index)
        if step == 0:
            lax.fori_loop(1, total, send_gain, 0)
    pltpu.make_async_copy(gains, gains, gain_sem.at[1]).wait()
    gain_out[...] = jnp.sum(gains[...], axis=0)
    for index in range(count):
        core(index).wait_send()
        one(index).wait_send()
        two(index).wait_send()
        gone = got_z[index].at[pl.ds(0, depth - 1)]
        pltpu.make_async_copy(gone, gone, send_sem.at[index, 3]).wait()
    rest = gains.at[pl.ds(0, total - 1)]
    pltpu.make_async_copy(rest, rest, gain_sem.at[0]).wait()


def scatter_all(depth, d_qkv, d_squares, d_kv, d_gains, collective):
    items = [
        (0, 0, 3, 0), (0, 3, 6, 1),
        (2, 0, 1, 0), (2, 1, 2, 1),
        (1, 0, 1, 0), (1, 1, 2, 1),
        (1, 2, 3, 0),
    ]
    count = len(items)
    parts = (d_qkv, d_squares, d_kv)
    own, core, one, two, along = [], [], [], [], []
    for buffer, first, last, kind in items:
        rows, width = parts[buffer].shape[-2:]
        blocks = last - first
        own.append(pltpu.VMEM((blocks, depth, 2, 2, rows, width), jnp.bfloat16))
        core.append(pltpu.VMEM((blocks, depth, 2, 2, rows, width), jnp.bfloat16))
        one.append(pltpu.VMEM((blocks, depth, 2, rows, width), jnp.bfloat16))
        two.append(pltpu.VMEM((blocks, depth, rows, width), jnp.bfloat16))
        along.append(pltpu.VMEM((depth, blocks, rows, width), jnp.bfloat16))
    outs = [jax.ShapeDtypeStruct((p.shape[0],) + p.shape[-2:], jnp.float32) for p in parts]
    outs.append(jax.ShapeDtypeStruct(d_gains.shape[1:], jnp.float32))
    vmem = pl.BlockSpec(memory_space=pltpu.VMEM)
    return pl.pallas_call(
        functools.partial(scatter_kernel, depth, items),
        out_shape=outs,
        in_specs=[ANY] * 4,
        out_specs=[vmem] * 4,
        scratch_shapes=own + core + one + two + along + [
            pltpu.VMEM(d_gains.shape, jnp.float32),
            pltpu.SemaphoreType.DMA((count,)),
            pltpu.SemaphoreType.DMA((count, 4)),
            pltpu.SemaphoreType.DMA((count, 4)),
            pltpu.SemaphoreType.DMA((2,)),
        ],
        compiler_params=pltpu.CompilerParams(
            collective_id=collective, has_side_effects=True, vmem_limit_bytes=60 * 2**20
        ),
    )(d_qkv, d_squares, d_kv, d_gains)


HEADS = 12
HEAD_DIM = 64
SPAN = 64
NEIGHBOURS = 2
NEIGH_LEN = 128
MICRO = 2
UNITS = MICRO * HEADS
AXES = ("blk", "head")
TILE = 256
LEAD = SPAN - 1
SCORE_SCALE = 1.0 / math.sqrt(HEAD_DIM)
LOG2E = math.log2(math.e)


def tile_at(ref, index, row):
    return ref[row, :, pl.ds(pl.multiple_of(index * TILE, TILE), TILE)]


def row_at(ref, index):
    return ref[:, pl.ds(pl.multiple_of(index * TILE, TILE), TILE)]


def tile_mask(key_tile, query_tile, first_row):
    key_place = key_tile * TILE + lax.broadcasted_iota(jnp.int32, (TILE, TILE), 0)
    query_place = query_tile * TILE + lax.broadcasted_iota(jnp.int32, (TILE, TILE), 1)
    return (key_place <= query_place) & (key_place >= first_row)


def attn_forward_kernel(low_ref, first_ref, qkv_ref, shifted_ref, mixed_ref, total_ref):
    tiles = qkv_ref.shape[-1] // TILE

    def one_query(query_tile, carry):
        query_t = tile_at(qkv_ref, query_tile, 0)
        first_row = row_at(first_ref, query_tile)

        def one_key(step, state):
            peak, weight, mixed = state
            key_tile = query_tile - step
            keys = tile_at(qkv_ref, key_tile, 1).T
            scores = jnp.dot(keys, query_t, preferred_element_type=jnp.float32) * (SCORE_SCALE * LOG2E)
            scores = jnp.where(tile_mask(key_tile, query_tile, first_row), scores, -1e30)
            new_peak = jnp.maximum(peak, jnp.max(scores, axis=0, keepdims=True))
            probs = jnp.exp2(scores - new_peak)
            fade = jnp.exp2(peak - new_peak)
            weight = weight * fade + jnp.sum(probs, axis=0, keepdims=True)
            mixed = mixed * fade + jnp.dot(
                tile_at(qkv_ref, key_tile, 2), probs.astype(jnp.bfloat16), preferred_element_type=jnp.float32
            )
            return new_peak, weight, mixed

        start = (
            jnp.full((1, TILE), -1e30, jnp.float32),
            jnp.zeros((1, TILE), jnp.float32),
            jnp.zeros((HEAD_DIM, TILE), jnp.float32),
        )
        steps = query_tile + 1 - low_ref[query_tile]
        peak, weight, mixed = lax.fori_loop(0, steps, one_key, start)
        columns = pl.ds(pl.multiple_of(query_tile * TILE, TILE), TILE)
        mixed_ref[:, columns] = mixed / weight
        total_ref[:, columns] = peak + jnp.log2(weight)
        return carry

    lax.fori_loop(0, tiles, one_query, 0)
    length = qkv_ref.shape[-1]

    def turn(step, carry):
        rows = pl.ds(pl.multiple_of(step * 16, 16), 16)
        shifted_ref[rows, :] = pltpu.roll(mixed_ref[rows, :], length - LEAD, 1).astype(jnp.bfloat16)
        return carry

    lax.fori_loop(0, HEAD_DIM // 16, turn, 0)


def attn_backward_kernel(
    low_ref, high_ref, first_ref, qkv_ref, shifted_ref, mixed_ref, total_ref, out_ref, grad_ref, dq_ref, delta_ref
):
    length = qkv_ref.shape[-1]
    tiles = length // TILE
    delta_ref[...] = jnp.zeros_like(delta_ref)

    def turn(step, carry):
        rows = pl.ds(pl.multiple_of(step * 16, 16), 16)
        grad = pltpu.roll(shifted_ref[rows, :].astype(jnp.float32), LEAD, 1)
        grad_ref[rows, :] = grad.astype(jnp.bfloat16)
        delta_ref[...] += jnp.sum(grad * mixed_ref[rows, :], axis=0, keepdims=True)
        dq_ref[rows, :] = jnp.zeros((16, length), jnp.float32)
        return carry

    lax.fori_loop(0, HEAD_DIM // 16, turn, 0)

    def one_key(key_tile, carry):
        key_t = tile_at(qkv_ref, key_tile, 1)
        keys = key_t.T
        values = tile_at(qkv_ref, key_tile, 2).T

        def one_query(query_tile, state):
            d_key, d_value = state
            query_t = tile_at(qkv_ref, query_tile, 0)
            grad_t = row_at(grad_ref, query_tile)
            scores = jnp.dot(keys, query_t, preferred_element_type=jnp.float32) * (SCORE_SCALE * LOG2E)
            allowed = tile_mask(key_tile, query_tile, row_at(first_ref, query_tile))
            probs = jnp.where(allowed, jnp.exp2(scores - row_at(total_ref, query_tile)), 0.0)
            d_probs = jnp.dot(values, grad_t, preferred_element_type=jnp.float32)
            d_scores = (probs * (d_probs - row_at(delta_ref, query_tile))).astype(jnp.bfloat16)
            d_value = d_value + jnp.dot(
                probs.astype(jnp.bfloat16), grad_t.T, preferred_element_type=jnp.float32
            )
            d_key = d_key + jnp.dot(d_scores, query_t.T, preferred_element_type=jnp.float32)
            columns = pl.ds(pl.multiple_of(query_tile * TILE, TILE), TILE)
            dq_ref[:, columns] += jnp.dot(key_t, d_scores, preferred_element_type=jnp.float32)
            return d_key, d_value

        zeros = jnp.zeros((TILE, HEAD_DIM), jnp.float32)
        d_key, d_value = lax.fori_loop(key_tile, high_ref[key_tile], one_query, (zeros, zeros))
        columns = pl.ds(pl.multiple_of(key_tile * TILE, TILE), TILE)
        out_ref[1, :, columns] = (d_key * SCORE_SCALE).T.astype(jnp.bfloat16)
        out_ref[2, :, columns] = d_value.T.astype(jnp.bfloat16)
        return carry

    lax.fori_loop(0, tiles, one_key, 0)

    def finish(step, carry):
        rows = pl.ds(pl.multiple_of(step * 16, 16), 16)
        out_ref[0, rows, :] = (dq_ref[rows, :] * SCORE_SCALE).astype(jnp.bfloat16)
        return carry

    lax.fori_loop(0, HEAD_DIM // 16, finish, 0)


SMEM = pl.BlockSpec(memory_space=pltpu.SMEM)
VMEM = pl.BlockSpec(memory_space=pltpu.VMEM)


def local_params():
    return pltpu.CompilerParams(vmem_limit_bytes=60 * 2**20)


def attn_forward(low, first, qkv):
    width, length = qkv.shape[1:]
    return pl.pallas_call(
        attn_forward_kernel,
        out_shape=[
            jax.ShapeDtypeStruct((width, length), jnp.bfloat16),
            jax.ShapeDtypeStruct((width, length), jnp.float32),
            jax.ShapeDtypeStruct((1, length), jnp.float32),
        ],
        in_specs=[SMEM, VMEM, VMEM],
        out_specs=[VMEM] * 3,
        compiler_params=local_params(),
        cost_estimate=pl.CostEstimate(flops=10**9, bytes_accessed=4 * 10**6, transcendentals=4 * 10**6),
    )(low, first, qkv)


def attn_backward(low, high, first, qkv, shifted, mixed, totals):
    width, length = qkv.shape[1:]
    return pl.pallas_call(
        attn_backward_kernel,
        out_shape=jax.ShapeDtypeStruct((3, width, length), jnp.bfloat16),
        in_specs=[SMEM, SMEM] + [VMEM] * 5,
        out_specs=VMEM,
        scratch_shapes=[
            pltpu.VMEM((width, length), jnp.bfloat16),
            pltpu.VMEM((width, length), jnp.float32),
            pltpu.VMEM((1, length), jnp.float32),
        ],
        compiler_params=local_params(),
        cost_estimate=pl.CostEstimate(flops=3 * 10**9, bytes_accessed=4 * 10**6, transcendentals=4 * 10**6),
    )(low, high, first, qkv, shifted, mixed, totals)


def layer_norm(values, norm_gain):
    centred = values - jnp.mean(values, axis=-1, keepdims=True)
    spread = jnp.mean(centred * centred, axis=-1, keepdims=True)
    return centred * lax.rsqrt(spread + 1e-05) * norm_gain


def norm_backward(values, norm_gain, grad_out):
    result, pullback = jax.vjp(layer_norm, values, norm_gain)
    return pullback(grad_out)


def gelu_tanh(values):
    return jax.nn.gelu(values, approximate=True)


def soft_forward(scores):
    maximum = jnp.max(scores, axis=-1, keepdims=True)
    exp_rows = jnp.exp(scores - maximum)
    row_total = jnp.sum(exp_rows, axis=-1, keepdims=True)
    return (exp_rows / row_total, maximum + jnp.log(row_total))


def soft_backward(scores, log_total, grad_probs):
    attn_probs = jnp.exp(scores - log_total)
    row_delta = jnp.sum(attn_probs * grad_probs, axis=-1, keepdims=True)
    return (attn_probs, (attn_probs * (grad_probs - row_delta)).astype(jnp.bfloat16))


def split_cross(query_groups, pair_groups):
    group_count, span_rows, model_width = query_groups.shape
    pair_rows = pair_groups.shape[1]
    query_rows = query_groups.reshape(group_count, span_rows, HEADS, HEAD_DIM)
    key_rows = pair_groups[..., :model_width].reshape(group_count, pair_rows, HEADS, HEAD_DIM)
    value_rows = pair_groups[..., model_width:].reshape(group_count, pair_rows, HEADS, HEAD_DIM)
    return (query_rows, key_rows, value_rows)


def cross_forward(query_groups, pair_groups, score_scale):
    group_count, span_rows, model_width = query_groups.shape
    query_rows, key_rows, value_rows = split_cross(query_groups, pair_groups)
    scores = (
        jnp.einsum("cqhd,ckhd->chqk", query_rows, key_rows, preferred_element_type=jnp.float32)
        * score_scale
    )
    attn_probs, log_total = soft_forward(scores)
    mixed_rows = jnp.einsum(
        "chqk,ckhd->cqhd",
        attn_probs.astype(jnp.bfloat16),
        value_rows,
        preferred_element_type=jnp.float32,
    )
    return (mixed_rows.reshape(group_count, span_rows, model_width), log_total)


def cross_backward(query_groups, pair_groups, log_total, grad_groups, score_scale):
    group_count, span_rows, model_width = query_groups.shape
    pair_rows = pair_groups.shape[1]
    query_rows, key_rows, value_rows = split_cross(query_groups, pair_groups)
    grad_rows = grad_groups.reshape(group_count, span_rows, HEADS, HEAD_DIM)
    scores = (
        jnp.einsum("cqhd,ckhd->chqk", query_rows, key_rows, preferred_element_type=jnp.float32)
        * score_scale
    )
    grad_probs = jnp.einsum(
        "cqhd,ckhd->chqk", grad_rows, value_rows, preferred_element_type=jnp.float32
    )
    attn_probs, grad_scores = soft_backward(scores, log_total, grad_probs)
    grad_query = (
        jnp.einsum("chqk,ckhd->cqhd", grad_scores, key_rows, preferred_element_type=jnp.float32)
        * score_scale
    )
    grad_key = (
        jnp.einsum("chqk,cqhd->ckhd", grad_scores, query_rows, preferred_element_type=jnp.float32)
        * score_scale
    )
    grad_value = jnp.einsum(
        "chqk,cqhd->ckhd",
        attn_probs.astype(jnp.bfloat16),
        grad_rows,
        preferred_element_type=jnp.float32,
    )
    grad_pairs = jnp.concatenate(
        [
            grad_key.reshape(group_count, pair_rows, model_width),
            grad_value.reshape(group_count, pair_rows, model_width),
        ],
        axis=-1,
    )
    return (grad_query.reshape(group_count, span_rows, model_width), grad_pairs)


def dot32(left, right):
    return jnp.dot(left, right, preferred_element_type=jnp.float32)


def outer(left, right):
    return jnp.einsum("td,te->de", left, right, preferred_element_type=jnp.float32)


def turn_heads(values, cosine, sine):
    first_half, second_half = values[:, :32], values[:, 32:]
    return jnp.concatenate(
        [first_half * cosine - second_half * sine, second_half * cosine + first_half * sine], axis=1
    )


def on_device(
    hidden_in,
    segment_ids,
    neighbour_valid,
    neighbours,
    out_grad,
    norm_attn,
    w_qkv,
    w_attn_out,
    norm_cross,
    w_cross_q,
    w_cross_kv,
    w_cross_out,
    norm_mlp,
    w_up,
    w_down,
):
    micro, tok_count, model_width = hidden_in.shape
    blk_count = lax.axis_size("blk")
    depth = blk_count // 4
    total = blk_count * 2
    length = tok_count * total
    row_count = micro * tok_count
    gain_rows = norm_attn.shape[0]
    span_count = tok_count // SPAN
    pair_rows = NEIGHBOURS * NEIGH_LEN
    device = lax.axis_index(AXES)

    up_full = lax.all_gather(w_up, AXES, axis=0, tiled=True)
    down_full = lax.all_gather(w_down, AXES, axis=0, tiled=True)

    small = jnp.zeros((16, 128), jnp.bfloat16)
    for row, gain in enumerate((norm_attn, norm_cross, norm_mlp)):
        small = small.at[row, :gain_rows].set(gain)
    small = small.at[3 : 3 + micro, :tok_count].set(segment_ids.astype(jnp.bfloat16))
    got_qkv, got_sq, got_kv, got_small, lead_hid, lead_grad = gather_all(
        depth, w_qkv, w_attn_out, w_cross_q, w_cross_out, w_cross_kv, small, hidden_in, out_grad
    )
    gains = got_small[:, :3, :gain_rows].astype(jnp.float32).transpose(1, 0, 2).reshape(3, model_width)
    gain_attn, gain_cross, gain_mlp = gains[0], gains[1], gains[2]
    seg_full = got_small[:, 3 : 3 + micro, :tok_count].transpose(1, 0, 2).reshape(micro, length)
    seg_full = seg_full.astype(jnp.int32)
    qkv_blocks = got_qkv.reshape(6, model_width, model_width // 2)
    squares = got_sq.reshape(3, model_width, model_width)
    attn_out_full, cross_q_full, cross_out_full = squares[0], squares[1], squares[2]
    kv_blocks = got_kv.reshape(2, model_width, model_width)

    token_index = device * tok_count + jnp.arange(tok_count, dtype=jnp.int32)
    first_of = jnp.sum(
        (seg_full[:, None, :] < segment_ids[:, :, None]).astype(jnp.int32), axis=-1
    )
    local_pos = token_index[None] - first_of
    frequency = jnp.exp(
        jnp.arange(HEAD_DIM // 2, dtype=jnp.float32) * (-2.0 * math.log(10000.0) / HEAD_DIM)
    )
    angles = frequency[:, None, None] * local_pos.astype(jnp.float32)[None]
    cosine, sine = jnp.cos(angles), jnp.sin(angles)

    unit, holder = unit_of(device, total)
    seg_unit = lax.dynamic_index_in_dim(seg_full, unit // HEADS, 0, keepdims=False)
    seg_tiles = seg_unit.reshape(length // TILE, TILE)
    tile_first = jnp.sum((seg_unit[None] < seg_tiles[:, :1]).astype(jnp.int32), axis=-1)
    inside = jnp.sum((seg_tiles[:, None, :] < seg_tiles[:, :, None]).astype(jnp.int32), axis=-1)
    tile_index = jnp.arange(length // TILE, dtype=jnp.int32)
    first_row = jnp.where(
        seg_tiles == seg_tiles[:, :1], tile_first[:, None], tile_index[:, None] * TILE + inside
    ).reshape(1, length)
    low = tile_first // TILE
    high = jnp.sum((low[None] <= tile_index[:, None]).astype(jnp.int32), axis=-1)
    low = jnp.where(holder, low, tile_index + 1)
    high = jnp.where(holder, high, 0)

    hidden = hidden_in.astype(jnp.float32)
    normed_attn = layer_norm(hidden, gain_attn).astype(jnp.bfloat16).reshape(row_count, model_width)
    raw = jnp.einsum("bde,td->bet", qkv_blocks, normed_attn, preferred_element_type=jnp.float32)
    raw = raw.reshape(3, HEADS, HEAD_DIM, micro, tok_count)
    rotated = jnp.stack(
        [turn_heads(raw[0], cosine, sine), turn_heads(raw[1], cosine, sine), raw[2]]
    ).astype(jnp.bfloat16)
    message = rotated.transpose(3, 1, 0, 2, 4).reshape(UNITS, 3, HEAD_DIM, tok_count)
    unit_qkv = to_units(total, message, 1)
    shifted, mixed, totals = attn_forward(low, first_row, unit_qkv)
    (attended_t,) = to_tokens(total, shifted[None], (), 2)
    attended_t = attended_t.reshape(micro, model_width, tok_count)

    def shift(rows, lead):
        return jnp.concatenate([rows[:, LEAD:], lead[:, :LEAD]], axis=1).reshape(row_count, model_width)

    hidden_s = shift(hidden_in, lead_hid).astype(jnp.float32)
    grad_low = shift(out_grad, lead_grad)
    cotangent = grad_low.astype(jnp.float32)
    after_attn = hidden_s + jnp.einsum(
        "mdt,de->mte", attended_t, attn_out_full, preferred_element_type=jnp.float32
    ).reshape(row_count, model_width)
    normed_cross = layer_norm(after_attn, gain_cross).astype(jnp.bfloat16)
    cross_query = dot32(normed_cross, cross_q_full).astype(jnp.bfloat16)
    neigh_rows = neighbours.reshape(micro * span_count * pair_rows, model_width)
    groups = micro * span_count
    pairs_local = jnp.concatenate(
        [dot32(neigh_rows, kv_blocks[0]).astype(jnp.bfloat16), dot32(neigh_rows, kv_blocks[1]).astype(jnp.bfloat16)],
        axis=1,
    ).reshape(groups, pair_rows, 2 * model_width)
    shifted_index = token_index + LEAD
    used = jnp.where(
        shifted_index[None] < length, jnp.repeat(neighbour_valid, SPAN, axis=1).astype(jnp.float32), 0.0
    ).reshape(row_count, 1)
    query_groups = cross_query.reshape(groups, SPAN, model_width)
    cross_rows, cross_total = cross_forward(query_groups, pairs_local, SCORE_SCALE)
    cross_mixed = (cross_rows.reshape(row_count, model_width) * used).astype(jnp.bfloat16)
    after_cross = after_attn + dot32(cross_mixed, cross_out_full)
    normed_mlp = layer_norm(after_cross, gain_mlp).astype(jnp.bfloat16)
    mlp_upper = dot32(normed_mlp, up_full)
    activated, gelu_pull = jax.vjp(gelu_tanh, mlp_upper)
    activated = activated.astype(jnp.bfloat16)
    result_rows = (after_cross + dot32(activated, down_full)).astype(jnp.bfloat16)
    result_rows = result_rows.reshape(micro, tok_count, model_width)
    d_activated = dot32(grad_low, down_full.T)
    d_upper = gelu_pull(d_activated)[0].astype(jnp.bfloat16)
    d_normed_mlp = dot32(d_upper, up_full.T)

    up_share = lax.psum_scatter(
        outer(normed_mlp, d_upper).astype(jnp.bfloat16), AXES, scatter_dimension=0, tiled=True
    ).astype(jnp.float32)
    down_share = lax.psum_scatter(
        outer(activated, grad_low).astype(jnp.bfloat16), AXES, scatter_dimension=0, tiled=True
    ).astype(jnp.float32)

    d_second_in, d_gain_mlp = norm_backward(after_cross, gain_mlp, d_normed_mlp)
    d_second = cotangent + d_second_in
    d_second_low = d_second.astype(jnp.bfloat16)
    d_mixed = dot32(d_second_low, cross_out_full.T).astype(jnp.bfloat16)
    d_groups = (d_mixed.astype(jnp.float32) * used).astype(jnp.bfloat16).reshape(groups, SPAN, model_width)
    grad_query_groups, d_pairs = cross_backward(
        query_groups, pairs_local, cross_total, d_groups, SCORE_SCALE
    )
    d_cross_query = grad_query_groups.reshape(row_count, model_width).astype(jnp.bfloat16)
    d_normed_cross = dot32(d_cross_query, cross_q_full.T)
    d_first_in, d_gain_cross = norm_backward(after_attn, gain_cross, d_normed_cross)
    d_first = d_second + d_first_in
    d_first_low = d_first.astype(jnp.bfloat16).reshape(micro, tok_count, model_width)
    d_attended_t = jnp.einsum(
        "de,mte->mdt", attn_out_full, d_first_low, preferred_element_type=jnp.float32
    ).astype(jnp.bfloat16)
    unit_grad = to_units(total, d_attended_t.reshape(UNITS, 1, HEAD_DIM, tok_count), 3)
    unit_back = attn_backward(low, high, first_row, unit_qkv, unit_grad[0], mixed, totals)
    d_first = d_first.reshape(micro, tok_count, model_width)
    sent_t, tail_first, tail_result = to_tokens(
        total, unit_back, (d_first[:, tok_count - 64 :], result_rows[:, tok_count - 64 :]), 4
    )

    def unshift(rows, tail):
        return jnp.concatenate([tail[:, 1:], rows[:, : tok_count - LEAD]], axis=1)

    output = unshift(result_rows, tail_result)
    d_first_home = unshift(d_first, tail_first)
    sent_t = sent_t.reshape(micro, HEADS, 3, HEAD_DIM, tok_count).transpose(2, 1, 3, 0, 4)
    sent_t = sent_t.astype(jnp.float32)
    raw_t = jnp.stack(
        [turn_heads(sent_t[0], cosine, -sine), turn_heads(sent_t[1], cosine, -sine), sent_t[2]]
    ).astype(jnp.bfloat16).reshape(6, model_width // 2, row_count)
    d_normed_attn = jnp.einsum("bet,bde->td", raw_t, qkv_blocks, preferred_element_type=jnp.float32)
    d_hidden_in, d_gain_attn = norm_backward(
        hidden, gain_attn, d_normed_attn.reshape(micro, tok_count, model_width)
    )
    grad_in = (d_first_home + d_hidden_in).astype(jnp.bfloat16)

    d_pairs_low = d_pairs.astype(jnp.bfloat16).reshape(groups * pair_rows, 2 * model_width)
    d_keys, d_values = d_pairs_low[:, :model_width], d_pairs_low[:, model_width:]
    d_neigh = (
        jnp.einsum("te,de->td", d_keys, kv_blocks[0], preferred_element_type=jnp.float32)
        + jnp.einsum("te,de->td", d_values, kv_blocks[1], preferred_element_type=jnp.float32)
    ).astype(jnp.bfloat16)
    grad_neighbours = d_neigh.reshape(neighbours.shape)

    def blocks_of(array):
        return array.astype(jnp.bfloat16).reshape(
            array.shape[0], depth, 2, 2, 2, gain_rows, array.shape[-1]
        )

    d_qkv = jnp.einsum("td,bet->bde", normed_attn, raw_t, preferred_element_type=jnp.float32)
    d_sq = jnp.stack(
        [
            jnp.einsum("mdt,mte->de", attended_t, d_first_low, preferred_element_type=jnp.float32),
            outer(normed_cross, d_cross_query),
            outer(cross_mixed, d_second_low),
        ]
    )
    d_kv = jnp.stack([outer(neigh_rows, d_keys), outer(neigh_rows, d_values)])
    d_gains = jnp.stack([d_gain_attn, d_gain_cross, d_gain_mlp]).reshape(3, total, gain_rows)
    d_gains = jnp.zeros((total, 8, 128), jnp.float32).at[:, :3, :gain_rows].set(d_gains.transpose(1, 0, 2))
    s_qkv, s_sq, s_kv, s_gain = scatter_all(
        depth, blocks_of(d_qkv), blocks_of(d_sq), blocks_of(d_kv), d_gains, 5
    )
    return (
        output,
        grad_in,
        grad_neighbours,
        s_gain[0, :gain_rows],
        s_qkv.transpose(1, 0, 2).reshape(gain_rows, 3 * model_width),
        s_sq[0],
        s_gain[1, :gain_rows],
        s_sq[1],
        s_kv.transpose(1, 0, 2).reshape(gain_rows, 2 * model_width),
        s_sq[2],
        s_gain[2, :gain_rows],
        up_share,
        down_share,
    )


def solution(mesh):
    placed = (
        P(None, ("blk", "head"), None),
        P(None, ("blk", "head")),
        P(None, ("blk", "head")),
        P(None, ("blk", "head"), None, None, None),
        P(None, ("blk", "head"), None),
        P(("blk", "head")),
        P(("blk", "head"), None),
        P(("blk", "head"), None),
        P(("blk", "head")),
        P(("blk", "head"), None),
        P(("blk", "head"), None),
        P(("blk", "head"), None),
        P(("blk", "head")),
        P(("blk", "head"), None),
        P(("blk", "head"), None),
    )
    return jax.shard_map(
        on_device,
        mesh=mesh,
        in_specs=placed,
        out_specs=(
            P(None, ("blk", "head"), None),
            P(None, ("blk", "head"), None),
            P(None, ("blk", "head"), None, None, None),
            P(("blk", "head")),
            P(("blk", "head"), None),
            P(("blk", "head"), None),
            P(("blk", "head")),
            P(("blk", "head"), None),
            P(("blk", "head"), None),
            P(("blk", "head"), None),
            P(("blk", "head")),
            P(("blk", "head"), None),
            P(("blk", "head"), None),
        ),
        check_vma=False,
    )
```

time: 1330 us -> 585 us (0.44)
  blocking collectives: 396 us -> 0 us
  Pallas kernels: 0 us -> 342 us
  starting transfers between devices: 273 us -> 0.16 us
  waiting for transfers between devices: 223 us -> 1.42 us
  matrix products: 168 us -> 74.7 us
  other arithmetic: 99.9 us -> 37.8 us
  local copies, waits for them, and re-layouts: 139 us -> 103 us
    pallas_call x0 -> x8, Pallas kernels: none -> 342 us  [the longest x1 82.2 us: gather_all(): pl.pallas_call(functools.partial(gather_kernel, depth, items), out_shape=...]
    ppermute x40 -> x0, starting transfers between devices: 212 us -> none  [from_behind(): lax.ppermute(value, axis, [(source, source + steps) for source in range(f...]
    all_to_all x3 -> x0, blocking collectives: 156 us -> none  [the longest x1 56.4 us: on_device(): lax.all_to_all(halves[8].astype(jnp.bfloat16), 'head', split_axis=1, conc...]
    all_gather x2 -> x0, blocking collectives: 136 us -> none  [the longest x1 70.2 us: on_device(): lax.all_gather(segment_ids, ('blk', 'head'), axis=1, tiled=True)]
    ppermute x40 -> x0, waiting for transfers between devices: 132 us -> none  [from_behind(): lax.ppermute(value, axis, [(source, source + steps) for source in range(f...]
    unnamed x2 -> x0, blocking collectives: 104 us -> none
    dot_general x47 -> x24, matrix products: 156 us -> 63.2 us  [the longest x10 33.6 us: dot32(): return jnp.dot(left, right, preferred_element_type=jnp.float32)]
    all_to_all x15 -> x0, starting transfers between devices: 60.4 us -> none  [the longest x4 16.9 us: to_heads(): lax.all_to_all(packed, 'head', split_axis=2, concat_axis=0, tiled=True)]
  transfers between devices with their start and end apart: 69 -> 4, of which waited for: 22 -> 0; matrix products, arithmetic and copies ran while one was open for 26% -> 33% of each run, Pallas kernels for 0% -> 59%
where the time goes in v1:
time: 585 us; the launch traced here: 574 us
  Pallas kernels  342 us (58%)
  local copies, waits for them, and re-layouts  103 us (18%)
  matrix products  74.7 us (13%)
  other arithmetic  37.8 us (6%)
  between operations  15.6 us (3%)
    pallas_call x1, Pallas kernels, gather_all(): pl.pallas_call(functools.partial(gather_kernel, depth, items), out_shape=...  82.2 us
    pallas_call x1, Pallas kernels, scatter_all(): pl.pallas_call(functools.partial(scatter_kernel, depth, items), out_shape...  72.7 us
    pallas_call x2, Pallas kernels, to_units(): pl.pallas_call(functools.partial(to_units_kernel, total), out_shape=jax.S...  65.6 us
    pallas_call x2, Pallas kernels, to_tokens(): pl.pallas_call(functools.partial(to_tokens_kernel, total, count), out_sha...  62.3 us
    dot_general x10, matrix products, dot32(): return jnp.dot(left, right, preferred_element_type=jnp.float32)  33.6 us
    pallas_call x1, Pallas kernels, attn_backward(): pl.pallas_call(attn_backward_kernel, out_shape=jax.ShapeDtypeStruct((3, w...  29.5 us
    pallas_call x1, Pallas kernels, attn_forward(): pl.pallas_call(attn_forward_kernel, out_shape=[jax.ShapeDtypeStruct((widt...  29.3 us
    unnamed x193, local copies, waits for them, and re-layouts  15.2 us
  transfers between devices with their start and end apart: 4, of which 0 were waited for; matrix products, arithmetic and copies ran while one was open for 33% of the time, Pallas kernels for 59%

profile of v1, /device:TPU:0, one launch (start us, length us, event | category | flops | bytes accessed | tf_op | source)
XLA Modules:
  0.0 574.5 jit_solution(1859556601769752178)
XLA Ops:
  18.0 82.2 %shard_map.246 = (bf16[6,4,2,2,2,24,384]{6,5,4,3,2,1,0:T(8,128)(2,1)}, bf16[3,4,2,2,2,24,768]{6,5,4,3,2,1,0:T(8,128)(2,1)}, bf16[2,4,2,2,2,24,768]{6,5,4,3,2,1,0...) custom-call(bf16[24,2304]{1,0:T(8,128)(2,1)} %refs_0_.1, ...), custom_call_target="tpu_custom_call" | custom-call | tf_op jit(solution)/shard_map/pallas_call | solution.py:192
  107.1 3.3 fusion.66
  128.2 45.2 %shard_map.247.qkv_ref = bf16[3,64,4096]{2,1,0:T(8,128)(2,1)} custom-call(bf16[24,3,64,128]{3,2,1,0:T(8,128)(2,1)} %bitcast.254), custom_call_target="tpu_custom_call" | custom-call | tf_op jit(solution)/shard_map/pallas_call | solution.py:258
  174.6 29.3 %shard_map.248 = (bf16[64,4096]{1,0:T(8,128)(2,1)}, f32[64,4096]{1,0:T(8,128)}, f32[1,4096]{1,0:T(1,128)}) custom-call(s32[16]{0:T(128)} %get-tuple-element.120.low_ref, s32[1,4096]{1,0:T(1,128)} %compare_select_fusion.first_ref, bf16[3,64,4096]{2,1,0:T(8,128)(2,1)} %shard_map.247.qkv_ref), custom_call_target="tpu_custom_call" | custom-call | flops 1000000000 | bytes 4000000 | tf_op jit(solution)/shard_map/pallas_call | solution.py:668
  203.9 21.2 %shard_map.249 = bf16[24,1,64,128]{3,2,1,0:T(8,128)(2,1)} custom-call(bf16[1,64,4096]{2,1,0:T(8,128)(2,1)} %bitcast.283), custom_call_target="tpu_custom_call" | custom-call | tf_op jit(solution)/shard_map/pallas_call | solution.py:320
  226.4 4.5 fusion.58
  237.0 3.0 fusion.15
  243.5 6.2 %reshape.561 = bf16[4,256,1536]{1,0,2:T(4,128)(2,1)} reshape(bf16[1024,1536]{0,1:T(8,128)(2,1)} %pad_maximum_fusion.1) | data formatting | bytes 6291456 | tf_op jit(solution)/shard_map/reshape | solution.py:906
  249.7 3.0 fusion.59
  260.1 3.0 copy.179
  276.4 5.5 fusion.67
  281.9 8.0 %fusion.6 = (bf16[256,3072]{1,0:T(8,128)(2,1)S(1)}, f32[256,3072]{1,0:T(8,128)}) fusion(f32[256,3072]{1,0:T(8,128)} %fusion.67, bf16[768,3072]{1,0:T(8,128)(2,1)} %all-gather.5.cloned.1.call-done, f32[256,768]{1,0:T(8,128)S(1)} %get-tuple-element.168, f32[768]{0:T(1024)S(1)} %mul.463, f32[256]{0:T(256)} %fusion.49, f32[256]{0:T(256)} %copy-done.64), kind=kOutput, calls=%fused_computation.14 | convolution fusion | flops 1224474624 | bytes 13374464 | tf_op jit(solution)/shard_map/dot_general | solution.py:791
  291.0 3.8 convolution_convert_fusion.1
  294.9 5.3 fusion.23
  301.7 4.5 multiply_reduce_fusion.2
  312.4 4.2 multiply_reduce_fusion
  341.4 20.5 %shard_map.250 = bf16[1,64,4096]{2,1,0:T(8,128)(2,1)} custom-call(bf16[24,1,64,128]{3,2,1,0:T(8,128)(2,1)} %bitcast.271), custom_call_target="tpu_custom_call" | custom-call | tf_op jit(solution)/shard_map/pallas_call | solution.py:258
  361.9 6.3 %convolution_convert_fusion = bf16[3072,768]{1,0:T(8,128)(2,1)} fusion(bf16[256,768]{1,0:T(8,128)(2,1)S(1)} %bitcast.246, f32[256,3072]{1,0:T(8,128)} %get-tuple-element.170), kind=kOutput, calls=%fused_computation | convolution fusion | flops 1217396736 | bytes 8257536 | tf_op jit(solution)/shard_map/td,te->de/dot_general | solution.py:795
  368.2 29.5 %shard_map.251.refs_0_ = bf16[3,64,4096]{2,1,0:T(8,128)(2,1)} custom-call(s32[16]{0:T(128)} %get-tuple-element.120.low_ref, s32[16]{0:T(128)} %broadcast_select_fusion.1.high_ref, s32[1,4096]{1,0:T(1,128)} %compare_select_fusion.first_ref, bf16[3,64,4096]{2,1,0:T(8,128)(2,1)} %shard_map.247.qkv_ref, bf16[64,4096]{1,0:T(8,128)(2,1)} %bitcast.282, ...), custom_call_target="tpu_custom_call" | custom-call | flops 3000000000 | bytes 4000000 | tf_op jit(solution)/shard_map/pallas_call | solution.py:684
  397.6 41.1 %shard_map.252 = (bf16[24,3,64,128]{3,2,1,0:T(8,128)(2,1)}, f32[2,64,768]{2,1,0:T(8,128)}, bf16[2,64,768]{2,1,0:T(8,128)(2,1)}) custom-call(bf16[3,64,4096]{2,1,0:T(8,128)(2,1)} %shard_map.251.refs_0_, f32[2,64,768]{2,1,0:T(8,128)} %slice.303.refs_1_, bf16[2,64,768]{2,1,0:T(8,128)(2,1)} %slice.304.refs_2_), custom_call_target="tpu_custom_call" | custom-call | tf_op jit(solution)/shard_map/pallas_call | solution.py:320
  448.5 3.2 convert_element_type.244
  453.1 3.7 fusion.38
  462.5 6.1 %copy.155 = bf16[6,768,384]{2,1,0:T(8,128)(2,1)} copy(bf16[6,768,384]{1,2,0:T(8,128)(2,1)} %convert_bitcast_fusion) | data formatting | bytes 7077888 | tf_op jit(solution)/shard_map/convert_element_type | solution.py:980
  477.0 72.7 %shard_map.253 = (f32[6,24,384]{2,1,0:T(8,128)}, f32[3,24,768]{2,1,0:T(8,128)}, f32[2,24,768]{2,1,0:T(8,128)}, f32[8,128]{1,0:T(8,128)}) custom-call(bf16[6,4,2,2,2,24,384]{6,5,4,3,2,1,0:T(8,128)(2,1)} %bitcast.237, bf16[3,4,2,2,2,24,768]{6,5,4,3,2,1,0:T(8,128)(2,1)} %pad_maximum_fusion.refs_1_, ...), custom_call_target="tpu_custom_call" | custom-call | tf_op jit(solution)/shard_map/pallas_call | solution.py:511
  (354 shorter events, 143.7 us)
Async XLA Ops:
  7.2 229.8 %copy-start = (bf16[2,2,2,128,768]{4,3,2,1,0:T(8,128)(2,1)S(1)}, bf16[2,2,2,128,768]{4,3,2,1,0:T(8,128)(2,1)}, u32[]{:S(2)}) copy-start(bf16[2,2,2,128,768]{4,3,2,1,0:T(8,128)(2,1)} %param.28) | copy-start | bytes 4718596
  7.2 98.6 %copy-start.3 = (bf16[2,128,768]{2,1,0:T(8,128)(2,1)S(1)}, bf16[2,128,768]{2,1,0:T(8,128)(2,1)}, u32[]{:S(2)}) copy-start(bf16[2,128,768]{2,1,0:T(8,128)(2,1)} %refs_6_.1) | copy-start | bytes 1179652
  7.2 94.8 %copy-start.89 = (s32[2,128]{1,0:T(2,128)S(1)}, s32[2,128]{1,0:T(2,128)}, u32[]{:S(2)}) copy-start(s32[2,128]{1,0:T(2,128)} %param.26) | copy-start | bytes 3076
  7.2 269.1 %all-gather.3.cloned.1.call-start = ((), (), s32[]{:S(2)}) async-start(), calls=%async_computation.2 | async-start | bytes 4866048 | tf_op jit(solution)/shard_map/all_gather | solution.py:834
  8.0 273.9 %all-gather.5.cloned.1.call-start = ((), (), s32[]{:S(2)}) async-start(), calls=%async_computation.3 | async-start | bytes 4866048 | tf_op jit(solution)/shard_map/all_gather | solution.py:833
  8.7 555.5 %reduce-scatter.3.cloned.1.call-start = ((), (), s32[]{:S(2)}) async-start(), calls=%async_computation.4 | async-start | bytes 4866048 | tf_op jit(solution)/shard_map/reduce_scatter | solution.py:925
  104.4 10.7 %copy-start.51 = (s32[1,4096]{1,0:T(1,128)}, s32[1,4096]{1,0:T(1,128)S(1)}, u32[]{:S(2)}) copy-start(s32[1,4096]{1,0:T(1,128)S(1)} %get-tuple-element.123) | copy-start | bytes 49156
  127.1 46.9 %copy-start.52 = (s32[1,4096]{1,0:T(1,128)S(1)}, s32[1,4096]{1,0:T(1,128)}, u32[]{:S(2)}) copy-start(s32[1,4096]{1,0:T(1,128)} %copy-done.51) | copy-start | bytes 49156
  127.1 46.9 %copy-start.59 = (s32[1,1,16,256]{3,1,2,0:T(1,128)S(1)}, s32[1,1,16,256]{3,1,2,0:T(1,128)}, u32[]{:S(2)}) copy-start(s32[1,1,16,256]{3,1,2,0:T(1,128)} %copy.195) | copy-start | bytes 49156
  127.1 46.9 %copy-start.60 = (s32[1,1,16,256]{3,1,2,0:T(1,128)S(1)}, s32[1,1,16,256]{3,1,2,0:T(1,128)}, u32[]{:S(2)}) copy-start(s32[1,1,16,256]{3,1,2,0:T(1,128)} %copy.194) | copy-start | bytes 49156
  127.1 46.8 %copy-start.61 = (s32[1,1,16,256]{3,1,2,0:T(1,128)S(1)}, s32[1,1,16,256]{3,1,2,0:T(1,128)}, u32[]{:S(2)}) copy-start(s32[1,1,16,256]{3,1,2,0:T(1,128)} %copy.193) | copy-start | bytes 49156
  174.6 51.7 %copy-start.43 = (bf16[2,65,768]{2,1,0:T(8,128)(2,1)S(1)}, bf16[2,65,768]{2,1,0:T(8,128)(2,1)}, u32[]{:S(2)}) copy-start(bf16[2,65,768]{2,1,0:T(8,128)(2,1)} %slice.260) | copy-start | bytes 599044
  174.6 51.7 %copy-start.50 = (bf16[2,64,768]{2,1,0:T(8,128)(2,1)S(1)}, bf16[2,64,768]{2,1,0:T(8,128)(2,1)}, u32[]{:S(2)}) copy-start(bf16[2,64,768]{2,1,0:T(8,128)(2,1)} %get-tuple-element.92) | copy-start | bytes 589828
  237.0 16.6 %copy-start.13 = (bf16[4,64,12,64]{1,3,2,0:T(8,128)(2,1)}, bf16[4,64,12,64]{1,3,2,0:T(8,128)(2,1)S(1)}, u32[]{:S(2)}) copy-start(bf16[4,64,12,64]{1,3,2,0:T(8,128)(2,1)S(1)} %copy.151) | copy-start | bytes 1179652
  281.9 9.2 %copy-start.73 = (f32[256]{0:T(256)S(1)}, f32[256]{0:T(256)}, u32[]{:S(2)}) copy-start(f32[256]{0:T(256)} %fusion.49) | copy-start | bytes 3076
  294.8 271.0 %reduce-scatter.5.cloned.1.call-start = ((), (), s32[]{:S(2)}) async-start(), calls=%async_computation.5 | async-start | bytes 4866048 | tf_op jit(solution)/shard_map/reduce_scatter | solution.py:928
  339.3 22.6 %copy-start.17 = (bf16[2,128,768]{2,1,0:T(8,128)(2,1)S(1)}, bf16[2,128,768]{2,1,0:T(8,128)(2,1)}, u32[]{:S(2)}) copy-start(bf16[2,128,768]{2,1,0:T(8,128)(2,1)} %pad_maximum_fusion.3) | copy-start | bytes 1179652
  397.6 44.6 %copy-start.33 = (bf16[768,256]{0,1:T(8,128)(2,1)S(1)}, bf16[768,256]{0,1:T(8,128)(2,1)}, u32[]{:S(2)}) copy-start(bf16[768,256]{0,1:T(8,128)(2,1)} %get-tuple-element.143) | copy-start | bytes 1179652
  397.6 45.5 %copy-start.23 = (bf16[24,1,64,128]{3,2,1,0:T(8,128)(2,1)S(1)}, bf16[24,1,64,128]{3,2,1,0:T(8,128)(2,1)}, u32[]{:S(2)}) copy-start(bf16[24,1,64,128]{3,2,1,0:T(8,128)(2,1)} %shard_map.249) | copy-start | bytes 1179652
  477.0 78.0 %copy-start.85 = (f32[2,128]{1,0:T(2,128)S(1)}, f32[2,128]{1,0:T(2,128)}, u32[]{:S(2)}) copy-start(f32[2,128]{1,0:T(2,128)} %get-tuple-element.110) | copy-start | bytes 3076
  477.0 80.9 %copy-start.27 = (f32[2,65,768]{2,1,0:T(8,128)S(1)}, f32[2,65,768]{2,1,0:T(8,128)}, u32[]{:S(2)}) copy-start(f32[2,65,768]{2,1,0:T(8,128)} %slice.306) | copy-start | bytes 1198084
  477.0 80.9 %copy-start.76 = (f32[2,128]{1,0:T(2,128)S(1)}, f32[2,128]{1,0:T(2,128)}, u32[]{:S(2)}) copy-start(f32[2,128]{1,0:T(2,128)} %copy-done.75) | copy-start | bytes 3076
  549.8 10.3 %copy-start.30 = (bf16[96,8,4,256]{3,1,2,0:T(8,128)(2,1)S(1)}, bf16[96,8,4,256]{3,1,2,0:T(8,128)(2,1)}, u32[]{:S(2)}) copy-start(bf16[96,8,4,256]{3,1,2,0:T(8,128)(2,1)} %copy.196) | copy-start | bytes 4718596
  549.8 10.3 %copy-start.41 = (bf16[1,4,2,2,2,24,768]{6,5,4,3,2,1,0:T(8,128)(2,1)S(1)}, bf16[1,4,2,2,2,24,768]{6,5,4,3,2,1,0:T(8,128)(2,1)}, u32[]{:S(2)}) copy-start(bf16[1,4,2,2,2,24,768]{6,5,4,3,2,1,0:T(8,128)(2,1)} %get-tuple-element.178) | copy-start | bytes 3538948
  (73 other events, 224.2 us)
Sparse Core Ops, SparseCore 0:
  11.0 83.1 all-gather.2
  97.1 78.8 all-gather.4
  294.9 117.3 reduce-scatter.2
  418.5 121.4 reduce-scatter.4

commit v2 on v1

--- a/solution.py
+++ b/solution.py
@@ -696,6 +696,628 @@
     )(low, high, first, qkv, shifted, mixed, totals)
 
 
+def dot_nn(left, right):
+    return jnp.dot(left, right, preferred_element_type=jnp.float32)
+
+
+def dot_nt(left, right):
+    return lax.dot_general(left, right, (((1,), (1,)), ((), ())), preferred_element_type=jnp.float32)
+
+
+def dot_tn(left, right):
+    return lax.dot_general(left, right, (((0,), (0,)), ((), ())), preferred_element_type=jnp.float32)
+
+
+def norm_parts(values):
+    centred = values - jnp.mean(values, axis=-1, keepdims=True)
+    scale = lax.rsqrt(jnp.mean(centred * centred, axis=-1, keepdims=True) + 1e-05)
+    return centred * scale, scale
+
+
+def norm_pull(values, gain, grad):
+    unit, scale = norm_parts(values)
+    scaled = grad * gain
+    pulled = scale * (
+        scaled
+        - jnp.mean(scaled, axis=-1, keepdims=True)
+        - unit * jnp.mean(scaled * unit, axis=-1, keepdims=True)
+    )
+    return pulled, jnp.sum(grad * unit, axis=0, keepdims=True)
+
+
+def shift_rows(rows, lead):
+    joined = jnp.concatenate([rows.astype(jnp.float32), lead.astype(jnp.float32)], axis=0)
+    return pltpu.roll(joined, joined.shape[0] - LEAD, 0)[: rows.shape[0]]
+
+
+def stack_pair(rows):
+    lane = lax.broadcasted_iota(jnp.int32, rows.shape, 1)
+    zero = jnp.zeros_like(rows)
+    return jnp.concatenate(
+        [jnp.where(lane < HEAD_DIM, rows, zero), jnp.where(lane < HEAD_DIM, zero, rows)], axis=0
+    )
+
+
+def unstack_pair(rows):
+    lane = lax.broadcasted_iota(jnp.int32, (SPAN, 2 * HEAD_DIM), 1)
+    return jnp.where(lane < HEAD_DIM, rows[:SPAN], rows[SPAN:])
+
+
+def middle_kernel(
+    att_ref, hid_ref, lead_hid_ref, grad_ref, lead_grad_ref, gain_ref, used_ref, sq_ref, kv_hbm, neigh_hbm,
+    up_hbm, down_hbm,
+    result_ref, first_ref, d_att_ref, n2_ref, d_cq_ref, cm_ref, gc_ref, ga_ref, gy_ref, act_ref, d_pair_ref,
+    d_gain_ref, d_up_hbm,
+    kv_ref, neigh_ref, up_ref, down_ref, att_rows, second_ref, cq_ref, pair_ref, prob_ref, acc_ref, d_n3_ref,
+    n3_ref, n3t_ref, d_up_ref, sems,
+):
+    micro, tokens, width = hid_ref.shape
+    rows = micro * tokens
+    pulls = [
+        pltpu.make_async_copy(src, dst, sems.at[index])
+        for index, (src, dst) in enumerate(
+            [(kv_hbm, kv_ref), (neigh_hbm, neigh_ref), (up_hbm, up_ref), (down_hbm, down_ref)]
+        )
+    ]
+    for pull in pulls:
+        pull.start()
+    gain_cross, gain_mlp = gain_ref[1:2, :], gain_ref[2:3, :]
+    for index in range(micro):
+        part = pl.ds(index * tokens, tokens)
+        hidden = shift_rows(hid_ref[index], lead_hid_ref[index])
+        gy_ref[part, :] = shift_rows(grad_ref[index], lead_grad_ref[index]).astype(jnp.bfloat16)
+        first_ref[part, :] = hidden + dot_tn(att_ref[index], sq_ref[0])
+    n2_ref[...] = (norm_parts(first_ref[...])[0] * gain_cross).astype(jnp.bfloat16)
+    cq_ref[...] = dot_nn(n2_ref[...], sq_ref[1]).astype(jnp.bfloat16)
+
+    pulls[0].wait()
+    pulls[1].wait()
+    chunk = 256
+    chunks = neigh_ref.shape[0] // chunk
+
+    def make_pairs(step, carry):
+        side, block = step // chunks, lax.rem(step, chunks)
+        part = pl.ds(pl.multiple_of(block * chunk, chunk), chunk)
+        pair_ref[side, part, :] = dot_nn(neigh_ref[part, :], kv_ref[side]).astype(jnp.bfloat16)
+        return carry
+
+    lax.fori_loop(0, 2 * chunks, make_pairs, 0)
+    couples = HEADS // 2
+    pair_rows = NEIGHBOURS * NEIGH_LEN
+    groups = rows // SPAN
+
+    def where(step):
+        group, couple = step // couples, lax.rem(step, couples)
+        tok = pl.ds(pl.multiple_of(group * SPAN, SPAN), SPAN)
+        key = pl.ds(pl.multiple_of(group * pair_rows, pair_rows), pair_rows)
+        lanes = pl.ds(pl.multiple_of(couple * 2 * HEAD_DIM, 2 * HEAD_DIM), 2 * HEAD_DIM)
+        return tok, key, lanes
+
+    def cross_step(step, carry):
+        tok, key, lanes = where(step)
+        query = stack_pair(cq_ref[tok, lanes])
+        scores = dot_nt(query, pair_ref[0, key, lanes]) * SCORE_SCALE
+        weights = jnp.exp(scores - jnp.max(scores, axis=-1, keepdims=True))
+        probs = weights / jnp.sum(weights, axis=-1, keepdims=True)
+        prob_ref[step] = probs
+        mixed = unstack_pair(dot_nn(probs.astype(jnp.bfloat16), pair_ref[1, key, lanes]))
+        cm_ref[tok, lanes] = (mixed * used_ref[tok, :]).astype(jnp.bfloat16)
+        return carry
+
+    lax.fori_loop(0, groups * couples, cross_step, 0)
+    second_ref[...] = first_ref[...] + dot_nn(cm_ref[...], sq_ref[2])
+    n3 = (norm_parts(second_ref[...])[0] * gain_mlp).astype(jnp.bfloat16)
+    n3_ref[...] = n3
+    n3t_ref[...] = n3.T
+    acc_ref[...] = second_ref[...]
+    d_n3_ref[...] = jnp.zeros_like(d_n3_ref)
+    pulls[2].wait()
+    pulls[3].wait()
+    ff_blocks = up_ref.shape[1] // width
+
+    def mlp_step(step, carry):
+        cols = pl.ds(pl.multiple_of(step * width, width), width)
+        upper = dot_nn(n3_ref[...], up_ref[:, cols])
+        square = upper * upper
+        flat = jnp.tanh(math.sqrt(2.0 / math.pi) * upper * (1.0 + 0.044715 * square))
+        half = 0.5 * (1.0 + flat)
+        active = (upper * half).astype(jnp.bfloat16)
+        act_ref[:, cols] = active
+        slope = half + 0.5 * upper * (1.0 - flat * flat) * math.sqrt(2.0 / math.pi) * (
+            1.0 + 3.0 * 0.044715 * square
+        )
+        d_upper = (dot_nt(gy_ref[...], down_ref[cols, :]) * slope).astype(jnp.bfloat16)
+        acc_ref[...] += dot_nn(active, down_ref[cols, :])
+        d_n3_ref[...] += dot_nt(d_upper, up_ref[:, cols])
+        d_up_ref[:, cols] = dot_nn(n3t_ref[...], d_upper).astype(jnp.bfloat16)
+        pltpu.make_async_copy(d_up_ref.at[:, cols], d_up_hbm.at[:, cols], sems.at[4]).start()
+        return carry
+
+    lax.fori_loop(0, ff_blocks, mlp_step, 0)
+    result_ref[...] = acc_ref[...].astype(jnp.bfloat16)
+    pulled, d_gain_mlp = norm_pull(second_ref[...], gain_mlp, d_n3_ref[...])
+    d_second = gy_ref[...].astype(jnp.float32) + pulled
+    acc_ref[...] = d_second
+    gc_ref[...] = d_second.astype(jnp.bfloat16)
+    att_rows[...] = (
+        dot_nt(gc_ref[...], sq_ref[2]).astype(jnp.bfloat16).astype(jnp.float32) * used_ref[...]
+    ).astype(jnp.bfloat16)
+
+    def cross_back(step, carry):
+        tok, key, lanes = where(step)
+        grad = stack_pair(att_rows[tok, lanes])
+        query = stack_pair(cq_ref[tok, lanes])
+        probs = prob_ref[step]
+        d_probs = dot_nt(grad, pair_ref[1, key, lanes])
+        d_scores = (
+            probs * (d_probs - jnp.sum(probs * d_probs, axis=-1, keepdims=True))
+        ).astype(jnp.bfloat16)
+        d_query = unstack_pair(dot_nn(d_scores, pair_ref[0, key, lanes]))
+        d_cq_ref[tok, lanes] = (d_query * SCORE_SCALE).astype(jnp.bfloat16)
+        d_pair_ref[0, key, lanes] = (dot_tn(d_scores, query) * SCORE_SCALE).astype(jnp.bfloat16)
+        d_pair_ref[1, key, lanes] = dot_tn(probs.astype(jnp.bfloat16), grad).astype(jnp.bfloat16)
+        return carry
+
+    lax.fori_loop(0, groups * couples, cross_back, 0)
+    pulled, d_gain_cross = norm_pull(first_ref[...], gain_cross, dot_nt(d_cq_ref[...], sq_ref[1]))
+    d_first = acc_ref[...] + pulled
+    first_ref[...] = d_first
+    ga_ref[...] = d_first.astype(jnp.bfloat16)
+    for index in range(micro):
+        d_att_ref[index] = dot_nt(sq_ref[0], ga_ref[pl.ds(index * tokens, tokens), :]).astype(jnp.bfloat16)
+    d_gain_ref[...] = jnp.concatenate([d_gain_cross, d_gain_mlp, jnp.zeros((6, width), jnp.float32)], axis=0)
+    pltpu.make_async_copy(d_up_ref, d_up_hbm, sems.at[4]).wait()
+
+
+def middle(attended_t, hidden, lead_hid, grads, lead_grad, gains, used, squares, kv, neigh, up, down):
+    micro, tokens, width = hidden.shape
+    rows = micro * tokens
+    ff = up.shape[1]
+    low = jnp.bfloat16
+    out_shape = [
+        jax.ShapeDtypeStruct((rows, width), low),
+        jax.ShapeDtypeStruct((rows, width), jnp.float32),
+        jax.ShapeDtypeStruct((micro, width, tokens), low),
+        jax.ShapeDtypeStruct((rows, width), low),
+        jax.ShapeDtypeStruct((rows, width), low),
+        jax.ShapeDtypeStruct((rows, width), low),
+        jax.ShapeDtypeStruct((rows, width), low),
+        jax.ShapeDtypeStruct((rows, width), low),
+        jax.ShapeDtypeStruct((rows, width), low),
+        jax.ShapeDtypeStruct((rows, ff), low),
+        jax.ShapeDtypeStruct((2,) + neigh.shape, low),
+        jax.ShapeDtypeStruct((8, width), jnp.float32),
+        jax.ShapeDtypeStruct((width, ff), low),
+    ]
+    steps = rows // SPAN * HEADS // 2
+    scratch = [
+        pltpu.VMEM(kv.shape, low),
+        pltpu.VMEM(neigh.shape, low),
+        pltpu.VMEM(up.shape, low),
+        pltpu.VMEM(down.shape, low),
+        pltpu.VMEM((rows, width), low),
+        pltpu.VMEM((rows, width), jnp.float32),
+        pltpu.VMEM((rows, width), low),
+        pltpu.VMEM((2,) + neigh.shape, low),
+        pltpu.VMEM((steps, 2 * SPAN, NEIGHBOURS * NEIGH_LEN), jnp.float32),
+        pltpu.VMEM((rows, width), jnp.float32),
+        pltpu.VMEM((rows, width), jnp.float32),
+        pltpu.VMEM((rows, width), low),
+        pltpu.VMEM((width, rows), low),
+        pltpu.VMEM((width, ff), low),
+        pltpu.SemaphoreType.DMA((5,)),
+    ]
+    return pl.pallas_call(
+        middle_kernel,
+        out_shape=out_shape,
+        in_specs=[VMEM] * 8 + [ANY] * 4,
+        out_specs=[VMEM] * 12 + [ANY],
+        scratch_shapes=scratch,
+        compiler_params=local_params(),
+        cost_estimate=pl.CostEstimate(flops=12 * 10**9, bytes_accessed=40 * 10**6, transcendentals=10**6),
+    )(attended_t, hidden, lead_hid, grads, lead_grad, gains, used, squares, kv, neigh, up, down)
+
+
+def last_kernel(depth, items, skew, *refs):
+    count = len(items)
+    (
+        back_ref, result_ref, first_ref, n2_ref, d_cq_ref, cm_ref, gc_ref, ga_ref, gy_ref, act_ref, d_pair_ref,
+        att_ref, neigh_ref, kv_ref, qkv_ref, hidden_ref, gain_ref, cos_ref, sin_ref, d_gain_rest_ref,
+    ) = refs[:20]
+    (
+        output_ref, grad_in_ref, grad_neigh_ref, out_qkv, out_att, out_cq, out_co, out_kv, out_down, gain_out,
+    ) = refs[20:30]
+    full = refs[30 : 30 + count]
+    got_core = refs[30 + count : 30 + 2 * count]
+    got_one = refs[30 + 2 * count : 30 + 3 * count]
+    got_two = refs[30 + 3 * count : 30 + 4 * count]
+    got_z = refs[30 + 4 * count : 30 + 5 * count]
+    (
+        sent_ref, tail_first, tail_result, raw_ref, n1t_ref, d_n1_ref, temp_ref, gain_mine, gain_got, gain_z,
+        send_sem, recv_sem, unit_send, unit_recv, tail_send, tail_recv, gain_send, gain_recv,
+    ) = refs[30 + 5 * count :]
+    micro, tokens, width = hidden_ref.shape
+    total = depth * 8
+    z, y, c, x = coords()
+    me = lax.axis_index("blk") * 2 + lax.axis_index("head")
+    mine, holder = unit_of(me, total)
+    whole = slice(None)
+    all_barrier(total, me)
+
+    after = lax.rem(me + 1, total)
+    after_at = (after // 2, lax.rem(after, 2))
+    tails = []
+    for index in range(micro):
+        part = pl.ds(index * tokens + tokens - 64, 64)
+        tails.append(
+            remote(first_ref.at[part], tail_first.at[index], tail_send.at[index], tail_recv.at[index], after_at)
+        )
+        tails.append(
+            remote(
+                result_ref.at[part], tail_result.at[index],
+                tail_send.at[micro + index], tail_recv.at[micro + index], after_at,
+            )
+        )
+
+    def slot(device):
+        return back_ref.at[:, :, pl.ds(pl.multiple_of(device * tokens, 128), tokens)]
+
+    @pl.when(holder)
+    def _():
+        pltpu.make_async_copy(slot(me), sent_ref.at[mine], unit_recv).start()
+
+        def send(step, carry):
+            peer = lax.rem(me + step, total)
+            remote(
+                slot(peer), sent_ref.at[mine], unit_send, unit_recv, (peer // 2, lax.rem(peer, 2))
+            ).start()
+            return carry
+
+        lax.fori_loop(1, total, send, 0)
+
+    for tail in tails:
+        tail.start()
+
+    slab = full[0].shape[-2]
+
+    def spread(index, block):
+        buffer = full[index]
+        cols = buffer.shape[-1]
+
+        def body(level, carry):
+            for place_in in range(8):
+                at = pl.multiple_of((level * 8 + place_in) * slab, 8)
+                buffer[block, level, place_in // 4, (place_in // 2) % 2, place_in % 2] = temp_ref[
+                    pl.ds(at, slab), :cols
+                ].astype(jnp.bfloat16)
+            return carry
+
+        lax.fori_loop(0, depth, body, 0)
+
+    down_index = [index for index, item in enumerate(items) if item[0] == "down"]
+
+    def make_down():
+        def body(level, carry):
+            cols = pl.ds(pl.multiple_of(level * width, width), width)
+            temp_ref[...] = dot_tn(act_ref[:, cols], gy_ref[...])
+            for place_in in range(8):
+                for part, index in enumerate(down_index):
+                    at = place_in * slab * len(down_index) + part * slab
+                    full[index][0, level, place_in // 4, (place_in // 2) % 2, place_in % 2] = temp_ref[
+                        pl.ds(at, slab), :
+                    ].astype(jnp.bfloat16)
+            return carry
+
+        lax.fori_loop(0, depth, body, 0)
+
+    def take_units():
+        @pl.when(holder)
+        def _():
+            part = back_ref.at[:, :, pl.ds(0, tokens * (total - 1))]
+            pltpu.make_async_copy(part, part, unit_send).wait()
+
+        pltpu.make_async_copy(sent_ref, sent_ref, unit_recv).wait()
+        half = HEAD_DIM // 2
+
+        def body(head, carry):
+            for index in range(micro):
+                lanes = pl.ds(index * tokens, tokens)
+                cosine, sine = cos_ref[index], sin_ref[index]
+                for part in range(3):
+                    value = sent_ref[index * HEADS + head, part].astype(jnp.float32)
+                    at = pl.multiple_of(part * width + head * HEAD_DIM, HEAD_DIM)
+                    if part < 2:
+                        first_half, second_half = value[:half], value[half:]
+                        value = jnp.concatenate(
+                            [
+                                first_half * cosine + second_half * sine,
+                                second_half * cosine - first_half * sine,
+                            ],
+                            axis=0,
+                        )
+                    raw_ref[pl.ds(at, HEAD_DIM), lanes] = value.astype(jnp.bfloat16)
+            return carry
+
+        lax.fori_loop(0, HEADS, body, 0)
+        for index in range(micro):
+            normed = norm_parts(hidden_ref[index].astype(jnp.float32))[0] * gain_ref[0:1, :]
+            n1t_ref[:, pl.ds(index * tokens, tokens)] = normed.astype(jnp.bfloat16).T
+
+    def make(index):
+        kind, which = items[index][:2]
+        if kind == "down":
+            if index == down_index[0]:
+                make_down()
+            return
+        if kind == "kv":
+            temp_ref[...] = dot_tn(neigh_ref[...], d_pair_ref[which])
+        elif kind == "att":
+            temp_ref[...] = dot_nn(att_ref[0], ga_ref[pl.ds(0, tokens), :])
+            for step in range(1, micro):
+                temp_ref[...] += dot_nn(att_ref[step], ga_ref[pl.ds(step * tokens, tokens), :])
+        elif kind == "cq":
+            temp_ref[...] = dot_tn(n2_ref[...], d_cq_ref[...])
+        elif kind == "co":
+            temp_ref[...] = dot_tn(cm_ref[...], gc_ref[...])
+        else:
+            if which == 0:
+                take_units()
+            for block in range(2):
+                half = width // 2
+                at = which * width + block * half
+                temp_ref[:, :half] = dot_nt(n1t_ref[...], raw_ref[pl.ds(at, half), :])
+                spread(index, block)
+            return
+        spread(index, 0)
+
+    def core(index):
+        return remote(
+            full[index].at[whole, whole, whole, 1 - c], got_core[index],
+            send_sem.at[index, 0], recv_sem.at[index, 0], place(z, y, 1 - c, x),
+        )
+
+    def one(index):
+        if items[index][2] == 0:
+            src, where = full[index].at[whole, whole, 1 - y, c], place(z, 1 - y, c, x)
+        else:
+            src, where = full[index].at[whole, whole, whole, c, 1 - x], place(z, y, c, 1 - x)
+        return remote(src, got_one[index], send_sem.at[index, 1], recv_sem.at[index, 1], where)
+
+    def two(index):
+        if items[index][2] == 0:
+            src, where = full[index].at[whole, whole, y, c, 1 - x], place(z, y, c, 1 - x)
+        else:
+            src, where = full[index].at[whole, whole, 1 - y, c, x], place(z, 1 - y, c, x)
+        return remote(src, got_two[index], send_sem.at[index, 2], recv_sem.at[index, 2], where)
+
+    def send_z(index):
+        for step in range(1, depth):
+            other = lax.rem(z + step, depth)
+            remote(
+                full[index].at[whole, other, y, c, x], got_z[index].at[z],
+                send_sem.at[index, 3], recv_sem.at[index, 3], place(other, y, c, x),
+            ).start()
+
+    def add_into(target, source):
+        target[...] = (target[...].astype(jnp.float32) + source[...].astype(jnp.float32)).astype(
+            jnp.bfloat16
+        )
+
+    def each_level(index, body):
+        blocks = full[index].shape[0]
+        lax.fori_loop(
+            0, blocks * depth, lambda step, carry: (body(step // depth, lax.rem(step, depth)), carry)[1], 0
+        )
+
+    def sum_core(index):
+        def body(block, level):
+            for row in range(2):
+                for col in range(2):
+                    add_into(
+                        full[index].at[block, level, row, c, col], got_core[index].at[block, level, row, col]
+                    )
+
+        each_level(index, body)
+
+    def sum_one(index):
+        def body(block, level):
+            for side in range(2):
+                if items[index][2] == 0:
+                    target = full[index].at[block, level, y, c, side]
+                else:
+                    target = full[index].at[block, level, side, c, x]
+                add_into(target, got_one[index].at[block, level, side])
+
+        each_level(index, body)
+
+    def sum_two(index):
+        each_level(
+            index,
+            lambda block, level: add_into(
+                full[index].at[block, level, y, c, x], got_two[index].at[block, level]
+            ),
+        )
+
+    def sum_z(index):
+        kind, which = items[index][:2]
+        for block in range(full[index].shape[0]):
+            value = full[index][block, z, y, c, x].astype(jnp.float32)
+            for step in range(1, depth):
+                value = value + got_z[index][lax.rem(z + step, depth), block].astype(jnp.float32)
+            if kind == "down":
+                out_down[pl.ds(which * slab, slab), :] = value
+            elif kind == "kv":
+                out_kv[:, pl.ds(which * width, width)] = value
+            elif kind == "qkv":
+                out_qkv[:, pl.ds(which * width + block * (width // 2), width // 2)] = value
+            else:
+                {"att": out_att, "cq": out_cq, "co": out_co}[kind][...] = value
+
+    def phase(index, number):
+        if number == 0:
+            make(index)
+            core(index).start()
+        elif number == 1:
+            core(index).wait_recv()
+            sum_core(index)
+            one(index).start()
+        elif number == 2:
+            one(index).wait_recv()
+            sum_one(index)
+            two(index).start()
+        elif number == 3:
+            two(index).wait_recv()
+            sum_two(index)
+            send_z(index)
+        else:
+            landed = got_z[index].at[pl.ds(0, depth - 1)]
+            pltpu.make_async_copy(landed, landed, recv_sem.at[index, 3]).wait()
+            sum_z(index)
+
+    def gain_copy(stage):
+        where = (place(z, y, 1 - c, x), place(z, 1 - y, c, x), place(z, y, c, 1 - x))[stage]
+        return remote(
+            gain_mine.at[stage], gain_got.at[stage], gain_send.at[stage], gain_recv.at[stage], where
+        )
+
+    def gain_phase(number):
+        if number == 0:
+            gain_copy(0).start()
+        elif number < 4:
+            gain_copy(number - 1).wait_recv()
+            gain_mine[number] = gain_mine[number - 1] + gain_got[number - 1]
+            if number < 3:
+                gain_copy(number).start()
+            else:
+                for step in range(1, depth):
+                    other = lax.rem(z + step, depth)
+                    remote(
+                        gain_mine.at[3], gain_z.at[z], gain_send.at[3], gain_recv.at[3], place(other, y, c, x)
+                    ).start()
+        else:
+            landed = gain_z.at[pl.ds(0, depth - 1)]
+            pltpu.make_async_copy(landed, landed, gain_recv.at[3]).wait()
+            value = gain_mine[3]
+            for step in range(1, depth):
+                value = value + gain_z[lax.rem(z + step, depth)]
+            gain_out[...] = value
+
+    def neighbours_part(block):
+        chunk = 256
+        part = pl.ds(block * chunk, chunk)
+        grad_neigh_ref[part, :] = (
+            dot_nt(d_pair_ref[0, part, :], kv_ref[0]) + dot_nt(d_pair_ref[1, part, :], kv_ref[1])
+        ).astype(jnp.bfloat16)
+
+    def input_part():
+        half = width // 2
+        blocks = qkv_ref.shape[0]
+        d_n1_ref[...] = dot_nn(qkv_ref[0], raw_ref[pl.ds(0, half), :])
+        for block in range(1, blocks):
+            d_n1_ref[...] += dot_nn(qkv_ref[block], raw_ref[pl.ds(block * half, half), :])
+        for tail in tails:
+            tail.wait()
+        d_gain = jnp.zeros((1, width), jnp.float32)
+        for index in range(micro):
+            part = pl.ds(index * tokens, tokens)
+            d_normed = d_n1_ref[:, part].T
+            pulled, part_gain = norm_pull(hidden_ref[index].astype(jnp.float32), gain_ref[0:1, :], d_normed)
+            d_gain = d_gain + part_gain
+            joined = jnp.concatenate([tail_first[index], first_ref[part, :]], axis=0)
+            home = pltpu.roll(joined, joined.shape[0] - 1, 0)[:tokens]
+            grad_in_ref[part, :] = (home + pulled).astype(jnp.bfloat16)
+            joined = jnp.concatenate(
+                [tail_result[index].astype(jnp.float32), result_ref[part, :].astype(jnp.float32)], axis=0
+            )
+            output_ref[part, :] = pltpu.roll(joined, joined.shape[0] - 1, 0)[:tokens].astype(jnp.bfloat16)
+        gain_mine[0] = jnp.concatenate([d_gain, d_gain_rest_ref[0:7, :]], axis=0)
+
+    pairs = (count + 1) // 2
+    chunks = neigh_ref.shape[0] // 256
+    for step in range(pairs + 1 + skew * 4):
+        for number in range(4, -1, -1):
+            pair = step - skew * number
+            if 0 <= pair < pairs:
+                for index in range(2 * pair, min(2 * pair + 2, count)):
+                    phase(index, number)
+            elif pair == pairs:
+                if number == 0:
+                    input_part()
+                gain_phase(number)
+        if 1 <= step <= chunks:
+            neighbours_part(step - 1)
+    for index in range(count):
+        core(index).wait_send()
+        one(index).wait_send()
+        two(index).wait_send()
+        gone = got_z[index].at[pl.ds(0, depth - 1)]
+        pltpu.make_async_copy(gone, gone, send_sem.at[index, 3]).wait()
+    for stage in range(3):
+        gain_copy(stage).wait_send()
+    gone = gain_z.at[pl.ds(0, depth - 1)]
+    pltpu.make_async_copy(gone, gone, gain_send.at[3]).wait()
+
+
+def last(depth, collective, ff, *args):
+    hidden = args[15]
+    micro, tokens, width = hidden.shape
+    rows = micro * tokens
+    total = depth * 8
+    slab = width // total
+    neigh_rows = args[12].shape[0]
+    items = [
+        ("down", 0, 0), ("down", 1, 1), ("down", 2, 0), ("down", 3, 1), ("kv", 0, 0), ("kv", 1, 1),
+        ("att", 0, 0), ("cq", 0, 1), ("co", 0, 0), ("qkv", 0, 1), ("qkv", 1, 0), ("qkv", 2, 1),
+    ]
+    count = len(items)
+    low, high = jnp.bfloat16, jnp.float32
+    out_shape = [
+        jax.ShapeDtypeStruct((rows, width), low),
+        jax.ShapeDtypeStruct((rows, width), low),
+        jax.ShapeDtypeStruct((neigh_rows, width), low),
+        jax.ShapeDtypeStruct((slab, 3 * width), high),
+        jax.ShapeDtypeStruct((slab, width), high),
+        jax.ShapeDtypeStruct((slab, width), high),
+        jax.ShapeDtypeStruct((slab, width), high),
+        jax.ShapeDtypeStruct((slab, 2 * width), high),
+        jax.ShapeDtypeStruct((ff // total, width), high),
+        jax.ShapeDtypeStruct((8, width), high),
+    ]
+    full, core, one, two, along = [], [], [], [], []
+    for kind, which, order in items:
+        blocks, cols = (2, width // 2) if kind == "qkv" else (1, width)
+        full.append(pltpu.VMEM((blocks, depth, 2, 2, 2, slab, cols), low))
+        core.append(pltpu.VMEM((blocks, depth, 2, 2, slab, cols), low))
+        one.append(pltpu.VMEM((blocks, depth, 2, slab, cols), low))
+        two.append(pltpu.VMEM((blocks, depth, slab, cols), low))
+        along.append(pltpu.VMEM((depth, blocks, slab, cols), low))
+    dma = pltpu.SemaphoreType.DMA
+    scratch = full + core + one + two + along + [
+        pltpu.VMEM((UNITS, 3, HEAD_DIM, tokens), low),
+        pltpu.VMEM((micro, 64, width), high),
+        pltpu.VMEM((micro, 64, width), low),
+        pltpu.VMEM((3 * width, rows), low),
+        pltpu.VMEM((width, rows), low),
+        pltpu.VMEM((width, rows), high),
+        pltpu.VMEM((width, width), high),
+        pltpu.VMEM((4, 8, width), high),
+        pltpu.VMEM((3, 8, width), high),
+        pltpu.VMEM((depth, 8, width), high),
+        dma((count, 4)), dma((count, 4)), dma, dma, dma((2 * micro,)), dma((2 * micro,)), dma((4,)), dma((4,)),
+    ]
+    return pl.pallas_call(
+        functools.partial(last_kernel, depth, items, 1),
+        out_shape=out_shape,
+        in_specs=[ANY] + [VMEM] * 19,
+        out_specs=[VMEM] * 10,
+        scratch_shapes=scratch,
+        compiler_params=pltpu.CompilerParams(
+            collective_id=collective, has_side_effects=True, vmem_limit_bytes=62 * 2**20
+        ),
+        cost_estimate=pl.CostEstimate(flops=10**10, bytes_accessed=40 * 10**6, transcendentals=0),
+    )(*args)
+
+
 def layer_norm(values, norm_gain):
     centred = values - jnp.mean(values, axis=-1, keepdims=True)
     spread = jnp.mean(centred * centred, axis=-1, keepdims=True)
@@ -705,90 +1327,6 @@
 def norm_backward(values, norm_gain, grad_out):
     result, pullback = jax.vjp(layer_norm, values, norm_gain)
     return pullback(grad_out)
-
-
-def gelu_tanh(values):
-    return jax.nn.gelu(values, approximate=True)
-
-
-def soft_forward(scores):
-    maximum = jnp.max(scores, axis=-1, keepdims=True)
-    exp_rows = jnp.exp(scores - maximum)
-    row_total = jnp.sum(exp_rows, axis=-1, keepdims=True)
-    return (exp_rows / row_total, maximum + jnp.log(row_total))
-
-
-def soft_backward(scores, log_total, grad_probs):
-    attn_probs = jnp.exp(scores - log_total)
-    row_delta = jnp.sum(attn_probs * grad_probs, axis=-1, keepdims=True)
-    return (attn_probs, (attn_probs * (grad_probs - row_delta)).astype(jnp.bfloat16))
-
-
-def split_cross(query_groups, pair_groups):
-    group_count, span_rows, model_width = query_groups.shape
-    pair_rows = pair_groups.shape[1]
-    query_rows = query_groups.reshape(group_count, span_rows, HEADS, HEAD_DIM)
-    key_rows = pair_groups[..., :model_width].reshape(group_count, pair_rows, HEADS, HEAD_DIM)
-    value_rows = pair_groups[..., model_width:].reshape(group_count, pair_rows, HEADS, HEAD_DIM)
-    return (query_rows, key_rows, value_rows)
-
-
-def cross_forward(query_groups, pair_groups, score_scale):
-    group_count, span_rows, model_width = query_groups.shape
-    query_rows, key_rows, value_rows = split_cross(query_groups, pair_groups)
-    scores = (
-        jnp.einsum("cqhd,ckhd->chqk", query_rows, key_rows, preferred_element_type=jnp.float32)
-        * score_scale
-    )
-    attn_probs, log_total = soft_forward(scores)
-    mixed_rows = jnp.einsum(
-        "chqk,ckhd->cqhd",
-        attn_probs.astype(jnp.bfloat16),
-        value_rows,
-        preferred_element_type=jnp.float32,
-    )
-    return (mixed_rows.reshape(group_count, span_rows, model_width), log_total)
-
-
-def cross_backward(query_groups, pair_groups, log_total, grad_groups, score_scale):
-    group_count, span_rows, model_width = query_groups.shape
-    pair_rows = pair_groups.shape[1]
-    query_rows, key_rows, value_rows = split_cross(query_groups, pair_groups)
-    grad_rows = grad_groups.reshape(group_count, span_rows, HEADS, HEAD_DIM)
-    scores = (
-        jnp.einsum("cqhd,ckhd->chqk", query_rows, key_rows, preferred_element_type=jnp.float32)
-        * score_scale
-    )
-    grad_probs = jnp.einsum(
-        "cqhd,ckhd->chqk", grad_rows, value_rows, preferred_element_type=jnp.float32
-    )
-    attn_probs, grad_scores = soft_backward(scores, log_total, grad_probs)
-    grad_query = (
-        jnp.einsum("chqk,ckhd->cqhd", grad_scores, key_rows, preferred_element_type=jnp.float32)
-        * score_scale
-    )
-    grad_key = (
-        jnp.einsum("chqk,cqhd->ckhd", grad_scores, query_rows, preferred_element_type=jnp.float32)
-        * score_scale
-    )
-    grad_value = jnp.einsum(
-        "chqk,cqhd->ckhd",
-        attn_probs.astype(jnp.bfloat16),
-        grad_rows,
-        preferred_element_type=jnp.float32,
-    )
-    grad_pairs = jnp.concatenate(
-        [
-            grad_key.reshape(group_count, pair_rows, model_width),
-            grad_value.reshape(group_count, pair_rows, model_width),
-        ],
-        axis=-1,
-    )
-    return (grad_query.reshape(group_count, span_rows, model_width), grad_pairs)
-
-
-def dot32(left, right):
-    return jnp.dot(left, right, preferred_element_type=jnp.float32)
 
 
 def outer(left, right):
@@ -841,12 +1379,11 @@
         depth, w_qkv, w_attn_out, w_cross_q, w_cross_out, w_cross_kv, small, hidden_in, out_grad
     )
     gains = got_small[:, :3, :gain_rows].astype(jnp.float32).transpose(1, 0, 2).reshape(3, model_width)
-    gain_attn, gain_cross, gain_mlp = gains[0], gains[1], gains[2]
+    gain_attn = gains[0]
     seg_full = got_small[:, 3 : 3 + micro, :tok_count].transpose(1, 0, 2).reshape(micro, length)
     seg_full = seg_full.astype(jnp.int32)
     qkv_blocks = got_qkv.reshape(6, model_width, model_width // 2)
     squares = got_sq.reshape(3, model_width, model_width)
-    attn_out_full, cross_q_full, cross_out_full = squares[0], squares[1], squares[2]
     kv_blocks = got_kv.reshape(2, model_width, model_width)
 
     token_index = device * tok_count + jnp.arange(tok_count, dtype=jnp.int32)
@@ -887,66 +1424,42 @@
     (attended_t,) = to_tokens(total, shifted[None], (), 2)
     attended_t = attended_t.reshape(micro, model_width, tok_count)
 
-    def shift(rows, lead):
-        return jnp.concatenate([rows[:, LEAD:], lead[:, :LEAD]], axis=1).reshape(row_count, model_width)
-
-    hidden_s = shift(hidden_in, lead_hid).astype(jnp.float32)
-    grad_low = shift(out_grad, lead_grad)
-    cotangent = grad_low.astype(jnp.float32)
-    after_attn = hidden_s + jnp.einsum(
-        "mdt,de->mte", attended_t, attn_out_full, preferred_element_type=jnp.float32
-    ).reshape(row_count, model_width)
-    normed_cross = layer_norm(after_attn, gain_cross).astype(jnp.bfloat16)
-    cross_query = dot32(normed_cross, cross_q_full).astype(jnp.bfloat16)
-    neigh_rows = neighbours.reshape(micro * span_count * pair_rows, model_width)
-    groups = micro * span_count
-    pairs_local = jnp.concatenate(
-        [dot32(neigh_rows, kv_blocks[0]).astype(jnp.bfloat16), dot32(neigh_rows, kv_blocks[1]).astype(jnp.bfloat16)],
-        axis=1,
-    ).reshape(groups, pair_rows, 2 * model_width)
     shifted_index = token_index + LEAD
     used = jnp.where(
         shifted_index[None] < length, jnp.repeat(neighbour_valid, SPAN, axis=1).astype(jnp.float32), 0.0
     ).reshape(row_count, 1)
-    query_groups = cross_query.reshape(groups, SPAN, model_width)
-    cross_rows, cross_total = cross_forward(query_groups, pairs_local, SCORE_SCALE)
-    cross_mixed = (cross_rows.reshape(row_count, model_width) * used).astype(jnp.bfloat16)
-    after_cross = after_attn + dot32(cross_mixed, cross_out_full)
-    normed_mlp = layer_norm(after_cross, gain_mlp).astype(jnp.bfloat16)
-    mlp_upper = dot32(normed_mlp, up_full)
-    activated, gelu_pull = jax.vjp(gelu_tanh, mlp_upper)
-    activated = activated.astype(jnp.bfloat16)
-    result_rows = (after_cross + dot32(activated, down_full)).astype(jnp.bfloat16)
-    result_rows = result_rows.reshape(micro, tok_count, model_width)
-    d_activated = dot32(grad_low, down_full.T)
-    d_upper = gelu_pull(d_activated)[0].astype(jnp.bfloat16)
-    d_normed_mlp = dot32(d_upper, up_full.T)
-
-    up_share = lax.psum_scatter(
-        outer(normed_mlp, d_upper).astype(jnp.bfloat16), AXES, scatter_dimension=0, tiled=True
-    ).astype(jnp.float32)
-    down_share = lax.psum_scatter(
-        outer(activated, grad_low).astype(jnp.bfloat16), AXES, scatter_dimension=0, tiled=True
-    ).astype(jnp.float32)
-
-    d_second_in, d_gain_mlp = norm_backward(after_cross, gain_mlp, d_normed_mlp)
-    d_second = cotangent + d_second_in
-    d_second_low = d_second.astype(jnp.bfloat16)
-    d_mixed = dot32(d_second_low, cross_out_full.T).astype(jnp.bfloat16)
-    d_groups = (d_mixed.astype(jnp.float32) * used).astype(jnp.bfloat16).reshape(groups, SPAN, model_width)
-    grad_query_groups, d_pairs = cross_backward(
-        query_groups, pairs_local, cross_total, d_groups, SCORE_SCALE
+    neigh_rows = neighbours.reshape(micro * span_count * pair_rows, model_width)
+    (
+        result_rows, d_first, d_attended_t, normed_cross, d_cross_query, cross_mixed, d_second_low, d_first_low,
+        grad_low, activated, d_pairs, d_gain_rest, d_up,
+    ) = middle(
+        attended_t, hidden_in, lead_hid, out_grad, lead_grad, gains, used, squares, kv_blocks, neigh_rows,
+        up_full, down_full,
     )
-    d_cross_query = grad_query_groups.reshape(row_count, model_width).astype(jnp.bfloat16)
-    d_normed_cross = dot32(d_cross_query, cross_q_full.T)
-    d_first_in, d_gain_cross = norm_backward(after_attn, gain_cross, d_normed_cross)
-    d_first = d_second + d_first_in
-    d_first_low = d_first.astype(jnp.bfloat16).reshape(micro, tok_count, model_width)
-    d_attended_t = jnp.einsum(
-        "de,mte->mdt", attn_out_full, d_first_low, preferred_element_type=jnp.float32
-    ).astype(jnp.bfloat16)
+    up_share = lax.psum_scatter(d_up, AXES, scatter_dimension=0, tiled=True).astype(jnp.float32)
+    in_kernel = gain_rows % 8 == 0
+    if not in_kernel:
+        down_share = lax.psum_scatter(
+            outer(activated, grad_low).astype(jnp.bfloat16), AXES, scatter_dimension=0, tiled=True
+        ).astype(jnp.float32)
     unit_grad = to_units(total, d_attended_t.reshape(UNITS, 1, HEAD_DIM, tok_count), 3)
     unit_back = attn_backward(low, high, first_row, unit_qkv, unit_grad[0], mixed, totals)
+    if in_kernel:
+        (
+            output, grad_in, grad_neighbours, s_qkv, s_att, s_cq, s_co, s_kv, s_down, s_gain,
+        ) = last(
+            depth, 5, w_up.shape[1],
+            unit_back, result_rows, d_first, normed_cross, d_cross_query, cross_mixed, d_second_low, d_first_low,
+            grad_low, activated, d_pairs, attended_t, neigh_rows, kv_blocks, qkv_blocks, hidden_in, gains,
+            cosine.transpose(1, 0, 2), sine.transpose(1, 0, 2), d_gain_rest,
+        )
+        own_gain = lax.dynamic_slice_in_dim(s_gain, device * gain_rows, gain_rows, 1)
+        return (
+            output.reshape(hidden_in.shape), grad_in.reshape(hidden_in.shape),
+            grad_neighbours.reshape(neighbours.shape),
+            own_gain[0], s_qkv, s_att, own_gain[1], s_cq, s_kv, s_co, own_gain[2], up_share, s_down,
+        )
+    result_rows = result_rows.reshape(micro, tok_count, model_width)
     d_first = d_first.reshape(micro, tok_count, model_width)
     sent_t, tail_first, tail_result = to_tokens(
         total, unit_back, (d_first[:, tok_count - 64 :], result_rows[:, tok_count - 64 :]), 4
@@ -968,8 +1481,8 @@
     )
     grad_in = (d_first_home + d_hidden_in).astype(jnp.bfloat16)
 
-    d_pairs_low = d_pairs.astype(jnp.bfloat16).reshape(groups * pair_rows, 2 * model_width)
-    d_keys, d_values = d_pairs_low[:, :model_width], d_pairs_low[:, model_width:]
+    d_keys, d_values = d_pairs[0], d_pairs[1]
+    d_first_low = d_first_low.reshape(micro, tok_count, model_width)
     d_neigh = (
         jnp.einsum("te,de->td", d_keys, kv_blocks[0], preferred_element_type=jnp.float32)
         + jnp.einsum("te,de->td", d_values, kv_blocks[1], preferred_element_type=jnp.float32)
@@ -990,10 +1503,10 @@
         ]
     )
     d_kv = jnp.stack([outer(neigh_rows, d_keys), outer(neigh_rows, d_values)])
-    d_gains = jnp.stack([d_gain_attn, d_gain_cross, d_gain_mlp]).reshape(3, total, gain_rows)
+    d_gains = jnp.stack([d_gain_attn, d_gain_rest[0], d_gain_rest[1]]).reshape(3, total, gain_rows)
     d_gains = jnp.zeros((total, 8, 128), jnp.float32).at[:, :3, :gain_rows].set(d_gains.transpose(1, 0, 2))
     s_qkv, s_sq, s_kv, s_gain = scatter_all(
-        depth, blocks_of(d_qkv), blocks_of(d_sq), blocks_of(d_kv), d_gains, 5
+        depth, blocks_of(d_qkv), blocks_of(d_sq), blocks_of(d_kv), d_gains, 6
     )
     return (
         output,

time: 585 us -> 447 us (0.76); the launches traced: 574 us -> 446 us
  local copies, waits for them, and re-layouts: 103 us -> 22.2 us
  matrix products: 74.7 us -> 3.22 us
  Pallas kernels: 342 us -> 393 us
  other arithmetic: 37.8 us -> 11.8 us
    pallas_call x1 -> x2, Pallas kernels: 72.7 us -> 170 us  [the longest x1 124 us: last(): pl.pallas_call(functools.partial(last_kernel, depth, items, 1), out_shape...]
    dot_general x29 -> x0, matrix products: 71.4 us -> none  [the longest x10 33.6 us: dot32(): return jnp.dot(left, right, preferred_element_type=jnp.float32)]
    pallas_call x2 -> x1, Pallas kernels: 62.3 us -> 23.7 us  [to_tokens(): pl.pallas_call(functools.partial(to_tokens_kernel, total, count), out_sha...]
    convert_element_type x8 -> x0, local copies, waits for them, and re-layouts: 18.3 us -> none  [the longest x1 6.11 us: blocks_of(): array.astype(jnp.bfloat16)]
    slice x14 -> x1, local copies, waits for them, and re-layouts: 17.9 us -> 0.05 us  [on_device(): gain_attn = gains[0]]
    another operation x9 -> x0, local copies, waits for them, and re-layouts: 14.1 us -> none  [the longest x2 4.94 us: on_device(): cross_rows.reshape(row_count, model_width) * used]
    reshape x4 -> x1, local copies, waits for them, and re-layouts: 10.7 us -> 0.69 us  [on_device(): got_small[:, :3, :gain_rows].astype(jnp.float32).transpose(1, 0, 2)]
    pallas_call x2, Pallas kernels: 65.6 us -> 55.8 us  [to_units(): pl.pallas_call(functools.partial(to_units_kernel, total), out_shape=jax.S...]
  transfers between devices with their start and end apart: 4 -> 3, of which waited for: 0 -> 0; matrix products, arithmetic and copies ran while one was open for 33% -> 6% of each run, Pallas kernels for 59% -> 78%
where the time goes in v2:
time: 447 us; the launch traced here: 446 us
  Pallas kernels  393 us (88%)
  local copies, waits for them, and re-layouts  22.2 us (5%)
  between operations  14.3 us (3%)
  other arithmetic  11.8 us (3%)
    pallas_call x1, Pallas kernels, last(): pl.pallas_call(functools.partial(last_kernel, depth, items, 1), out_shape...  124 us
    pallas_call x1, Pallas kernels, gather_all(): pl.pallas_call(functools.partial(gather_kernel, depth, items), out_shape=...  80.7 us
    pallas_call x2, Pallas kernels, to_units(): pl.pallas_call(functools.partial(to_units_kernel, total), out_shape=jax.S...  55.8 us
    pallas_call x1, Pallas kernels, middle(): pl.pallas_call(middle_kernel, out_shape=out_shape, in_specs=[VMEM] * 8 +...  45.7 us
    pallas_call x1, Pallas kernels, attn_backward(): pl.pallas_call(attn_backward_kernel, out_shape=jax.ShapeDtypeStruct((3, w...  31.5 us
    pallas_call x1, Pallas kernels, attn_forward(): pl.pallas_call(attn_forward_kernel, out_shape=[jax.ShapeDtypeStruct((widt...  31.4 us
    pallas_call x1, Pallas kernels, to_tokens(): pl.pallas_call(functools.partial(to_tokens_kernel, total, count), out_sha...  23.7 us
    unnamed x63, local copies, waits for them, and re-layouts  12.2 us
  transfers between devices with their start and end apart: 3, of which 0 were waited for; matrix products, arithmetic and copies ran while one was open for 6% of the time, Pallas kernels for 78%

profile of v2, /device:TPU:0, one launch (start us, length us, event | category | flops | bytes accessed | tf_op | source)
XLA Modules:
  0.0 445.8 jit_solution(111170438937534861)
XLA Ops:
  10.2 0.8 scatter.15
  11.0 0.8 scatter.16
  12.5 80.7 %shard_map.246 = (bf16[6,4,2,2,2,24,384]{6,5,4,3,2,1,0:T(8,128)(2,1)}, bf16[3,4,2,2,2,24,768]{6,5,4,3,2,1,0:T(8,128)(2,1)}, bf16[2,4,2,2,2,24,768]{6,5,4,3,2,1,0...) custom-call(bf16[24,2304]{1,0:T(8,128)(2,1)} %refs_0_.1, ...), custom_call_target="tpu_custom_call" | custom-call | tf_op jit(solution)/shard_map/pallas_call | solution.py:192
  93.2 0.9 convert_bitcast_fusion.1
  96.4 1.3 convert_reduce_fusion.1
  99.1 0.8 convert_bitcast_fusion
  101.3 3.2 fusion.9
  104.8 1.0 fusion.6
  105.8 1.5 squeeze.20
  109.7 1.1 pad_maximum_fusion
  110.8 39.6 %shard_map.247.qkv_ref = bf16[3,64,4096]{2,1,0:T(8,128)(2,1)} custom-call(bf16[24,3,64,128]{3,2,1,0:T(8,128)(2,1)} %bitcast.61), custom_call_target="tpu_custom_call" | custom-call | tf_op jit(solution)/shard_map/pallas_call | solution.py:258
  151.7 31.4 %shard_map.248 = (bf16[64,4096]{1,0:T(8,128)(2,1)}, f32[64,4096]{1,0:T(8,128)}, f32[1,4096]{1,0:T(1,128)}) custom-call(s32[16]{0:T(128)} %get-tuple-element.125.low_ref, s32[1,4096]{1,0:T(1,128)} %compare_select_fusion.first_ref, bf16[3,64,4096]{2,1,0:T(8,128)(2,1)} %shard_map.247.qkv_ref), custom_call_target="tpu_custom_call" | custom-call | flops 1000000000 | bytes 4000000 | tf_op jit(solution)/shard_map/pallas_call | solution.py:668
  183.1 23.7 %shard_map.249 = bf16[24,1,64,128]{3,2,1,0:T(8,128)(2,1)} custom-call(bf16[1,64,4096]{2,1,0:T(8,128)(2,1)} %bitcast.67), custom_call_target="tpu_custom_call" | custom-call | tf_op jit(solution)/shard_map/pallas_call | solution.py:320
  208.6 45.7 %shard_map.250 = (bf16[256,768]{1,0:T(8,128)(2,1)}, f32[256,768]{1,0:T(8,128)}, bf16[2,768,128]{2,1,0:T(8,128)(2,1)}, bf16[256,768]{1,0:T(8,128)(2,1)}, bf16[256...) custom-call(bf16[2,768,128]{2,1,0:T(8,128)(2,1)} %bitcast.68, ...), custom_call_target="tpu_custom_call" | custom-call | flops 12000000000 | bytes 40000000 | tf_op jit(solution)/shard_map/pallas_call | solution.py:910
  255.0 0.8 multiply_sine_fusion
  255.8 16.2 %shard_map.251 = bf16[1,64,4096]{2,1,0:T(8,128)(2,1)} custom-call(bf16[24,1,64,128]{3,2,1,0:T(8,128)(2,1)} %bitcast.70), custom_call_target="tpu_custom_call" | custom-call | tf_op jit(solution)/shard_map/pallas_call | solution.py:258
  272.0 31.5 %shard_map.252.refs_0_ = bf16[3,64,4096]{2,1,0:T(8,128)(2,1)} custom-call(s32[16]{0:T(128)} %get-tuple-element.125.low_ref, s32[16]{0:T(128)} %broadcast_select_fusion.high_ref, s32[1,4096]{1,0:T(1,128)} %compare_select_fusion.first_ref, bf16[3,64,4096]{2,1,0:T(8,128)(2,1)} %shard_map.247.qkv_ref, bf16[64,4096]{1,0:T(8,128)(2,1)} %bitcast.66, ...), custom_call_target="tpu_custom_call" | custom-call | flops 3000000000 | bytes 4000000 | tf_op jit(solution)/shard_map/pallas_call | solution.py:684
  303.5 124.0 %shard_map.253 = (bf16[256,768]{1,0:T(8,128)(2,1)}, bf16[256,768]{1,0:T(8,128)(2,1)}, bf16[1024,768]{1,0:T(8,128)(2,1)}, f32[24,2304]{1,0:T(8,128)}, f32[24,768]...) custom-call(bf16[3,64,4096]{2,1,0:T(8,128)(2,1)} %shard_map.252.refs, ...), custom_call_target="tpu_custom_call" | custom-call | flops 10000000000 | bytes 40000000 | tf_op jit(solution)/shard_map/pallas_call | solution.py:1308
  427.5 0.9 constant_dynamic-slice_fusion
  428.9 1.6 convert_element_type.73
  430.5 1.8 copy.100
  432.4 1.8 copy.101
  434.2 1.1 copy.102
  438.6 0.7 copy.108
  (110 shorter events, 18.4 us)
Async XLA Ops:
  7.2 93.5 %copy-start = (bf16[2,128,768]{2,1,0:T(8,128)(2,1)S(1)}, bf16[2,128,768]{2,1,0:T(8,128)(2,1)}, u32[]{:S(2)}) copy-start(bf16[2,128,768]{2,1,0:T(8,128)(2,1)} %refs_15_.1) | copy-start | bytes 1179652
  7.2 201.4 %all-gather.3.cloned.1.call-start = ((), (), s32[]{:S(2)}) async-start(), calls=%async_computation.1 | async-start | bytes 4866048 | tf_op jit(solution)/shard_map/all_gather | solution.py:1371
  7.9 200.7 %all-gather.5.cloned.1.call-start = ((), (), s32[]{:S(2)}) async-start(), calls=%async_computation.2 | async-start | bytes 4866048 | tf_op jit(solution)/shard_map/all_gather | solution.py:1372
  8.7 420.2 %reduce-scatter.2.cloned.1.call-start = ((), (), s32[]{:S(2)}) async-start(), calls=%async_computation.3 | async-start | bytes 4866048 | tf_op jit(solution)/shard_map/reduce_scatter | solution.py:1439
  94.1 7.2 %copy-start.4 = (s32[2,4096]{1,0:T(2,128)}, s32[2,4096]{1,0:T(2,128)S(1)}, u32[]{:S(2)}) copy-start(s32[2,4096]{1,0:T(2,128)S(1)} %convert_bitcast_fusion.1) | copy-start | bytes 98308
  95.7 5.7 %copy-start.17 = (s32[16]{0:T(128)}, s32[16]{0:T(128)S(1)}, u32[]{:S(2)}) copy-start(s32[16]{0:T(128)S(1)} %convert_reduce_fusion.3) | copy-start | bytes 196
  105.8 2.0 copy-start.5
  105.8 2.0 copy-start.21
  107.8 1.6 copy-start.19
  109.7 40.8 %copy-start.18 = (s32[16]{0:T(128)S(1)}, s32[16]{0:T(128)}, u32[]{:S(2)}) copy-start(s32[16]{0:T(128)} %copy-done.17) | copy-start | bytes 196
  109.7 41.3 %copy-start.11 = (s32[1,1,16,256]{3,1,2,0:T(1,128)S(1)}, s32[1,1,16,256]{3,1,2,0:T(1,128)}, u32[]{:S(2)}) copy-start(s32[1,1,16,256]{3,1,2,0:T(1,128)} %copy.74) | copy-start | bytes 49156
  109.7 41.3 %copy-start.12 = (s32[1,1,16,256]{3,1,2,0:T(1,128)S(1)}, s32[1,1,16,256]{3,1,2,0:T(1,128)}, u32[]{:S(2)}) copy-start(s32[1,1,16,256]{3,1,2,0:T(1,128)} %copy.75) | copy-start | bytes 49156
  109.7 41.3 %copy-start.13 = (s32[1,1,16,256]{3,1,2,0:T(1,128)S(1)}, s32[1,1,16,256]{3,1,2,0:T(1,128)}, u32[]{:S(2)}) copy-start(s32[1,1,16,256]{3,1,2,0:T(1,128)} %copy.73) | copy-start | bytes 49156
  151.6 55.1 %copy-start.6 = (f32[3,32,24]{2,1,0:T(8,128)S(1)}, f32[3,32,24]{2,1,0:T(8,128)}, u32[]{:S(2)}) copy-start(f32[3,32,24]{2,1,0:T(8,128)} %copy.65) | copy-start | bytes 27652
  151.7 55.8 %copy-start.22 = (s32[2,2]{1,0:T(2,128)S(1)}, s32[2,2]{1,0:T(2,128)}, u32[]{:S(2)}) copy-start(s32[2,2]{1,0:T(2,128)} %param.25) | copy-start | bytes 52
  254.3 0.7 copy-start.16
  254.3 0.7 copy-start.20
  427.4 6.7 %copy-start.1 = (bf16[1024,768]{1,0:T(8,128)(2,1)S(1)}, bf16[1024,768]{1,0:T(8,128)(2,1)}, u32[]{:S(2)}) copy-start(bf16[1024,768]{1,0:T(8,128)(2,1)} %get-tuple-element.116) | copy-start | bytes 4718596
  430.5 4.8 %copy-start.3 = (f32[24,2304]{1,0:T(8,128)S(1)}, f32[24,2304]{1,0:T(8,128)}, u32[]{:S(2)}) copy-start(f32[24,2304]{1,0:T(8,128)} %get-tuple-element.167) | copy-start | bytes 663556
  432.3 3.7 copy-start.10
  432.3 4.3 copy-start.9
  432.3 5.0 %copy-start.7 = (f32[24,1536]{1,0:T(8,128)S(1)}, f32[24,1536]{1,0:T(8,128)}, u32[]{:S(2)}) copy-start(f32[24,1536]{1,0:T(8,128)} %get-tuple-element.171) | copy-start | bytes 442372
  432.3 5.6 %copy-start.8 = (f32[24,768]{1,0:T(8,128)S(1)}, f32[24,768]{1,0:T(8,128)}, u32[]{:S(2)}) copy-start(f32[24,768]{1,0:T(8,128)} %get-tuple-element.172) | copy-start | bytes 221188
  432.3 6.2 %copy-start.2 = (f32[96,768]{1,0:T(8,128)S(1)}, f32[96,768]{1,0:T(8,128)}, u32[]{:S(2)}) copy-start(f32[96,768]{1,0:T(8,128)} %get-tuple-element.175) | copy-start | bytes 884740
  (2 other events, 1.2 us)
Sparse Core Ops, SparseCore 0:
  10.9 81.8 all-gather.2
  95.8 74.3 all-gather.4
  254.5 134.2 reduce-scatter.1

commit v3 on v2

--- a/solution.py
+++ b/solution.py
@@ -534,8 +534,9 @@
 MICRO = 2
 UNITS = MICRO * HEADS
 AXES = ("blk", "head")
-TILE = 256
+TILE = 512
 LEAD = SPAN - 1
+DOC_MAX = 2000
 SCORE_SCALE = 1.0 / math.sqrt(HEAD_DIM)
 LOG2E = math.log2(math.e)
 
@@ -549,8 +550,8 @@
 
 
 def tile_mask(key_tile, query_tile, first_row):
-    key_place = key_tile * TILE + lax.broadcasted_iota(jnp.int32, (TILE, TILE), 0)
-    query_place = query_tile * TILE + lax.broadcasted_iota(jnp.int32, (TILE, TILE), 1)
+    key_place = key_tile * TILE + lax.broadcasted_iota(jnp.int32, (TILE, 1), 0)
+    query_place = query_tile * TILE + lax.broadcasted_iota(jnp.int32, (1, TILE), 1)
     return (key_place <= query_place) & (key_place >= first_row)
 
 
@@ -696,6 +697,395 @@
     )(low, high, first, qkv, shifted, mixed, totals)
 
 
+def first_kernel(depth, items, *refs):
+    count = len(items)
+    w_refs = refs[:7]
+    small_ref, hid_ref, grad_ref = refs[7:10]
+    (
+        qkv_out, sq_out, kv_out, up_out, down_out, lead_hid, lead_grad, gain_out, cos_out, sin_out,
+        unit_out, mixed_out, total_out, start_out, att_out,
+    ) = refs[10:25]
+    (
+        qkv_ref, small_all, hid_vmem, n1_ref, temp_ref, note_ref, turned_ref, doc_ref,
+        own_sem, send_sem, recv_sem, misc_sem, lead_send, lead_recv, load_sem, unit_send, unit_recv,
+        att_send, att_recv,
+    ) = refs[25:]
+    z, y, c, x = coords()
+    total = depth * 8
+    me = lax.axis_index("blk") * 2 + lax.axis_index("head")
+    mine, holder = unit_of(me, total)
+    slab = w_refs[0].shape[0]
+    micro, tokens, width = hid_ref.shape
+    homes = (qkv_ref, sq_out, kv_out, up_out, down_out)
+    whole = slice(None)
+
+    def view(item, zs, ys, cs, xs):
+        buffer, first, last, kind = item
+        if buffer == 4:
+            return down_out.at[zs, ys, cs, xs, pl.ds(first, last - first)]
+        return homes[buffer].at[pl.ds(first, last - first), zs, ys, cs, xs]
+
+    load = pltpu.make_async_copy(hid_ref, hid_vmem, load_sem.at[0])
+    load.start()
+    own = []
+    for index, item in enumerate(items):
+        buffer, first, last, kind = item
+        cols = homes[buffer].shape[-1]
+        if buffer == 4:
+            moves = [(w_refs[6].at[pl.ds(first, last - first)], view(item, z, y, c, x))]
+        elif buffer == 1:
+            moves = [(w_refs[1 + block], sq_out.at[block, z, y, c, x]) for block in range(first, last)]
+        else:
+            source = w_refs[(0, None, 4, 5)[buffer]]
+            moves = [
+                (source.at[:, pl.ds(block * cols, cols)], homes[buffer].at[block, z, y, c, x])
+                for block in range(first, last)
+            ]
+        for src, dst in moves:
+            pltpu.make_async_copy(src, dst, own_sem.at[index]).start()
+        mirror = view(item, z, y, c, x)
+        own.append(pltpu.make_async_copy(mirror, mirror, own_sem.at[index]))
+    pltpu.make_async_copy(small_ref, small_all.at[me], misc_sem.at[1]).start()
+    all_barrier(total, me)
+
+    def send_small(step, carry):
+        peer = lax.rem(me + step, total)
+        remote(
+            small_ref, small_all.at[me], misc_sem.at[0], misc_sem.at[1], (peer // 2, lax.rem(peer, 2))
+        ).start()
+        return carry
+
+    prev = lax.rem(me + total - 1, total)
+    prev_at = (prev // 2, lax.rem(prev, 2))
+    leads = [
+        remote(hid_ref.at[:, pl.ds(0, 64)], lead_hid, lead_send.at[0], lead_recv.at[0], prev_at),
+        remote(grad_ref.at[:, pl.ds(0, 64)], lead_grad, lead_send.at[1], lead_recv.at[1], prev_at),
+    ]
+
+    def start(index):
+        own[index].wait()
+        item = items[index]
+        for step in range(1, depth):
+            other = lax.rem(z + step, depth)
+            remote(
+                view(item, z, y, c, x), view(item, z, y, c, x),
+                send_sem.at[index, 0], recv_sem.at[index, 0], place(other, y, c, x),
+            ).start()
+
+    def bulk(index, phase):
+        item = items[index]
+        first_x = item[3] == 0
+        if phase == 1:
+            ref = view(item, whole, y, c, x)
+            where = place(z, y, c, 1 - x) if first_x else place(z, 1 - y, c, x)
+        elif phase == 2:
+            ref = view(item, whole, y, c, whole) if first_x else view(item, whole, whole, c, x)
+            where = place(z, 1 - y, c, x) if first_x else place(z, y, c, 1 - x)
+        else:
+            ref = view(item, whole, whole, c, whole)
+            where = place(z, y, 1 - c, x)
+        return remote(ref, ref, send_sem.at[index, phase], recv_sem.at[index, phase], where)
+
+    def arrived(index, phase):
+        if phase == 0:
+            ref = view(items[index], pl.ds(0, depth - 1), y, c, x)
+            pltpu.make_async_copy(ref, ref, recv_sem.at[index, 0]).wait()
+        else:
+            bulk(index, phase).wait_recv()
+
+    def sent(index, phase):
+        if phase == 0:
+            ref = view(items[index], pl.ds(0, depth - 1), y, c, x)
+            pltpu.make_async_copy(ref, ref, send_sem.at[index, 0]).wait()
+        else:
+            bulk(index, phase).wait_send()
+
+    pairs = (count + 1) // 2
+
+    def gather_step(step):
+        for phase in range(4, -1, -1):
+            pair = step - phase
+            if not 0 <= pair < pairs:
+                continue
+            for index in range(2 * pair, min(2 * pair + 2, count)):
+                if phase == 0:
+                    start(index)
+                else:
+                    arrived(index, phase - 1)
+                    if phase < 4:
+                        bulk(index, phase).start()
+
+    half_dim = HEAD_DIM // 2
+
+    def tables():
+        lane = lax.broadcasted_iota(jnp.int32, (half_dim, tokens), 1)
+        order = lax.broadcasted_iota(jnp.int32, (half_dim, tokens), 0)
+        frequency = jnp.exp(order.astype(jnp.float32) * (-2.0 * math.log(10000.0) / HEAD_DIM))
+        angles = (me * tokens + lane).astype(jnp.float32) * frequency
+        cos_out[...] = jnp.cos(angles)
+        sin_out[...] = jnp.sin(angles)
+
+    def normalise():
+        load.wait()
+        pltpu.make_async_copy(small_all, small_all, misc_sem.at[1]).wait()
+        for peer in range(total):
+            temp_ref[pl.ds(peer * slab, slab), pl.ds(0, 128)] = small_all[peer, :slab, :].astype(jnp.float32)
+            doc_ref[pl.ds(peer, 1), :] = jnp.where(
+                mine < HEADS, small_all[peer, 32:33, :].astype(jnp.float32), small_all[peer, 33:34, :].astype(jnp.float32)
+            )
+        turned = temp_ref[:, pl.ds(0, 128)].T
+        gain_out[...] = jnp.concatenate(
+            [turned[0:1], turned[32:33], turned[64:65], jnp.zeros((5, width), jnp.float32)], axis=0
+        )
+        for index in range(micro):
+            unit_rows = norm_parts(hid_vmem[index].astype(jnp.float32))[0]
+            n1_ref[pl.ds(index * tokens, tokens), :] = (unit_rows * gain_out[0:1, :]).astype(jnp.bfloat16)
+
+    def project(part):
+        cols = qkv_ref.shape[-1]
+        heads = cols // HEAD_DIM
+        for half in range(2):
+            block = part * 2 + half
+            for level in range(depth):
+                for inner in range(8):
+                    at = (level * 8 + inner) * slab
+                    temp_ref[pl.ds(at, slab), :] = qkv_ref[
+                        block, level, inner // 4, (inner // 2) % 2, inner % 2
+                    ].astype(jnp.float32)
+            raw = dot_nn(n1_ref[...], temp_ref[...].astype(jnp.bfloat16))
+            for index in range(micro):
+                raw_t = raw[index * tokens : (index + 1) * tokens].T
+                for head in range(heads):
+                    value = raw_t[head * HEAD_DIM : (head + 1) * HEAD_DIM]
+                    if part < 2:
+                        first_half, second_half = value[:half_dim], value[half_dim:]
+                        value = jnp.concatenate(
+                            [
+                                first_half * cos_out[...] - second_half * sin_out[...],
+                                second_half * cos_out[...] + first_half * sin_out[...],
+                            ],
+                            axis=0,
+                        )
+                    note_ref[index * HEADS + half * heads + head, part] = value.astype(jnp.bfloat16)
+
+    def slot(device, part):
+        return unit_out.at[part, :, pl.ds(pl.multiple_of(device * tokens, 128), tokens)]
+
+    def send_part(part):
+        @pl.when(holder)
+        def _():
+            pltpu.make_async_copy(note_ref.at[mine, part], slot(me, part), unit_recv).start()
+
+        def send(step, carry):
+            peer = lax.rem(me + step, total)
+            unit, held = unit_of(peer, total)
+
+            @pl.when(held)
+            def _():
+                remote(
+                    note_ref.at[unit, part], slot(me, part), unit_send, unit_recv, (peer // 2, lax.rem(peer, 2))
+                ).start()
+
+            return carry
+
+        lax.fori_loop(1, total, send, 0)
+
+    def doc_starts():
+        docs = doc_ref[...]
+        lane = lax.broadcasted_iota(jnp.int32, docs.shape, 1)
+        row = lax.broadcasted_iota(jnp.int32, docs.shape, 0)
+        place_at = row * tokens + lane
+        before = jnp.where(
+            lane == 0, pltpu.roll(pltpu.roll(docs, 1, 0), 1, 1), pltpu.roll(docs, 1, 1)
+        )
+        begins = (docs != before) | (place_at == 0)
+        value = jnp.where(begins, place_at, 0).astype(jnp.float32)
+        step = 1
+        while step < tokens:
+            value = jnp.maximum(value, jnp.where(lane >= step, pltpu.roll(value, step, 1), 0.0))
+            step *= 2
+        carried = jnp.broadcast_to(jnp.max(value, axis=1, keepdims=True), docs.shape)
+        carried = jnp.where(row >= 1, pltpu.roll(carried, 1, 0), 0.0)
+        step = 1
+        while step < total:
+            carried = jnp.maximum(carried, jnp.where(row >= step, pltpu.roll(carried, step, 0), 0.0))
+            step *= 2
+        starts = jnp.maximum(value, carried).astype(jnp.int32)
+        for peer in range(total):
+            start_out[:, pl.ds(peer * tokens, tokens)] = starts[peer : peer + 1, :]
+
+    length = tokens * total
+    tiles = length // TILE
+    reach = (TILE + DOC_MAX - 2) // TILE
+
+    def open_units():
+        @pl.when(holder)
+        def _():
+            part = note_ref.at[pl.ds(0, UNITS - 1)]
+            pltpu.make_async_copy(unit_out, unit_out, unit_recv).wait()
+            pltpu.make_async_copy(part, part, unit_send).wait()
+
+        @pl.when(jnp.logical_not(holder))
+        def _():
+            pltpu.make_async_copy(note_ref, note_ref, unit_send).wait()
+
+    def attend(query_tile):
+        @pl.when(holder)
+        def _():
+            columns = pl.ds(query_tile * TILE, TILE)
+            query_t = unit_out[0, :, columns]
+            first_row = start_out[:, columns]
+
+            def one_key(step, state):
+                peak, weight, mixed = state
+                key_tile = query_tile - step
+                scores = dot_nn(tile_at(unit_out, key_tile, 1).T, query_t) * (SCORE_SCALE * LOG2E)
+                scores = jnp.where(tile_mask(key_tile, query_tile, first_row), scores, -1e30)
+                new_peak = jnp.maximum(peak, jnp.max(scores, axis=0, keepdims=True))
+                probs = jnp.exp2(scores - new_peak)
+                fade = jnp.exp2(peak - new_peak)
+                weight = weight * fade + jnp.sum(probs, axis=0, keepdims=True)
+                mixed = mixed * fade + dot_nn(tile_at(unit_out, key_tile, 2), probs.astype(jnp.bfloat16))
+                return new_peak, weight, mixed
+
+            begin = (
+                jnp.full((1, TILE), -1e30, jnp.float32),
+                jnp.zeros((1, TILE), jnp.float32),
+                jnp.zeros((HEAD_DIM, TILE), jnp.float32),
+            )
+            peak, weight, mixed = lax.fori_loop(0, min(query_tile, reach) + 1, one_key, begin)
+            mixed_out[:, columns] = mixed / weight
+            total_out[:, columns] = peak + jnp.log2(weight)
+
+    def back_slot(device):
+        return turned_ref.at[:, pl.ds(pl.multiple_of(device * tokens, 128), tokens)]
+
+    def send_back():
+        @pl.when(holder)
+        def _():
+            def turn(step, carry):
+                part = pl.ds(pl.multiple_of(step * 16, 16), 16)
+                turned_ref[part, :] = pltpu.roll(mixed_out[part, :], length - LEAD, 1).astype(jnp.bfloat16)
+                return carry
+
+            lax.fori_loop(0, HEAD_DIM // 16, turn, 0)
+            pltpu.make_async_copy(back_slot(me), att_out.at[mine], att_recv).start()
+
+            def send(step, carry):
+                peer = lax.rem(me + step, total)
+                remote(
+                    back_slot(peer), att_out.at[mine], att_send, att_recv, (peer // 2, lax.rem(peer, 2))
+                ).start()
+                return carry
+
+            lax.fori_loop(1, total, send, 0)
+
+    gather_step(0)
+    lax.fori_loop(1, total, send_small, 0)
+    tables()
+    gather_step(1)
+    gather_step(2)
+    for lead in leads:
+        lead.start()
+    normalise()
+    gather_step(3)
+    doc_starts()
+    for part in range(3):
+        gather_step(4 + part)
+        if part == 2:
+            keep = pltpu.make_async_copy(qkv_ref, qkv_out, load_sem.at[1])
+            keep.start()
+        project(part)
+        send_part(part)
+    wait_steps = 2
+    for step in range(wait_steps):
+        gather_step(7 + step)
+    open_units()
+    for tile in range(tiles):
+        attend(tile)
+        if tile % 2 == 1 and tile < tiles - 1:
+            gather_step(7 + wait_steps + tile // 2)
+    send_back()
+    for step in range(7 + wait_steps + (tiles - 1) // 2, pairs + 4):
+        gather_step(step)
+    for index in range(count):
+        for phase in range(4):
+            sent(index, phase)
+    for lead in leads:
+        lead.wait()
+    keep.wait()
+    rest = small_all.at[pl.ds(0, total - 1)]
+    pltpu.make_async_copy(rest, rest, misc_sem.at[0]).wait()
+    pltpu.make_async_copy(att_out, att_out, att_recv).wait()
+
+    @pl.when(holder)
+    def _():
+        part = turned_ref.at[:, pl.ds(0, tokens * (total - 1))]
+        pltpu.make_async_copy(part, part, att_send).wait()
+
+
+def first(depth, w_qkv, w_attn_out, w_cross_q, w_cross_out, w_kv, w_up, w_down, small, hidden, grads):
+    total = depth * 8
+    rows = w_qkv.shape[0]
+    down_rows = w_down.shape[0]
+    micro, tokens, width = hidden.shape
+    length = tokens * total
+    third = down_rows // 3
+    items = [
+        (0, 0, 1, 0), (0, 1, 2, 1), (0, 2, 3, 0), (0, 3, 4, 1), (0, 4, 5, 0), (0, 5, 6, 1),
+        (1, 0, 1, 0), (1, 1, 2, 1),
+        (2, 0, 1, 0), (2, 1, 2, 1),
+        (1, 2, 3, 0), (3, 0, 1, 1),
+        (3, 1, 2, 0), (3, 2, 3, 1),
+        (3, 3, 4, 0), (4, 0, third, 1),
+        (4, third, 2 * third, 0), (4, 2 * third, down_rows, 1),
+    ]
+    count = len(items)
+    low, high = jnp.bfloat16, jnp.float32
+    spots = (depth, 2, 2, 2)
+    qkv_shape = (6, *spots, rows, width // 2)
+    out_shape = [
+        jax.ShapeDtypeStruct(qkv_shape, low),
+        jax.ShapeDtypeStruct((3, *spots, rows, width), low),
+        jax.ShapeDtypeStruct((2, *spots, rows, width), low),
+        jax.ShapeDtypeStruct((w_up.shape[1] // width, *spots, rows, width), low),
+        jax.ShapeDtypeStruct((*spots, down_rows, width), low),
+        jax.ShapeDtypeStruct((micro, 64, width), low),
+        jax.ShapeDtypeStruct((micro, 64, width), low),
+        jax.ShapeDtypeStruct((8, width), high),
+        jax.ShapeDtypeStruct((HEAD_DIM // 2, tokens), high),
+        jax.ShapeDtypeStruct((HEAD_DIM // 2, tokens), high),
+        jax.ShapeDtypeStruct((3, HEAD_DIM, length), low),
+        jax.ShapeDtypeStruct((HEAD_DIM, length), high),
+        jax.ShapeDtypeStruct((1, length), high),
+        jax.ShapeDtypeStruct((1, length), jnp.int32),
+        jax.ShapeDtypeStruct((UNITS, HEAD_DIM, tokens), low),
+    ]
+    dma = pltpu.SemaphoreType.DMA
+    return pl.pallas_call(
+        functools.partial(first_kernel, depth, items),
+        out_shape=out_shape,
+        in_specs=[VMEM] * 8 + [ANY] * 2,
+        out_specs=[ANY] * 7 + [VMEM] * 8,
+        scratch_shapes=[
+            pltpu.VMEM(qkv_shape, low),
+            pltpu.VMEM((total,) + small.shape, low),
+            pltpu.VMEM(hidden.shape, low),
+            pltpu.VMEM((micro * tokens, width), low),
+            pltpu.VMEM((width, width // 2), high),
+            pltpu.VMEM((UNITS, 3, HEAD_DIM, tokens), low),
+            pltpu.VMEM((HEAD_DIM, length), low),
+            pltpu.VMEM((total, tokens), high),
+            dma((count,)), dma((count, 4)), dma((count, 4)), dma((2,)), dma((2,)), dma((2,)), dma((2,)), dma, dma,
+            dma, dma,
+        ],
+        compiler_params=pltpu.CompilerParams(
+            collective_id=0, has_side_effects=True, vmem_limit_bytes=62 * 2**20
+        ),
+        cost_estimate=pl.CostEstimate(flops=10**9, bytes_accessed=20 * 10**6, transcendentals=0),
+    )(w_qkv, w_attn_out, w_cross_q, w_cross_out, w_kv, w_up, w_down, small, hidden, grads)
+
+
 def dot_nn(left, right):
     return jnp.dot(left, right, preferred_element_type=jnp.float32)
 
@@ -813,11 +1203,11 @@
     d_n3_ref[...] = jnp.zeros_like(d_n3_ref)
     pulls[2].wait()
     pulls[3].wait()
-    ff_blocks = up_ref.shape[1] // width
+    ff_blocks = up_ref.shape[0]
 
     def mlp_step(step, carry):
         cols = pl.ds(pl.multiple_of(step * width, width), width)
-        upper = dot_nn(n3_ref[...], up_ref[:, cols])
+        upper = dot_nn(n3_ref[...], up_ref[step])
         square = upper * upper
         flat = jnp.tanh(math.sqrt(2.0 / math.pi) * upper * (1.0 + 0.044715 * square))
         half = 0.5 * (1.0 + flat)
@@ -828,7 +1218,7 @@
         )
         d_upper = (dot_nt(gy_ref[...], down_ref[cols, :]) * slope).astype(jnp.bfloat16)
         acc_ref[...] += dot_nn(active, down_ref[cols, :])
-        d_n3_ref[...] += dot_nt(d_upper, up_ref[:, cols])
+        d_n3_ref[...] += dot_nt(d_upper, up_ref[step])
         d_up_ref[:, cols] = dot_nn(n3t_ref[...], d_upper).astype(jnp.bfloat16)
         pltpu.make_async_copy(d_up_ref.at[:, cols], d_up_hbm.at[:, cols], sems.at[4]).start()
         return carry
@@ -872,7 +1262,7 @@
 def middle(attended_t, hidden, lead_hid, grads, lead_grad, gains, used, squares, kv, neigh, up, down):
     micro, tokens, width = hidden.shape
     rows = micro * tokens
-    ff = up.shape[1]
+    ff = up.shape[0] * width
     low = jnp.bfloat16
     out_shape = [
         jax.ShapeDtypeStruct((rows, width), low),
@@ -1022,7 +1412,7 @@
         def body(head, carry):
             for index in range(micro):
                 lanes = pl.ds(index * tokens, tokens)
-                cosine, sine = cos_ref[index], sin_ref[index]
+                cosine, sine = cos_ref[...], sin_ref[...]
                 for part in range(3):
                     value = sent_ref[index * HEADS + head, part].astype(jnp.float32)
                     at = pl.multiple_of(part * width + head * HEAD_DIM, HEAD_DIM)
@@ -1234,13 +1624,14 @@
 
     pairs = (count + 1) // 2
     chunks = neigh_ref.shape[0] // 256
-    for step in range(pairs + 1 + skew * 4):
+    for step in range(pairs + skew * 4):
         for number in range(4, -1, -1):
             pair = step - skew * number
-            if 0 <= pair < pairs:
-                for index in range(2 * pair, min(2 * pair + 2, count)):
-                    phase(index, number)
-            elif pair == pairs:
+            if not 0 <= pair < pairs:
+                continue
+            for index in range(2 * pair, min(2 * pair + 2, count)):
+                phase(index, number)
+            if pair == pairs - 1:
                 if number == 0:
                     input_part()
                 gain_phase(number)
@@ -1306,7 +1697,7 @@
         dma((count, 4)), dma((count, 4)), dma, dma, dma((2 * micro,)), dma((2 * micro,)), dma((4,)), dma((4,)),
     ]
     return pl.pallas_call(
-        functools.partial(last_kernel, depth, items, 1),
+        functools.partial(last_kernel, depth, items, 2),
         out_shape=out_shape,
         in_specs=[ANY] + [VMEM] * 19,
         out_specs=[VMEM] * 10,
@@ -1316,6 +1707,25 @@
         ),
         cost_estimate=pl.CostEstimate(flops=10**10, bytes_accessed=40 * 10**6, transcendentals=0),
     )(*args)
+
+
+def finish_kernel(copies, *refs):
+    for source, result in zip(refs[:copies], refs[copies:]):
+        result[...] = source[...].astype(result.dtype)
+
+
+def finish(arrays, low):
+    arrays = [*arrays, low]
+    copies = len(arrays)
+    vmem = pl.BlockSpec(memory_space=pltpu.VMEM)
+    return pl.pallas_call(
+        functools.partial(finish_kernel, copies),
+        out_shape=[jax.ShapeDtypeStruct(a.shape, a.dtype) for a in arrays[:-1]]
+        + [jax.ShapeDtypeStruct(low.shape, jnp.float32)],
+        in_specs=[vmem] * copies,
+        out_specs=[vmem] * copies,
+        compiler_params=pltpu.CompilerParams(vmem_limit_bytes=62 * 2**20),
+    )(*arrays)
 
 
 def layer_norm(values, norm_gain):
@@ -1368,60 +1778,88 @@
     pair_rows = NEIGHBOURS * NEIGH_LEN
     device = lax.axis_index(AXES)
 
-    up_full = lax.all_gather(w_up, AXES, axis=0, tiled=True)
-    down_full = lax.all_gather(w_down, AXES, axis=0, tiled=True)
-
-    small = jnp.zeros((16, 128), jnp.bfloat16)
-    for row, gain in enumerate((norm_attn, norm_cross, norm_mlp)):
-        small = small.at[row, :gain_rows].set(gain)
-    small = small.at[3 : 3 + micro, :tok_count].set(segment_ids.astype(jnp.bfloat16))
-    got_qkv, got_sq, got_kv, got_small, lead_hid, lead_grad = gather_all(
-        depth, w_qkv, w_attn_out, w_cross_q, w_cross_out, w_cross_kv, small, hidden_in, out_grad
-    )
-    gains = got_small[:, :3, :gain_rows].astype(jnp.float32).transpose(1, 0, 2).reshape(3, model_width)
-    gain_attn = gains[0]
-    seg_full = got_small[:, 3 : 3 + micro, :tok_count].transpose(1, 0, 2).reshape(micro, length)
-    seg_full = seg_full.astype(jnp.int32)
+    in_kernel = gain_rows % 8 == 0
+    token_index = device * tok_count + jnp.arange(tok_count, dtype=jnp.int32)
+    if in_kernel:
+        gain_lanes = jnp.concatenate(
+            [jnp.broadcast_to(gain[:, None], (gain_rows, 32)) for gain in (norm_attn, norm_cross, norm_mlp, norm_mlp)],
+            axis=1,
+        )
+        small = jnp.concatenate(
+            [
+                jnp.pad(gain_lanes, ((0, 32 - gain_rows), (0, 0))),
+                jnp.pad(segment_ids.astype(jnp.bfloat16), ((0, 16 - micro), (0, 0))),
+            ],
+            axis=0,
+        )
+        (
+            got_qkv, got_sq, got_kv, up_full, down_full, lead_hid, lead_grad, gains, cosine, sine,
+            unit_qkv, mixed, totals, first_row, attended_t,
+        ) = first(
+            depth, w_qkv, w_attn_out, w_cross_q, w_cross_out, w_cross_kv, w_up, w_down, small, hidden_in, out_grad
+        )
+        up_full = up_full.reshape(-1, model_width, model_width)
+        down_full = down_full.reshape(-1, model_width)
+        attended_t = attended_t.reshape(micro, model_width, tok_count)
+    else:
+        up_full = lax.all_gather(w_up, AXES, axis=0, tiled=True)
+        down_full = lax.all_gather(w_down, AXES, axis=0, tiled=True)
+        up_full = up_full.reshape(model_width, -1, model_width).transpose(1, 0, 2)
+        small = jnp.zeros((16, 128), jnp.bfloat16)
+        for row, gain in enumerate((norm_attn, norm_cross, norm_mlp)):
+            small = small.at[row, :gain_rows].set(gain)
+        small = small.at[3 : 3 + micro, :tok_count].set(segment_ids.astype(jnp.bfloat16))
+        got_qkv, got_sq, got_kv, got_small, lead_hid, lead_grad = gather_all(
+            depth, w_qkv, w_attn_out, w_cross_q, w_cross_out, w_cross_kv, small, hidden_in, out_grad
+        )
+        gains = got_small[:, :3, :gain_rows].astype(jnp.float32).transpose(1, 0, 2).reshape(3, model_width)
+        gain_attn = gains[0]
+        seg_full = got_small[:, 3 : 3 + micro, :tok_count].transpose(1, 0, 2).reshape(micro, length)
+        seg_full = seg_full.astype(jnp.int32)
     qkv_blocks = got_qkv.reshape(6, model_width, model_width // 2)
     squares = got_sq.reshape(3, model_width, model_width)
     kv_blocks = got_kv.reshape(2, model_width, model_width)
 
-    token_index = device * tok_count + jnp.arange(tok_count, dtype=jnp.int32)
-    first_of = jnp.sum(
-        (seg_full[:, None, :] < segment_ids[:, :, None]).astype(jnp.int32), axis=-1
-    )
-    local_pos = token_index[None] - first_of
-    frequency = jnp.exp(
-        jnp.arange(HEAD_DIM // 2, dtype=jnp.float32) * (-2.0 * math.log(10000.0) / HEAD_DIM)
-    )
-    angles = frequency[:, None, None] * local_pos.astype(jnp.float32)[None]
-    cosine, sine = jnp.cos(angles), jnp.sin(angles)
 
     unit, holder = unit_of(device, total)
-    seg_unit = lax.dynamic_index_in_dim(seg_full, unit // HEADS, 0, keepdims=False)
-    seg_tiles = seg_unit.reshape(length // TILE, TILE)
-    tile_first = jnp.sum((seg_unit[None] < seg_tiles[:, :1]).astype(jnp.int32), axis=-1)
-    inside = jnp.sum((seg_tiles[:, None, :] < seg_tiles[:, :, None]).astype(jnp.int32), axis=-1)
     tile_index = jnp.arange(length // TILE, dtype=jnp.int32)
-    first_row = jnp.where(
-        seg_tiles == seg_tiles[:, :1], tile_first[:, None], tile_index[:, None] * TILE + inside
-    ).reshape(1, length)
+    if in_kernel:
+        tile_first = first_row[0, ::TILE]
+    else:
+        seg_unit = lax.dynamic_index_in_dim(seg_full, unit // HEADS, 0, keepdims=False)
+        seg_tiles = seg_unit.reshape(length // TILE, TILE)
+        tile_first = jnp.sum((seg_unit[None] < seg_tiles[:, :1]).astype(jnp.int32), axis=-1)
+        inside = jnp.sum((seg_tiles[:, None, :] < seg_tiles[:, :, None]).astype(jnp.int32), axis=-1)
+        first_row = jnp.where(
+            seg_tiles == seg_tiles[:, :1], tile_first[:, None], tile_index[:, None] * TILE + inside
+        ).reshape(1, length)
     low = tile_first // TILE
     high = jnp.sum((low[None] <= tile_index[:, None]).astype(jnp.int32), axis=-1)
     low = jnp.where(holder, low, tile_index + 1)
     high = jnp.where(holder, high, 0)
 
-    hidden = hidden_in.astype(jnp.float32)
-    normed_attn = layer_norm(hidden, gain_attn).astype(jnp.bfloat16).reshape(row_count, model_width)
-    raw = jnp.einsum("bde,td->bet", qkv_blocks, normed_attn, preferred_element_type=jnp.float32)
-    raw = raw.reshape(3, HEADS, HEAD_DIM, micro, tok_count)
-    rotated = jnp.stack(
-        [turn_heads(raw[0], cosine, sine), turn_heads(raw[1], cosine, sine), raw[2]]
-    ).astype(jnp.bfloat16)
-    message = rotated.transpose(3, 1, 0, 2, 4).reshape(UNITS, 3, HEAD_DIM, tok_count)
-    unit_qkv = to_units(total, message, 1)
-    shifted, mixed, totals = attn_forward(low, first_row, unit_qkv)
-    (attended_t,) = to_tokens(total, shifted[None], (), 2)
+    if not in_kernel:
+        first_of = jnp.sum(
+            (seg_full[:, None, :] < segment_ids[:, :, None]).astype(jnp.int32), axis=-1
+        )
+        local_pos = token_index[None] - first_of
+        frequency = jnp.exp(
+            jnp.arange(HEAD_DIM // 2, dtype=jnp.float32) * (-2.0 * math.log(10000.0) / HEAD_DIM)
+        )
+        angles = frequency[:, None, None] * local_pos.astype(jnp.float32)[None]
+        cosine, sine = jnp.cos(angles), jnp.sin(angles)
+
+        hidden = hidden_in.astype(jnp.float32)
+        normed_attn = layer_norm(hidden, gain_attn).astype(jnp.bfloat16).reshape(row_count, model_width)
+        raw = jnp.einsum("bde,td->bet", qkv_blocks, normed_attn, preferred_element_type=jnp.float32)
+        raw = raw.reshape(3, HEADS, HEAD_DIM, micro, tok_count)
+        rotated = jnp.stack(
+            [turn_heads(raw[0], cosine, sine), turn_heads(raw[1], cosine, sine), raw[2]]
+        ).astype(jnp.bfloat16)
+        message = rotated.transpose(3, 1, 0, 2, 4).reshape(UNITS, 3, HEAD_DIM, tok_count)
+        unit_qkv = to_units(total, message, 1)
+        shifted, mixed, totals = attn_forward(low, first_row, unit_qkv)
+        (attended_t,) = to_tokens(total, shifted[None], (), 2)
     attended_t = attended_t.reshape(micro, model_width, tok_count)
 
     shifted_index = token_index + LEAD
@@ -1436,8 +1874,7 @@
         attended_t, hidden_in, lead_hid, out_grad, lead_grad, gains, used, squares, kv_blocks, neigh_rows,
         up_full, down_full,
     )
-    up_share = lax.psum_scatter(d_up, AXES, scatter_dimension=0, tiled=True).astype(jnp.float32)
-    in_kernel = gain_rows % 8 == 0
+    up_low = lax.psum_scatter(d_up, AXES, scatter_dimension=0, tiled=True)
     if not in_kernel:
         down_share = lax.psum_scatter(
             outer(activated, grad_low).astype(jnp.bfloat16), AXES, scatter_dimension=0, tiled=True
@@ -1451,14 +1888,23 @@
             depth, 5, w_up.shape[1],
             unit_back, result_rows, d_first, normed_cross, d_cross_query, cross_mixed, d_second_low, d_first_low,
             grad_low, activated, d_pairs, attended_t, neigh_rows, kv_blocks, qkv_blocks, hidden_in, gains,
-            cosine.transpose(1, 0, 2), sine.transpose(1, 0, 2), d_gain_rest,
+            cosine, sine, d_gain_rest,
         )
         own_gain = lax.dynamic_slice_in_dim(s_gain, device * gain_rows, gain_rows, 1)
+        (
+            output, grad_in, grad_neighbours, s_qkv, s_att, s_cq, s_co, s_kv, s_down, up_share,
+        ) = finish(
+            [
+                output, grad_in, grad_neighbours, s_qkv, s_att, s_cq, s_co, s_kv, s_down,
+            ],
+            up_low,
+        )
         return (
             output.reshape(hidden_in.shape), grad_in.reshape(hidden_in.shape),
             grad_neighbours.reshape(neighbours.shape),
             own_gain[0], s_qkv, s_att, own_gain[1], s_cq, s_kv, s_co, own_gain[2], up_share, s_down,
         )
+    up_share = up_low.astype(jnp.float32)
     result_rows = result_rows.reshape(micro, tok_count, model_width)
     d_first = d_first.reshape(micro, tok_count, model_width)
     sent_t, tail_first, tail_result = to_tokens(

time: 447 us -> 377 us (0.84)
  Pallas kernels: 393 us -> 354 us
  local copies, waits for them, and re-layouts: 22.2 us -> 4.7 us
  other arithmetic: 11.8 us -> 3.39 us
    pallas_call x2 -> x1, Pallas kernels: 55.8 us -> 14.1 us  [to_units(): pl.pallas_call(functools.partial(to_units_kernel, total), out_shape=jax.S...]
    pallas_call x4 -> x3, Pallas kernels: 260 us -> 272 us  [the longest x1 144 us: first(): pl.pallas_call(functools.partial(first_kernel, depth, items), out_shape=o...]
    unnamed x63 -> x3, local copies, waits for them, and re-layouts: 12.2 us -> 0.19 us
    pallas_call x1, Pallas kernels: 31.5 us -> 21.9 us  [attn_backward(): pl.pallas_call(attn_backward_kernel, out_shape=jax.ShapeDtypeStruct((3, w...]
  transfers between devices with their start and end apart: 3 -> 1, of which waited for: 0 -> 0; matrix products, arithmetic and copies ran while one was open for 6% -> 1% of each run, Pallas kernels for 78% -> 43%
where the time goes in v3:
time: 377 us; the launch traced here: 376 us
  Pallas kernels  354 us (94%)
  between operations  14.2 us (4%)
  local copies, waits for them, and re-layouts  4.7 us (1%)
    pallas_call x1, Pallas kernels, first(): pl.pallas_call(functools.partial(first_kernel, depth, items), out_shape=o...  144 us
    pallas_call x1, Pallas kernels, last(): pl.pallas_call(functools.partial(last_kernel, depth, items, 2), out_shape...  124 us
    pallas_call x1, Pallas kernels, middle(): pl.pallas_call(middle_kernel, out_shape=out_shape, in_specs=[VMEM] * 8 +...  45.6 us
    pallas_call x1, Pallas kernels, attn_backward(): pl.pallas_call(attn_backward_kernel, out_shape=jax.ShapeDtypeStruct((3, w...  21.9 us
    pallas_call x1, Pallas kernels, to_units(): pl.pallas_call(functools.partial(to_units_kernel, total), out_shape=jax.S...  14.1 us
  transfers between devices with their start and end apart: 1, of which 0 were waited for; matrix products, arithmetic and copies ran while one was open for 1% of the time, Pallas kernels for 43%

profile of v3, /device:TPU:0, one launch (start us, length us, event | category | flops | bytes accessed | tf_op | source)
XLA Modules:
  0.0 375.9 jit_solution(11113778873313319352)
XLA Ops:
  7.2 0.0 reduce-scatter.2.cloned.1.call-start
  7.3 0.7 convert_element_type.24
  7.9 0.7 convert_element_type.26
  8.6 0.2 copy.33
  8.8 0.1 broadcast_in_dim.25
  8.9 0.1 convert_element_type.28
  9.0 0.7 broadcast_in_dim.20
  9.8 0.7 broadcast_in_dim.21
  10.5 0.7 broadcast_in_dim.22
  11.2 0.1 fusion.8
  11.3 0.6 fusion.5.refs_7_
  11.9 0.7 bitcast_select_fusion.used_ref
  12.6 143.9 %shard_map.246 = (bf16[6,4,2,2,2,24,384]{6,5,4,3,2,1,0:T(8,128)(2,1)}, bf16[3,4,2,2,2,24,768]{6,5,4,3,2,1,0:T(8,128)(2,1)}, bf16[2,4,2,2,2,24,768]{6,5,4,3,2,1,0...) custom-call(bf16[24,2304]{1,0:T(8,128)(2,1)} %refs_0_.1, ...), custom_call_target="tpu_custom_call" | custom-call | flops 1000000000 | bytes 20000000 | tf_op jit(solution)/shard_map/pallas_call | solution.py:1065
  156.4 45.6 %shard_map.247 = (bf16[256,768]{1,0:T(8,128)(2,1)}, f32[256,768]{1,0:T(8,128)}, bf16[2,768,128]{2,1,0:T(8,128)(2,1)}, bf16[256,768]{1,0:T(8,128)(2,1)}, bf16[256...) custom-call(bf16[2,768,128]{2,1,0:T(8,128)(2,1)} %bitcast.52, ...), custom_call_target="tpu_custom_call" | custom-call | flops 12000000000 | bytes 40000000 | tf_op jit(solution)/shard_map/pallas_call | solution.py:1300
  202.1 0.0 reduce-scatter.2.cloned.1.call-update
  202.1 0.8 slice.12
  202.9 14.1 %shard_map.248 = bf16[1,64,4096]{2,1,0:T(8,128)(2,1)} custom-call(bf16[24,1,64,128]{3,2,1,0:T(8,128)(2,1)} %bitcast.39), custom_call_target="tpu_custom_call" | custom-call | tf_op jit(solution)/shard_map/pallas_call | solution.py:258
  217.1 0.1 convert_reduce_fusion
  217.2 0.5 broadcast_select_fusion
  217.7 21.9 %shard_map.249.refs_0_ = bf16[3,64,4096]{2,1,0:T(8,128)(2,1)} custom-call(s32[8]{0:T(128)} %get-tuple-element.113.low_ref, s32[8]{0:T(128)} %get-tuple-element.112.high_ref, s32[1,4096]{1,0:T(1,128)} %get-tuple-element.61.first_ref, bf16[3,64,4096]{2,1,0:T(8,128)(2,1)} %get-tuple-element.62.qkv_ref, bf16[64,4096]{1,0:T(8,128)(2,1)} %bitcast.38, ...), custom_call_target="tpu_custom_call" | custom-call | flops 3000000000 | bytes 4000000 | tf_op jit(solution)/shard_map/pallas_call | solution.py:685
  239.6 124.4 %shard_map.250 = (bf16[256,768]{1,0:T(8,128)(2,1)}, bf16[256,768]{1,0:T(8,128)(2,1)}, bf16[1024,768]{1,0:T(8,128)(2,1)}, f32[24,2304]{1,0:T(8,128)}, f32[24,768]...) custom-call(bf16[3,64,4096]{2,1,0:T(8,128)(2,1)} %shard_map.249.refs, ...), custom_call_target="tpu_custom_call" | custom-call | flops 10000000000 | bytes 40000000 | tf_op jit(solution)/shard_map/pallas_call | solution.py:1699
  364.0 0.8 constant_dynamic-slice_fusion
  364.8 0.5 slice_bitcast_fusion
  365.3 3.8 shard_map.251
  (5 shorter events, 0.0 us)
Async XLA Ops:
  7.2 358.1 %reduce-scatter.2.cloned.1.call-start = ((), (), s32[]{:S(2)}) async-start(), calls=%async_computation.1 | async-start | bytes 4866048 | tf_op jit(solution)/shard_map/reduce_scatter | solution.py:1877
Sparse Core Ops, SparseCore 0:
  202.2 139.5 reduce-scatter.1
